TPU v7x, 32 devices: a whole 2x2x4 slice. The times are simulated.
32 devices in a mesh: expert: 8 (over z, x), shard: 4 (over y, core).
Axes of the slice: x: 2, y: 2, z: 4, core: 2. Of those that a mesh axis runs over, the one named last changes fastest.
Arguments:
- layer_input: bfloat16 [4096, 2048], P('expert'), may hold values from -6 to 6
- doc_ids: int32 [4096], P('expert'), may hold values from 0 to 3, as said below
- routes: int32 [4096, 8], P('expert'), may hold values from 0 to 15, all different within a row; in each aligned block of 512 rows (0 to 511, 512 to 1023, ...) at most 384 rows name the same one
- norm1_gain: float32 [2048], replicated, may hold values from 0.5 to 1.5
- query_weight: bfloat16 [2048, 4096], P(None, 'shard'), may hold values from -0.125 to 0.125
- key_matrix: bfloat16 [2048, 512], P(None, 'shard'), may hold values from -0.125 to 0.125
- value_matrix: bfloat16 [2048, 512], P(None, 'shard'), may hold values from -0.125 to 0.125
- query_norm_gain: float32 [128], replicated, may hold values from 0.5 to 1.5
- key_norm_gain: float32 [128], replicated, may hold values from 0.5 to 1.5
- out_weight: bfloat16 [4096, 2048], P('shard'), may hold values from -0.375 to 0.375
- norm2_gain: float32 [2048], replicated, may hold values from 0.5 to 1.5
- router_weight: bfloat16 [2048, 16], replicated, may hold values from -0.0625 to 0.0625
- gate_weight: bfloat16 [16, 2048, 768], P('expert', None, 'shard'), may hold values from -0.125 to 0.125
- up_weight: bfloat16 [16, 2048, 768], P('expert', None, 'shard'), may hold values from -0.125 to 0.125
- down_weight: bfloat16 [16, 768, 2048], P('expert', 'shard'), may hold values from -0.875 to 0.875
- cotangent: bfloat16 [4096, 2048], P('expert'), may hold values from -6 to 6
Outputs:
- layer_out: bfloat16 [4096, 2048], P('expert')
- input_grad: bfloat16 [4096, 2048], P('expert')
- norm1_gain_grad: float32 [2048], replicated
- query_weight_grad: float32 [2048, 4096], P(None, 'shard')
- key_weight_grad: float32 [2048, 512], P(None, 'shard')
- value_weight_grad: float32 [2048, 512], P(None, 'shard')
- query_gain_grad: float32 [128], replicated
- key_gain_grad: float32 [128], replicated
- out_weight_grad: float32 [4096, 2048], P('shard')
- norm2_gain_grad: float32 [2048], replicated
- router_weight_grad: float32 [2048, 16], replicated
- gate_weight_grad: float32 [16, 2048, 768], P('expert', None, 'shard')
- up_weight_grad: float32 [16, 2048, 768], P('expert', None, 'shard')
- down_weight_grad: float32 [16, 768, 2048], P('expert', 'shard')
Inputs may be any that keep to these rules, and one draw needn't show every extreme that they name: `doc_ids`: along each device's 512 rows the numbers start at 0 and never fall; in every draw some device holds a single document of all 512 rows. `routes`: each row names 8 different experts. In each device's 512 rows no expert is named more than 384 times, a bound that some block reaches.
All inputs are finite; a program needn't handle non-finite values.
Results may differ from a plain program's by a relative error of at most 0.03.
Values may be sent and summed in bfloat16 or wider, within the bound.
A program may use at most 384 MiB of HBM per device.

v0:
```python
import jax
import jax.numpy as jnp
from jax import lax
from jax.sharding import PartitionSpec as P

EPS = 1e-06
THETA = 1000000.0


def root_mean_norm_forward(vector, scale_gain):
    inverse = lax.rsqrt(jnp.mean(vector * vector, axis=-1, keepdims=True) + EPS)
    return vector * inverse * scale_gain


def rope_tables(positions, head_size):
    half_size = head_size // 2
    frequency = THETA ** (-2.0 * jnp.arange(half_size, dtype=jnp.float32) / head_size)
    angles = positions.astype(jnp.float32)[:, None] * frequency[None, :]
    return (jnp.cos(angles), jnp.sin(angles))


def apply_rotary(vector, cosine_table, sine_values):
    half_size = vector.shape[-1] // 2
    first_half = vector[..., :half_size]
    second_half = vector[..., half_size:]
    cos_rows = cosine_table[:, None, :]
    sin_rows = sine_values[:, None, :]
    return jnp.concatenate(
        [
            first_half * cos_rows - second_half * sin_rows,
            second_half * cos_rows + first_half * sin_rows,
        ],
        axis=-1,
    )


def doc_positions(doc_ids):
    row_index = jnp.arange(doc_ids.shape[0], dtype=jnp.int32)
    doc_starts = jnp.concatenate([jnp.ones((1,), jnp.bool_), doc_ids[1:] != doc_ids[:-1]])
    first_row = lax.cummax(jnp.where(doc_starts, row_index, 0), axis=0)
    return row_index - first_row


def swiglu(gate_pre, up_pre):
    return jax.nn.silu(gate_pre) * up_pre


def send_owners(table):
    return lax.all_to_all(table, "expert", split_axis=0, concat_axis=0, tiled=True)


def send_tokens(table):
    return lax.all_to_all(table, "expert", split_axis=0, concat_axis=0, tiled=True)


def local(
    layer_input,
    doc_ids,
    routes,
    norm1_gain,
    query_weight,
    key_matrix,
    value_matrix,
    query_norm_gain,
    key_norm_gain,
    out_weight,
    norm2_gain,
    router_weight,
    gate_weight,
    up_weight,
    down_weight,
    cotangent,
):
    tokens_here, model_width = layer_input.shape
    head_size = query_norm_gain.shape[0]
    heads_here = query_weight.shape[1] // head_size
    kv_here = key_matrix.shape[1] // head_size
    group_size = heads_here // kv_here
    top_count = routes.shape[1]
    experts_all = router_weight.shape[1]
    local_experts = gate_weight.shape[0]
    expert_peers = lax.axis_size("expert")
    shard_count = lax.axis_size("shard")
    capacity = shard_count * max(
        1, (3 * tokens_here * top_count // (2 * experts_all) + shard_count - 1) // shard_count
    )
    score_scale = head_size ** (-0.5)
    inputs = layer_input.astype(jnp.float32)
    norm_one, pull_norm1 = jax.vjp(root_mean_norm_forward, inputs, norm1_gain)
    first_normed_input = norm_one.astype(jnp.bfloat16)
    query_linear = jnp.dot(
        first_normed_input, query_weight, preferred_element_type=jnp.float32
    ).reshape(tokens_here, heads_here, head_size)
    key_linear = jnp.dot(
        first_normed_input, key_matrix, preferred_element_type=jnp.float32
    ).reshape(tokens_here, kv_here, head_size)
    value_token_rows = (
        jnp.dot(first_normed_input, value_matrix, preferred_element_type=jnp.float32)
        .astype(jnp.bfloat16)
        .reshape(tokens_here, kv_here, head_size)
    )
    positions = doc_positions(doc_ids)
    cosine_table, sine_values = rope_tables(positions, head_size)

    def head_prep(linear, scale_gain):
        return apply_rotary(root_mean_norm_forward(linear, scale_gain), cosine_table, sine_values)

    query_rotated, pull_query = jax.vjp(head_prep, query_linear, query_norm_gain)
    key_rotated, pull_key = jax.vjp(head_prep, key_linear, key_norm_gain)
    query_low = query_rotated.astype(jnp.bfloat16).reshape(
        tokens_here, kv_here, group_size, head_size
    )
    key_low = key_rotated.astype(jnp.bfloat16)
    row_index = jnp.arange(tokens_here)
    allowed = (doc_ids[:, None] == doc_ids[None, :]) & (row_index[:, None] >= row_index[None, :])

    def masked_scores():
        raw_scores = (
            jnp.einsum("tkgd,skd->kgts", query_low, key_low, preferred_element_type=jnp.float32)
            * score_scale
        )
        return jnp.where(allowed, raw_scores, -1e30)

    scores = masked_scores()
    row_max = jnp.max(scores, axis=-1, keepdims=True)
    exp_scores = jnp.exp(scores - row_max)
    row_total = jnp.sum(exp_scores, axis=-1, keepdims=True)
    log_total = row_max + jnp.log(row_total)
    probs_low = (exp_scores / row_total).astype(jnp.bfloat16)
    mixture = jnp.einsum(
        "kgts,skd->tkgd", probs_low, value_token_rows, preferred_element_type=jnp.float32
    )
    mixed = mixture.astype(jnp.bfloat16).reshape(tokens_here, heads_here * head_size)
    attn_part = jnp.dot(mixed, out_weight, preferred_element_type=jnp.float32)
    attn_full = lax.psum(attn_part.astype(jnp.bfloat16), "shard").astype(jnp.float32)
    residual = inputs + attn_full
    norm_two, pull_norm2 = jax.vjp(root_mean_norm_forward, residual, norm2_gain)
    normed_two = norm_two.astype(jnp.bfloat16)
    logits = jnp.dot(normed_two, router_weight, preferred_element_type=jnp.float32)
    route_hot = routes[:, :, None] == jnp.arange(experts_all, dtype=jnp.int32)[None, None, :]
    route_float = route_hot.astype(jnp.float32)

    def gate_softmax(logit_rows):
        chosen = jnp.sum(route_float * logit_rows[:, None, :], axis=-1)
        return jax.nn.softmax(chosen, axis=-1)

    gate_probs, pull_gates = jax.vjp(gate_softmax, logits)
    route_int = route_hot.astype(jnp.int32)
    hit_count = jnp.sum(route_int, axis=1)
    before = jnp.cumsum(hit_count, axis=0) - hit_count
    slot_index = jnp.sum(route_int * before[:, None, :], axis=-1)
    flat_place = (routes * capacity + slot_index).reshape(-1)
    token_rows = jnp.broadcast_to(
        normed_two[:, None, :], (tokens_here, top_count, model_width)
    ).reshape(tokens_here * top_count, model_width)
    send_table = (
        jnp.zeros((experts_all * capacity, model_width), jnp.bfloat16)
        .at[flat_place]
        .set(token_rows)
    )
    send_table = send_table.reshape(expert_peers, local_experts, capacity, model_width)
    received = send_owners(send_table)
    gate_pre = jnp.einsum(
        "sjcd,jdf->sjcf", received, gate_weight, preferred_element_type=jnp.float32
    )
    up_pre = jnp.einsum("sjcd,jdf->sjcf", received, up_weight, preferred_element_type=jnp.float32)
    activated, pull_act = jax.vjp(swiglu, gate_pre, up_pre)
    act_low = activated.astype(jnp.bfloat16)
    expert_part = jnp.einsum(
        "sjcf,jfd->sjcd", act_low, down_weight, preferred_element_type=jnp.float32
    )
    expert_owned = lax.psum_scatter(
        expert_part.astype(jnp.bfloat16), "shard", scatter_dimension=3, tiled=True
    )
    returned = send_tokens(expert_owned)
    returned = returned.reshape(experts_all * capacity, -1)
    output_cols = returned[flat_place].reshape(tokens_here, top_count, -1)
    output_rows = lax.all_gather(output_cols, "shard", axis=2, tiled=True)
    output_wide = output_rows.astype(jnp.float32)
    expert_sum = jnp.sum(gate_probs[:, :, None] * output_wide, axis=1)
    layer_out = (residual + expert_sum).astype(jnp.bfloat16)
    grad_out = cotangent.astype(jnp.float32)
    d_gates = jnp.sum(grad_out[:, None, :] * output_wide, axis=-1)
    (d_logits,) = pull_gates(d_gates)
    d_logits_low = d_logits.astype(jnp.bfloat16)
    router_grad = jnp.einsum(
        "td,te->de", normed_two, d_logits_low, preferred_element_type=jnp.float32
    )
    d_from_router = jnp.einsum(
        "te,de->td", d_logits_low, router_weight, preferred_element_type=jnp.float32
    )
    d_pieces = (
        (gate_probs[:, :, None] * grad_out[:, None, :])
        .astype(jnp.bfloat16)
        .reshape(tokens_here * top_count, model_width)
    )
    grad_table = (
        jnp.zeros((experts_all * capacity, model_width), jnp.bfloat16).at[flat_place].set(d_pieces)
    )
    grad_table = grad_table.reshape(expert_peers, local_experts, capacity, model_width)
    d_owned = send_owners(grad_table)
    d_act = jnp.einsum("sjcd,jfd->sjcf", d_owned, down_weight, preferred_element_type=jnp.float32)
    down_grad = jnp.einsum("sjcf,sjcd->jfd", act_low, d_owned, preferred_element_type=jnp.float32)
    d_gate_pre, d_up_pre = pull_act(d_act)
    d_gate_low = d_gate_pre.astype(jnp.bfloat16)
    d_up_low = d_up_pre.astype(jnp.bfloat16)
    gate_grad = jnp.einsum(
        "sjcd,sjcf->jdf", received, d_gate_low, preferred_element_type=jnp.float32
    )
    up_grad = jnp.einsum("sjcd,sjcf->jdf", received, d_up_low, preferred_element_type=jnp.float32)
    d_rows = jnp.einsum(
        "sjcf,jdf->sjcd", d_gate_low, gate_weight, preferred_element_type=jnp.float32
    )
    d_rows = d_rows + jnp.einsum(
        "sjcf,jdf->sjcd", d_up_low, up_weight, preferred_element_type=jnp.float32
    )
    d_rows_owned = lax.psum_scatter(
        d_rows.astype(jnp.bfloat16), "shard", scatter_dimension=3, tiled=True
    )
    d_returned = send_tokens(d_rows_owned)
    d_returned = d_returned.reshape(experts_all * capacity, -1)
    d_slice = jnp.sum(
        d_returned[flat_place].reshape(tokens_here, top_count, -1).astype(jnp.float32), axis=1
    )
    d_from_experts = lax.all_gather(
        d_slice.astype(jnp.bfloat16), "shard", axis=1, tiled=True
    ).astype(d_slice.dtype)
    d_residual_norm, norm2_grad = pull_norm2(d_from_experts + d_from_router)
    d_residual = grad_out + d_residual_norm
    d_attn = d_residual.astype(jnp.bfloat16)
    out_grad = jnp.einsum("te,td->ed", mixed, d_attn, preferred_element_type=jnp.float32)
    d_mixed = jnp.einsum("td,ed->te", d_attn, out_weight, preferred_element_type=jnp.float32)
    d_mixed = d_mixed.astype(jnp.bfloat16).reshape(tokens_here, kv_here, group_size, head_size)
    probs_again = jnp.exp(masked_scores() - log_total)
    probs_again_low = probs_again.astype(jnp.bfloat16)
    d_probs = jnp.einsum(
        "tkgd,skd->kgts", d_mixed, value_token_rows, preferred_element_type=jnp.float32
    )
    d_values = jnp.einsum(
        "kgts,tkgd->skd", probs_again_low, d_mixed, preferred_element_type=jnp.float32
    )
    d_scores = probs_again * (d_probs - jnp.sum(probs_again * d_probs, axis=-1, keepdims=True))
    d_scores_low = d_scores.astype(jnp.bfloat16)
    d_query_rot = (
        jnp.einsum("kgts,skd->tkgd", d_scores_low, key_low, preferred_element_type=jnp.float32)
        * score_scale
    )
    d_key_rot = (
        jnp.einsum("kgts,tkgd->skd", d_scores_low, query_low, preferred_element_type=jnp.float32)
        * score_scale
    )
    d_query_lin, d_query_gain = pull_query(d_query_rot.reshape(tokens_here, heads_here, head_size))
    d_key_lin, d_key_gain = pull_key(d_key_rot)
    d_query_low = d_query_lin.astype(jnp.bfloat16).reshape(tokens_here, heads_here * head_size)
    d_key_low = d_key_lin.astype(jnp.bfloat16).reshape(tokens_here, kv_here * head_size)
    d_value_low = d_values.astype(jnp.bfloat16).reshape(tokens_here, kv_here * head_size)
    query_grad = jnp.einsum(
        "td,te->de", first_normed_input, d_query_low, preferred_element_type=jnp.float32
    )
    key_grad = jnp.einsum(
        "td,te->de", first_normed_input, d_key_low, preferred_element_type=jnp.float32
    )
    value_grad = jnp.einsum(
        "td,te->de", first_normed_input, d_value_low, preferred_element_type=jnp.float32
    )
    d_norm_part = jnp.einsum(
        "te,de->td", d_query_low, query_weight, preferred_element_type=jnp.float32
    )
    d_norm_part = d_norm_part + jnp.einsum(
        "te,de->td", d_key_low, key_matrix, preferred_element_type=jnp.float32
    )
    d_norm_part = d_norm_part + jnp.einsum(
        "te,de->td", d_value_low, value_matrix, preferred_element_type=jnp.float32
    )
    d_normed_one, d_query_gain, d_key_gain = (
        lax.psum(d_norm_part.astype(jnp.bfloat16), "shard").astype(jnp.float32),
        lax.psum(d_query_gain.astype(jnp.bfloat16), "shard").astype(jnp.float32),
        lax.psum(d_key_gain.astype(jnp.bfloat16), "shard").astype(jnp.float32),
    )
    d_input_norm, norm1_grad = pull_norm1(d_normed_one)
    input_grad = (d_residual + d_input_norm).astype(jnp.bfloat16)
    summed = (
        lax.psum(query_grad.astype(jnp.bfloat16), "expert").astype(jnp.float32),
        lax.psum(key_grad.astype(jnp.bfloat16), "expert").astype(jnp.float32),
        lax.psum(value_grad.astype(jnp.bfloat16), "expert").astype(jnp.float32),
        lax.psum(out_grad.astype(jnp.bfloat16), "expert").astype(jnp.float32),
        lax.psum(router_grad.astype(jnp.bfloat16), "expert").astype(jnp.float32),
        lax.psum(d_query_gain.astype(jnp.bfloat16), "expert").astype(jnp.float32),
        lax.psum(d_key_gain.astype(jnp.bfloat16), "expert").astype(jnp.float32),
        lax.psum(norm1_grad.astype(jnp.bfloat16), "expert").astype(jnp.float32),
        lax.psum(norm2_grad.astype(jnp.bfloat16), "expert").astype(jnp.float32),
    )
    (
        query_sum,
        key_sum,
        value_sum,
        out_sum,
        router_sum,
        query_gain_sum,
        key_gain_sum,
        norm1_sum,
        norm2_sum,
    ) = summed
    return (
        layer_out,
        input_grad,
        norm1_sum,
        query_sum,
        key_sum,
        value_sum,
        query_gain_sum,
        key_gain_sum,
        out_sum,
        norm2_sum,
        router_sum,
        gate_grad,
        up_grad,
        down_grad,
    )


def solution(mesh):
    return jax.shard_map(
        local,
        mesh=mesh,
        in_specs=(
            P("expert", None),
            P("expert"),
            P("expert", None),
            P(),
            P(None, "shard"),
            P(None, "shard"),
            P(None, "shard"),
            P(),
            P(),
            P("shard", None),
            P(),
            P(),
            P("expert", None, "shard"),
            P("expert", None, "shard"),
            P("expert", "shard", None),
            P("expert", None),
        ),
        out_specs=(
            P("expert", None),
            P("expert", None),
            P(),
            P(None, "shard"),
            P(None, "shard"),
            P(None, "shard"),
            P(),
            P(),
            P("shard", None),
            P(),
            P(),
            P("expert", None, "shard"),
            P("expert", None, "shard"),
            P("expert", "shard", None),
        ),
        check_vma=False,
    )
```

profile of v0, /device:TPU:8, one launch (start us, length us, event | category | flops | bytes accessed | tf_op | source)
XLA Modules:
  0.0 2267.7 jit_solution(12090309521088863377)
XLA Ops:
  33.7 3.7 convolution_convert_fusion.2
  39.5 50.7 %all-reduce.11.cloned.1.call-done = bf16[512,2048]{1,0:T(8,128)(2,1)} async-done(((bf16[512,2048]{1,0:T(8,128)(2,1)}), bf16[512,2048]{1,0:T(8,128)(2,1)}) %all-reduce.11.cloned.1.call-update) | async-done | bytes 2097168 | tf_op jit(solution)/shard_map/psum | solution.py:135
  94.8 7.9 broadcast_bitcast_fusion
  102.8 38.0 %scatter_custom_fusion = bf16[6144,2048]{1,0:T(8,128)(2,1)} fusion(s32[4096]{0:T(1024)S(1)} %bitcast.277, bf16[4096,2048]{1,0:T(8,128)(2,1)} %broadcast_bitcast_fusion, bf16[]{:T(256)} %constant.61.clone.1), kind=kCustom, calls=%fused_computation.23 | custom fusion | bytes 25166336 | tf_op jit(solution)/shard_map/scatter | solution.py:159
  140.8 6.8 all-to-all-start
  147.7 4.3 convert_element_type.203
  153.6 9.9 fusion.2
  163.6 38.1 %scatter_custom_fusion.1 = bf16[6144,2048]{1,0:T(8,128)(2,1)} fusion(s32[4096]{0:T(1024)S(1)} %bitcast.278, bf16[4096,2048]{1,0:T(8,128)(2,1)} %fusion.2, bf16[]{:T(256)} %constant.61.clone.1), kind=kCustom, calls=%fused_computation.21 | custom fusion | bytes 25166336 | tf_op jit(solution)/shard_map/scatter | solution.py:198
  201.6 486.4 %all-to-all-done = bf16[8,2,384,2048]{3,2,1,0:T(8,128)(2,1)} async-done(((bf16[8,2,384,2048]{3,2,1,0:T(8,128)(2,1)}), bf16[8,2,384,2048]{3,2,1,0:T(8,128)(2,1)}, u32[]{:S(2)}, u32[]{:S(2)}) %all-to-all-start) | async-done | bytes 25165856 | tf_op jit(solution)/shard_map/all_to_all | solution.py:49
  688.0 8.9 all-to-all-start.2
  697.3 15.1 fusion.8
  712.4 14.5 fusion.10
  726.9 509.5 %all-to-all-done.2 = bf16[8,2,384,2048]{3,2,1,0:T(8,128)(2,1)} async-done(((bf16[8,2,384,2048]{3,2,1,0:T(8,128)(2,1)}), bf16[8,2,384,2048]{3,2,1,0:T(8,128)(2,1)}, u32[]{:S(2)}, u32[]{:S(2)}) %all-to-all-start.2) | async-done | bytes 25165856 | tf_op jit(solution)/shard_map/all_to_all | solution.py:49
  1236.4 18.8 fusion.26
  1255.2 13.6 convert_bitcast_fusion
  1268.9 33.5 %fusion.52 = f32[2,8,384,2048]{3,2,1,0:T(8,128)} fusion(bf16[8,2,384,192]{2,3,0,1:T(8,128)(2,1)} %get-tuple-element.36, bf16[2,2048,192]{1,2,0:T(8,128)(2,1)S(1)} %copy-done.33), kind=kOutput, calls=%fused_computation.110 | convolution fusion | flops 4831838208 | bytes 54263808 | tf_op jit(solution)/shard_map/sjcf,jdf->sjcd/dot_general | solution.py:211
  1302.4 27.0 %fusion.3 = bf16[8,2,384,2048]{3,2,0,1:T(8,128)(2,1)} fusion(f32[2,8,384,2048]{3,2,1,0:T(8,128)} %fusion.52, bf16[8,2,384,192]{2,3,0,1:T(8,128)(2,1)} %get-tuple-element.35, bf16[2,2048,192]{1,2,0:T(8,128)(2,1)S(1)} %copy-done.34), kind=kOutput, calls=%fused_computation.11 | convolution fusion | flops 4857004032 | bytes 79429632 | tf_op jit(solution)/shard_map/sjcf,jdf->sjcd/dot_general | solution.py:214
  1329.4 120.5 %reduce-scatter.3.cloned.1.call-done = bf16[8,2,384,512]{3,2,0,1:T(8,128)(2,1)} async-done(((bf16[8,2,384,2048]{3,2,0,1:T(8,128)(2,1)}), bf16[8,2,384,512]{3,2,0,1:T(8,128)(2,1)}) %reduce-scatter.3.cloned.1.call-update) | async-done | bytes 6291472 | tf_op jit(solution)/shard_map/reduce_scatter | solution.py:172
  1450.0 6.0 copy.202
  1456.0 6.2 all-to-all-start.1
  1462.2 135.6 %all-to-all-done.1 = bf16[8,2,384,512]{3,2,1,0:T(8,128)(2,1)} async-done(((bf16[8,2,384,512]{3,2,1,0:T(8,128)(2,1)}), bf16[8,2,384,512]{3,2,1,0:T(8,128)(2,1)}, u32[]{:S(2)}, u32[]{:S(2)}) %all-to-all-start.1) | async-done | bytes 6291488 | tf_op jit(solution)/shard_map/all_to_all | solution.py:53
  1597.9 21.4 gather_fusion
  1619.3 13.7 reduce-scatter.5.cloned.1.call-done
  1633.0 3.4 copy.205
  1636.5 143.4 %all_to_all.20 = bf16[8,2,384,512]{3,2,1,0:T(8,128)(2,1)} all-to-all(bf16[8,2,384,512]{3,2,1,0:T(8,128)(2,1)S(1)} %copy.205), channel_id=1, replica_groups=mesh['expert'=8,'shard'=4] {'expert'}, dimensions={0} | all-to-all | bytes 12582912 | tf_op jit(solution)/shard_map/all_to_all | solution.py:53
  1779.8 21.1 gather_fusion.1
  1800.9 5.9 bitcast_reduce_fusion
  1807.0 17.3 fusion.1
  1824.5 3.5 all-gather.5.cloned.1.call-done
  1828.0 4.8 multiply_reduce_fusion
  1832.9 5.0 fusion.33
  1842.3 4.5 fusion.36
  1849.1 3.1 multiply_bitcast_fusion
  1858.0 8.1 copy.216
  1866.0 3.1 fusion.64
  1877.2 4.7 fusion.114
  1886.7 6.3 convolution_convert_fusion.1
  1893.0 4.4 convolution_convert_fusion
  1897.4 13.3 convolution_bitcast_fusion
  1910.8 13.3 convolution_bitcast_fusion.1
  1924.1 12.3 fusion.42
  1936.4 5.9 all-reduce.6
  1942.3 4.0 fusion.32
  1946.3 20.3 all-reduce.4
  1968.8 6.1 fusion.35
  1974.9 268.8 %all-reduce.15.cloned.1.call-done = (bf16[2048,1024]{1,0:T(8,128)(2,1)}, bf16[2048,128]{1,0:T(8,128)(2,1)}, bf16[2048,128]{1,0:T(8,128)(2,1)}, bf16[1024,2048]{1,0:T(8,128)(2,1)}, bf16[2048,16]{0,1:T(8,128)(2,1)}) async-done(((bf16[2048,1024]{1,0:T(8,128)(2,1)}, bf16[2048,128]{1,0:T(8,128)(2,1)}, bf16[2048,128]{1,0:T(8,128)(2,1)}, bf16[1024,2048]{1,0:T(8,128)(2,1)}, bf16[2048,16]{0,1:T(8,128)(2,1)}), ...) | async-done | bytes 9502736 | tf_op jit(solution)/shard_map/psum | solution.py:283
  2249.4 6.8 convert_element_type.226
  2256.2 4.4 convert_element_type.236
  (291 shorter events, 67.9 us)
Async XLA Ops:
  7.2 1229.2 %copy-start = (bf16[2,192,2048]{2,1,0:T(8,128)(2,1)S(1)}, bf16[2,192,2048]{2,1,0:T(8,128)(2,1)}, u32[]{:S(2)}) copy-start(bf16[2,192,2048]{2,1,0:T(8,128)(2,1)} %param.30) | copy-start | bytes 4718596
  7.2 7.4 copy-start.70
  7.2 7.4 copy-start.41
  7.2 82.9 %all-reduce.11.cloned.1.call-start = ((), (), s32[]{:S(2)}) async-start(), calls=%async_computation.6 | async-start | bytes 4194304 | tf_op jit(solution)/shard_map/psum | solution.py:135
  7.3 9.5 copy-start.82
  11.3 6.1 copy-start.76
  14.6 14.2 copy-start.52
  16.6 7.8 copy-start.29
  16.6 7.8 copy-start.31
  17.4 8.0 copy-start.35
  17.4 8.0 copy-start.37
  37.4 55.9 %copy-start.62 = (f32[2048]{0:T(1024)S(1)}, f32[2048]{0:T(1024)}, u32[]{:S(2)}) copy-start(f32[2048]{0:T(1024)} %param.26) | copy-start | bytes 24580
  39.4 124.1 %copy-start.58 = (s32[4096,1]{0,1:T(1,128)}, s32[4096,1]{0,1:T(1,128)S(1)}, u32[]{:S(2)}) copy-start(s32[4096,1]{0,1:T(1,128)S(1)} %compare_select_fusion) | copy-start | bytes 49156
  93.3 9.5 copy-start.74
  93.6 9.1 copy-start.78
  94.8 8.0 copy-start.7
  140.8 547.2 %all-to-all-start = ((bf16[8,2,384,2048]{3,2,1,0:T(8,128)(2,1)}), bf16[8,2,384,2048]{3,2,1,0:T(8,128)(2,1)}, u32[]{:S(2)}, u32[]{:S(2)}) async-start(bf16[8,2,384,2048]{3,2,1,0:T(8,128)(2,1)} %bitcast.268), calls=%async_computation | async-start | bytes 50331648 | tf_op jit(solution)/shard_map/all_to_all | solution.py:49
  152.7 10.8 copy-start.60
  153.3 10.2 copy-start.68
  153.5 10.1 copy-start.25
  688.0 548.4 %all-to-all-start.2 = ((bf16[8,2,384,2048]{3,2,1,0:T(8,128)(2,1)}), bf16[8,2,384,2048]{3,2,1,0:T(8,128)(2,1)}, u32[]{:S(2)}, u32[]{:S(2)}) async-start(bf16[8,2,384,2048]{3,2,1,0:T(8,128)(2,1)} %bitcast.269), calls=%async_computation.3 | async-start | bytes 50331648 | tf_op jit(solution)/shard_map/all_to_all | solution.py:49
  696.9 15.5 copy-start.33
  696.9 753.1 %reduce-scatter.3.cloned.1.call-start = ((), (), s32[]{:S(2)}) async-start(), calls=%async_computation.7 | async-start | bytes 31457280 | tf_op jit(solution)/shard_map/reduce_scatter | solution.py:172
  1268.9 364.2 %reduce-scatter.5.cloned.1.call-start = ((), (), s32[]{:S(2)}) async-start(), calls=%async_computation.9 | async-start | bytes 31457280 | tf_op jit(solution)/shard_map/reduce_scatter | solution.py:217
  1268.9 33.5 %copy-start.34 = (bf16[2,2048,192]{1,2,0:T(8,128)(2,1)S(1)}, bf16[2,2048,192]{1,2,0:T(8,128)(2,1)}, u32[]{:S(2)}) copy-start(bf16[2,2048,192]{1,2,0:T(8,128)(2,1)} %param.29) | copy-start | bytes 4718596
  1456.0 6.2 copy-start.59
  1456.0 141.8 %all-to-all-start.1 = ((bf16[8,2,384,512]{3,2,1,0:T(8,128)(2,1)}), bf16[8,2,384,512]{3,2,1,0:T(8,128)(2,1)}, u32[]{:S(2)}, u32[]{:S(2)}) async-start(bf16[8,2,384,512]{3,2,1,0:T(8,128)(2,1)} %copy.202), calls=%async_computation.2 | async-start | bytes 12582912 | tf_op jit(solution)/shard_map/all_to_all | solution.py:53
  1462.2 344.8 %all-gather.3.cloned.1.call-start = ((), (), s32[]{:S(2)}) async-start(), calls=%async_computation.8 | async-start | bytes 20971520 | tf_op jit(solution)/shard_map/all_gather | solution.py:178
  1619.3 208.7 %all-gather.5.cloned.1.call-start = ((), (), s32[]{:S(2)}) async-start(), calls=%async_computation.10 | async-start | bytes 2621440 | tf_op jit(solution)/shard_map/all_gather | solution.py:225
  1800.9 6.0 copy-start.69
  1800.9 6.1 copy-start.26
  1806.8 135.5 %all-reduce.13.cloned.1.call-start = ((), (), s32[]{:S(2)}) async-start(), calls=%async_computation.11 | async-start | bytes 4194304 | tf_op jit(solution)/shard_map/psum | solution.py:276
  1806.9 17.5 copy-start.40
  1806.9 17.5 copy-start.61
  1806.9 17.5 copy-start.45
  1806.9 21.1 copy-start.57
  1807.0 21.1 copy-start.63
  1807.0 21.0 copy-start.79
  1824.5 8.3 copy-start.75
  1828.0 12.3 slice-start
  1832.9 7.4 slice-start.1
  1884.0 359.7 %all-reduce.15.cloned.1.call-start = ((), (), s32[]{:S(2)}) async-start(), calls=%async_computation.12 | async-start | bytes 19005440 | tf_op jit(solution)/shard_map/psum | solution.py:283
  1886.7 6.3 copy-start.16
  1886.7 6.3 copy-start.92
  1897.4 13.4 copy-start.23
  1910.8 13.4 copy-start.22
  1936.4 32.4 %copy-start.73 = (f32[512]{0:T(512)S(1)}, f32[512]{0:T(512)}, u32[]{:S(2)}) copy-start(f32[512]{0:T(512)} %copy-done.72) | copy-start | bytes 6148
  2249.4 6.8 copy-start.24
  (57 other events, 199.6 us)
Sparse Core Ops, SparseCore 0:
  37.6 52.5 all-reduce.10
  1269.0 180.9 reduce-scatter.2
  1452.6 180.4 reduce-scatter.4
  1635.1 105.9 all-gather.2
  1806.9 21.0 all-gather.4
  1884.1 51.3 all-reduce.12
  1941.5 302.1 all-reduce.14
where the time goes:
time: 2280 us; the launch traced here: 2270 us
  waiting for transfers between devices  1590 us (70%)
  matrix products  220 us (10%)
  blocking collectives  170 us (7%)
  local copies, waits for them, and re-layouts  153 us (7%)
  other arithmetic  98.1 us (4%)
    all_to_all x2, waiting for transfers between devices, send_owners(): lax.all_to_all(table, 'expert', split_axis=0, concat_axis=0, tiled=True)  996 us
    psum x1, waiting for transfers between devices, local(): lax.psum(query_grad.astype(jnp.bfloat16), 'expert').astype(jnp.float32)  269 us
    all_to_all x1, blocking collectives, send_tokens(): lax.all_to_all(table, 'expert', split_axis=0, concat_axis=0, tiled=True)  143 us
    all_to_all x1, waiting for transfers between devices, send_tokens(): lax.all_to_all(table, 'expert', split_axis=0, concat_axis=0, tiled=True)  136 us
    reduce_scatter x1, waiting for transfers between devices, local(): lax.psum_scatter(expert_part.astype(jnp.bfloat16), 'shard', scatter_dimen...  121 us
    psum x1, waiting for transfers between devices, local(): lax.psum(attn_part.astype(jnp.bfloat16), 'shard').astype(jnp.float32)  50.7 us
  transfers between devices with their start and end apart: 10, of which 8 were waited for; matrix products, arithmetic and copies ran while one was open for 13% of the time, Pallas kernels for 0%

commit v1 on v0

v1 whole, which is shorter than its diff:
```python
import jax
import jax.numpy as jnp
from jax import lax
from jax.experimental import pallas as pl
from jax.experimental.pallas import tpu as pltpu
from jax.sharding import PartitionSpec as P

EPS = 1e-06
THETA = 1000000.0
BF = jnp.bfloat16
F32 = jnp.float32
MESH = pl.DeviceIdType.MESH
VMEM_ROWS = 1024


def dot(a, b):
    return jnp.dot(a, b, preferred_element_type=F32)


def dot_nt(a, b):
    return lax.dot_general(a, b, (((1,), (1,)), ((), ())), preferred_element_type=F32)


def dot_tn(a, b):
    return lax.dot_general(a, b, (((0,), (0,)), ((), ())), preferred_element_type=F32)


LINK_BYTES_PER_US = 1e5


def grid_of(axis):
    size = lax.axis_size(axis)
    lines = 4 if axis == "expert" else 2
    return axis, lines, size // lines, size // lines


def line_of(grid):
    return grid[0], grid[1], 1, grid[3]


def cross_of(grid):
    return grid[0], 1, grid[2], grid[3]


def position(grid):
    axis, lines, width, stride = grid
    me = lax.axis_index(axis)
    return me, me // stride if lines > 1 else 0, me % width if width > 1 else 0


def at_each_line(grid, act):
    _, z, _ = position(grid)
    for at in range(grid[1]):

        @pl.when(z == at)
        def _():
            act(at)


def greet(grids):
    barrier = pltpu.get_barrier_semaphore()
    count = 0
    for grid in grids:
        axis, lines, width, stride = grid
        me, z, b = position(grid)

        def signal(peer):
            pl.semaphore_signal(barrier, inc=1, device_id={axis: peer}, device_id_type=MESH)

        @pl.when(z < lines - 1)
        def _():
            signal(me + stride)

        @pl.when(z > 0)
        def _():
            signal(me - stride)

        for o in range(1, width):
            signal(me - b + (b + o) % width)
        count = count + width - 1
        count = count + (z < lines - 1).astype(jnp.int32) + (z > 0).astype(jnp.int32)
    pl.semaphore_wait(barrier, count)


def slice_of(ref, start, rows):
    if not isinstance(start, int):
        start = pl.multiple_of(start, rows)
    return ref.at[pl.ds(start, rows)]


class Gather:
    def __init__(self, grid, source, out, pieces, sems):
        self.axis, self.lines, self.width, self.stride = grid
        self.source, self.out, self.pieces = source, out, pieces
        self.rows_all = source.shape[0]
        self.rows = self.rows_all // pieces
        self.send_r, self.send_l, self.send_x, self.recv = sems
        self.me, _, self.b = position(grid)
        self.bytes = self.rows * source.shape[1] * jnp.dtype(source.dtype).itemsize

    @staticmethod
    def sems(grid, pieces):
        _, lines, width, _ = grid
        dma = pltpu.SemaphoreType.DMA
        return [
            dma((lines, pieces)),
            dma((lines, pieces)),
            dma((max(1, width - 1), lines, pieces)),
            dma((lines * width, pieces)),
        ]

    def copy(self, slot, p, sem, peer, own=False):
        place = slice_of(self.out, slot * self.rows_all + p * self.rows, self.rows)
        source = slice_of(self.source, p * self.rows, self.rows) if own else place
        return pltpu.make_async_remote_copy(
            src_ref=source,
            dst_ref=place,
            send_sem=sem,
            recv_sem=self.recv.at[slot, p],
            device_id={self.axis: peer},
            device_id_type=MESH,
        )

    def sends(self, z, origin, p):
        slot = origin * self.width + self.b
        own = origin == z
        copies = []
        if origin <= z and z < self.lines - 1:
            sem = self.send_r.at[z - origin, p]
            copies.append(self.copy(slot, p, sem, self.me + self.stride, own))
        if origin >= z and z > 0:
            sem = self.send_l.at[origin - z, p]
            copies.append(self.copy(slot, p, sem, self.me - self.stride, own))
        for o in range(1, self.width):
            peer = self.me - self.b + (self.b + o) % self.width
            copies.append(self.copy(slot, p, self.send_x.at[o - 1, origin, p], peer, own))
        return copies

    def start(self, z, p):
        for c in self.sends(z, z, p):
            c.start()

    def arrived(self, slot, p):
        self.copy(slot, p, self.send_r.at[0, p], self.me).wait_recv()

    def forward(self, z, origin, p):
        self.arrived(origin * self.width + self.b, p)
        for c in self.sends(z, origin, p):
            c.start()

    def arrived_across(self, z, p):
        for o in range(1, self.width):
            self.arrived(z * self.width + (self.b + o) % self.width, p)

    def wait_sends(self, z):
        for p in range(self.pieces):
            for origin in range(self.lines):
                for c in self.sends(z, origin, p):
                    c.wait_send()

    def finish(self, z):
        for p in range(self.pieces):
            for line in range(self.lines):
                self.arrived_across(line, p)
        self.wait_sends(z)

    def own_slot(self, z):
        return slice_of(self.out, (z * self.width + self.b) * self.rows_all, self.rows_all)


class Scatter:
    def __init__(self, grid, parts, buffers, pieces, sems):
        self.axis, self.lines, self.width, self.stride = grid
        self.parts, self.pieces = parts, pieces
        self.cross, self.right, self.left = buffers
        self.rows_all = parts.shape[0] // (self.lines * self.width)
        self.rows = self.rows_all // pieces
        self.cross_send, self.cross_recv, self.r_send, self.r_recv, self.l_send, self.l_recv = sems
        self.me, _, self.b = position(grid)
        self.bytes = self.rows * parts.shape[1] * jnp.dtype(parts.dtype).itemsize

    @staticmethod
    def sems(grid, pieces):
        _, lines, width, _ = grid
        dma = pltpu.SemaphoreType.DMA
        across = (max(1, width - 1), lines, pieces)
        return [dma(across), dma(across)] + [dma((lines, pieces)) for _ in range(4)]

    @staticmethod
    def buffers(grid, rows_all, columns, kind):
        _, lines, width, _ = grid
        line = pltpu.VMEM((lines * rows_all if lines > 1 else 16, columns), kind)
        return [pltpu.VMEM((max(1, width - 1) * lines * rows_all, columns), kind), line, line]

    def start_of(self, slot, p):
        return slot * self.rows_all + p * self.rows

    def cross_copy(self, o, k, p):
        peer = (self.b + o) % self.width
        return pltpu.make_async_remote_copy(
            src_ref=slice_of(self.parts, self.start_of(k * self.width + peer, p), self.rows),
            dst_ref=slice_of(self.cross, self.start_of((o - 1) * self.lines + k, p), self.rows),
            send_sem=self.cross_send.at[o - 1, k, p],
            recv_sem=self.cross_recv.at[o - 1, k, p],
            device_id={self.axis: self.me - self.b + peer},
            device_id_type=MESH,
        )

    def line_copy(self, k, p, rightward):
        into = self.right if rightward else self.left
        at = self.start_of(k, p)
        return pltpu.make_async_remote_copy(
            src_ref=slice_of(self.cross, at, self.rows),
            dst_ref=slice_of(into, at, self.rows),
            send_sem=(self.r_send if rightward else self.l_send).at[k, p],
            recv_sem=(self.r_recv if rightward else self.l_recv).at[k, p],
            device_id={self.axis: self.me + self.stride if rightward else self.me - self.stride},
            device_id_type=MESH,
        )

    def start_one(self, k, p):
        for o in range(1, self.width):
            self.cross_copy(o, k, p).start()

    def add(self, k, p, sources, target):
        block = min(16, self.rows)
        own = self.start_of(k * self.width + self.b, p)

        @pl.loop(0, self.rows // block)
        def _(i):
            def rows_at(start):
                return pl.ds(pl.multiple_of(start + i * block, block), block)

            total = self.parts[rows_at(own), :].astype(F32)
            for o in range(self.width - 1):
                at = rows_at(self.start_of(o * self.lines + k, p))
                total = total + self.cross[at, :].astype(F32)
            for source in sources:
                total = total + source[rows_at(self.start_of(k, p)), :].astype(F32)
            target(rows_at(p * self.rows), total)

    def sources(self, z, k, p):
        found = []
        if k >= z and z > 0:
            self.line_copy(k, p, True).wait_recv()
            found.append(self.right)
        if k <= z and z < self.lines - 1:
            self.line_copy(k, p, False).wait_recv()
            found.append(self.left)
        return found

    def reduce_one(self, z, k, p):
        for o in range(1, self.width):
            self.cross_copy(o, k, p).wait_recv()

        def put(at, total):
            offset = pl.multiple_of(at.start + k * self.rows_all, at.size)
            self.cross[pl.ds(offset, at.size), :] = total.astype(self.cross.dtype)

        self.add(k, p, self.sources(z, k, p), put)
        self.line_copy(k, p, k > z).start()

    def total(self, z, p, target):
        for o in range(1, self.width):
            self.cross_copy(o, z, p).wait_recv()
        self.add(z, p, self.sources(z, z, p), target)

    def finish(self, z):
        for p in range(self.pieces):
            for k in range(self.lines):
                for o in range(1, self.width):
                    self.cross_copy(o, k, p).wait_send()
                if k != z:
                    self.line_copy(k, p, k > z).wait_send()


def targets(lines, z):
    others = sorted((k for k in range(lines) if k != z), key=lambda k: (-abs(k - z), -k))
    return others + [z]


class Plan:
    def __init__(self, lines):
        self.lines = lines
        self.steps = [[] for _ in range(lines)]
        self.jobs = 0

    def job(self):
        self.jobs += 1
        return self.jobs

    def add(self, z, waits, act, sends, begin=0.0):
        self.steps[z].append((begin, waits, act, sends))

    def order(self):
        arrived = [dict() for _ in range(self.lines)]
        free = {}
        clock = [0.0] * self.lines
        left = [list(enumerate(steps)) for steps in self.steps]
        result = [[] for _ in range(self.lines)]
        while any(left):
            best = None
            for z in range(self.lines):
                for i, (begin, waits, act, sends) in left[z]:
                    if all(key in arrived[z] for key in waits):
                        ready = max([begin] + [arrived[z][key] for key in waits])
                        if best is None or (max(ready, clock[z]), ready, z, i) < best[0]:
                            best = ((max(ready, clock[z]), ready, z, i), act, sends)
            (now, _, z, i), act, sends = best
            left[z] = [entry for entry in left[z] if entry[0] != i]
            result[z].append((now, act))
            clock[z] = now + 0.7
            for link, time, to, key in sends:
                start = max(now + 1.0, free.get((z, link), 0.0))
                free[z, link] = start + time
                arrived[to][key] = start + time + 1.0
        return result

    def run(self, grid, result, begin, end):
        def act(z):
            for now, step in result[z]:
                if begin <= now < end:
                    step()

        at_each_line(grid, act)


    def run_step(self, grid, result, index, begin, each, steps, early=False):
        _, z, _ = position(grid)
        for at in range(self.lines):
            for now, step in result[at]:
                due = int((now - begin) // each)
                if early:
                    due = max(0, due)
                if 0 <= due < steps:

                    @pl.when(jnp.logical_and(z == at, index == due))
                    def _():
                        step()


def plan_scatter(plan, scatter, p, put, then=None, begin=0.0, start=True):
    n = plan.job()
    lines, width = scatter.lines, scatter.width
    time = 2 * scatter.bytes / LINK_BYTES_PER_US
    for z in range(lines):
        ready = begin if isinstance(begin, (int, float)) else None
        for i, k in enumerate(targets(lines, z)):
            first = ready if ready is not None else begin[i]
            if width > 1:
                plan.add(
                    z,
                    [],
                    (lambda k=k: scatter.start_one(k, p)) if start else (lambda: None),
                    [("x", time * (width - 1), z, (n, "c", k))],
                    first,
                )
            waits = [(n, "c", k)] if width > 1 else []
            if k >= z and z > 0:
                waits.append((n, "r", k))
            if k <= z and z < lines - 1:
                waits.append((n, "l", k))
            if k > z:
                sends = [("r", time, z + 1, (n, "r", k))]
            elif k < z:
                sends = [("l", time, z - 1, (n, "l", k))]
            else:
                follow, sends = then(z) if then else ((lambda: None), [])

                def last(z=z, follow=follow):
                    scatter.total(z, p, put)
                    follow()

                plan.add(z, waits, last, sends, first)
                continue
            plan.add(z, waits, lambda z=z, k=k: scatter.reduce_one(z, k, p), sends, first)


def gather_sends(gather, n, time, z, origin):
    sends = []
    if origin <= z and z < gather.lines - 1:
        sends.append(("r", time, z + 1, (n, "g", origin)))
    if origin >= z and z > 0:
        sends.append(("l", time, z - 1, (n, "g", origin)))
    if gather.width > 1:
        sends.append(("x", time * (gather.width - 1), z, (n, "gx", origin)))
    return sends


def plan_gather(plan, gather, p, begin=None):
    n = plan.job()
    time = 2 * gather.bytes / LINK_BYTES_PER_US
    for z in range(gather.lines):
        for origin in range(gather.lines):
            if origin != z:
                plan.add(
                    z,
                    [(n, "g", origin)],
                    lambda z=z, origin=origin: gather.forward(z, origin, p),
                    gather_sends(gather, n, time, z, origin),
                )

    def then(z):
        return (lambda: gather.start(z, p)), gather_sends(gather, n, time, z, z)

    if begin is not None:
        for z in range(gather.lines):
            act, sends = then(z)
            plan.add(z, [], act, sends, begin)
    return then


class Reduce:
    def __init__(self, grid, parts, out, scratch, pieces, line_first):
        self.grid, self.parts, self.out = grid, parts, out
        self.line_first = line_first
        self.pieces = pieces
        take = Taker(scratch)
        self.sums = take.one()
        if line_first:
            self.pair_sums, self.pair_all = take.take(2)
            self.first = Scatter(line_of(grid), parts, take.take(3), 1, take.take(6))
            self.second = Scatter(cross_of(grid), self.pair_sums, take.take(3), 1, take.take(6))
            self.third = Gather(cross_of(grid), self.sums, self.pair_all, 1, take.take(4))
            self.fourth = Gather(line_of(grid), self.pair_all, out, 1, take.take(4))
        else:
            self.scatter = Scatter(grid, parts, take.take(3), pieces, take.take(6))
            self.gather = Gather(grid, self.sums, out, pieces, take.take(4))
        self.own_sem = take.one()

    @staticmethod
    def scratch(grid, rows, columns, kind, pieces, line_first):
        _, lines, width, _ = grid
        count = rows // (lines * width)
        shapes = [pltpu.VMEM((count, columns), kind)]
        if line_first:
            line, cross = line_of(grid), cross_of(grid)
            shapes += [pltpu.VMEM((width * count, columns), kind)] * 2
            shapes += Scatter.buffers(line, width * count, columns, kind) + Scatter.sems(line, 1)
            shapes += Scatter.buffers(cross, count, columns, kind) + Scatter.sems(cross, 1)
            shapes += Gather.sems(cross, 1) + Gather.sems(line, 1)
        else:
            shapes += Scatter.buffers(grid, count, columns, kind) + Scatter.sems(grid, pieces)
            shapes += Gather.sems(grid, pieces)
        return shapes + [pltpu.SemaphoreType.DMA]

    @staticmethod
    def refs(line_first):
        return 1 + (2 + 9 + 9 + 8 if line_first else 9 + 4) + 1

    def put(self, at, total):
        self.sums[at, :] = total.astype(self.sums.dtype)

    def put_pair(self, at, total):
        self.pair_sums[at, :] = total.astype(self.pair_sums.dtype)

    def own_copy(self, z):
        if self.line_first:
            return pltpu.make_async_copy(self.pair_all, self.fourth.own_slot(z), self.own_sem)
        return pltpu.make_async_copy(self.sums, self.gather.own_slot(z), self.own_sem)

    def start_one(self, k, p):
        if not self.line_first:
            self.scatter.start_one(k, p)

    def plan(self, plan, begin=0.0, start=True):
        if not self.line_first:
            for p in range(self.pieces):
                then = plan_gather(plan, self.gather, p)
                plan_scatter(plan, self.scatter, p, self.put, then, begin, start)
            return
        n = plan.job()
        time = 2 * self.second.bytes / LINK_BYTES_PER_US * (self.grid[2] - 1)
        along = plan_gather(plan, self.fourth, 0)

        def cross(z):
            return (lambda: self.second.start_one(0, 0)), [("x", time, z, (n, "c"))]

        plan_scatter(plan, self.first, 0, self.put_pair, cross, begin)
        for z in range(self.grid[1]):

            def across(z=z):
                self.second.total(0, 0, self.put)
                self.third.start(0, 0)
                at = pl.multiple_of(self.third.b * self.third.rows_all, self.third.rows_all)
                self.pair_all[pl.ds(at, self.third.rows_all), :] = self.sums[...]

            plan.add(z, [(n, "c")], across, [("x", time, z, (n, "x"))])
            follow, sends = along(z)

            def spread(follow=follow):
                self.third.arrived_across(0, 0)
                follow()

            plan.add(z, [(n, "x")], spread, sends)

    def finish(self, z):
        self.own_copy(z).start()
        if self.line_first:
            self.first.finish(z)
            self.second.finish(0)
            self.third.wait_sends(0)
            self.fourth.finish(z)
        else:
            self.scatter.finish(z)
            self.gather.finish(z)
        self.own_copy(z).wait()


def hbm():
    return pl.BlockSpec(memory_space=pl.ANY)


def vmem():
    return pl.BlockSpec(memory_space=pltpu.VMEM)


def params(number, mib=56):
    return pltpu.CompilerParams(
        collective_id=number, has_side_effects=True, vmem_limit_bytes=mib * 1024 * 1024
    )


class Taker:
    def __init__(self, refs):
        self.refs = list(refs)

    def take(self, count):
        taken = self.refs[:count]
        del self.refs[:count]
        return taken

    def one(self):
        return self.take(1)[0]


ALWAYS = (0.0, 1e9)


def gather_rows(arrays, side_arrays, number, pieces):
    grid, side = grid_of("expert"), grid_of("shard")
    values = list(arrays) + list(side_arrays)
    grids = [grid] * len(arrays) + [side] * len(side_arrays)
    n = len(values)

    def kernel(*refs):
        take = Taker(refs)
        ins, outs, own_sems = take.take(n), take.take(n), take.one()
        jobs = [Gather(grids[i], ins[i], outs[i], pieces[i], take.take(4)) for i in range(n)]

        def own(i, z):
            return pltpu.make_async_copy(ins[i], jobs[i].own_slot(z), own_sems.at[i])

        def each(i, act):
            at_each_line(grids[i], act)

        for i in range(n):
            each(i, lambda z, i=i: own(i, z).start())
        greet([grid] + ([side] if side_arrays else []))
        plan = Plan(grid[1])
        for i in range(len(arrays)):
            for p in range(pieces[i]):
                plan_gather(plan, jobs[i], p, 0.0)
        order = plan.order()
        plan.run(grid, order, 0.0, 1.0)
        late = 0.0 if not side_arrays else 1.0
        for i in range(len(arrays), n):
            for p in range(pieces[i]):
                each(i, lambda z, i=i, p=p: jobs[i].start(z, p))
        if side_arrays:
            edge = 2 * jobs[-1].bytes / LINK_BYTES_PER_US + 4.0
            begin = late
            for p in range(pieces[-1]):
                plan.run(grid, order, begin, edge * (p + 1))
                begin = edge * (p + 1)
                for i in range(len(arrays), n):

                    def forward(z, i=i, p=p):
                        for origin in range(grids[i][1]):
                            if origin != z:
                                jobs[i].forward(z, origin, p)

                    each(i, forward)
            plan.run(grid, order, begin, 1e9)
        else:
            plan.run(grid, order, 1.0, 1e9)
        for i in range(n):
            each(i, lambda z, i=i: jobs[i].finish(z))
            each(i, lambda z, i=i: own(i, z).wait())

    scratch = [pltpu.SemaphoreType.DMA((n,))]
    for g, p in zip(grids, pieces):
        scratch += Gather.sems(g, p)
    return pl.pallas_call(
        kernel,
        out_shape=[
            jax.ShapeDtypeStruct((g[1] * g[2] * a.shape[0], a.shape[1]), a.dtype)
            for a, g in zip(values, grids)
        ],
        in_specs=[hbm()] * n,
        out_specs=[hbm()] * n,
        scratch_shapes=scratch,
        compiler_params=params(number),
        name="gather_rows",
    )(*values)


def scatter_rows(parts, axis, number, pieces):
    grid = grid_of(axis)
    columns = parts.shape[1]
    count = parts.shape[0] // (grid[1] * grid[2])

    def kernel(parts_ref, out_ref, cross, right, left, *sems):
        greet([grid])
        job = Scatter(grid, parts_ref, (cross, right, left), pieces, sems)

        def put(at, total):
            out_ref[at, :] = total

        plan = Plan(grid[1])
        for p in range(pieces):
            plan_scatter(plan, job, p, put)
        plan.run(grid, plan.order(), *ALWAYS)
        at_each_line(grid, job.finish)

    return pl.pallas_call(
        kernel,
        out_shape=jax.ShapeDtypeStruct((count, columns), F32),
        in_specs=[vmem()],
        out_specs=vmem(),
        scratch_shapes=Scatter.buffers(grid, count, columns, parts.dtype)
        + Scatter.sems(grid, pieces),
        compiler_params=params(number),
        name="scatter_" + axis,
    )(parts)


def sum_and_gather(across_first, line_first, small, rows, spread, number):
    grid, side = grid_of("expert"), grid_of("shard")
    size = grid[1] * grid[2]
    shards = side[1] * side[2]
    values = [across_first, line_first, small]
    moved = [small] + list(rows)
    m = len(moved)
    kinds = [(2, False), (1, True), (1, False)]

    def kernel(*refs):
        take = Taker(refs)
        first_ref, second_ref, spread_ref = take.take(3)
        side_ins = take.take(m)
        outs, rows_outs, spread_out = take.take(3), take.take(m - 1), take.one()
        small_all, small_parts, own_sems = take.take(3)
        ins = [first_ref, second_ref, small_parts]
        jobs = [
            Reduce(grid, ins[i], outs[i], take.take(Reduce.refs(kinds[i][1])), *kinds[i])
            for i in range(3)
        ]
        spread_job = Scatter(side, spread_ref, take.take(3), 1, take.take(6))
        side_outs = [small_all] + rows_outs
        side_jobs = [Gather(side, side_ins[i], side_outs[i], 1, take.take(4)) for i in range(m)]

        def own(z, i):
            return pltpu.make_async_copy(side_ins[i], side_jobs[i].own_slot(z), own_sems.at[i])

        def begin_side(z):
            for i in range(m):
                own(z, i).start()

        at_each_line(side, begin_side)
        greet([grid, side])
        edges = [0.0, 6.0, 16.0, 28.0, 55.0]
        plan = Plan(grid[1])
        jobs[1].plan(plan)
        jobs[0].plan(plan)
        jobs[2].plan(plan, edges[3])
        order = plan.order()
        plan.run(grid, order, 0.0, edges[1])
        at_each_line(side, lambda z: side_jobs[0].start(z, 0))
        plan.run(grid, order, edges[1], edges[2])

        def forward(z, chosen):
            for origin in range(side[1]):
                if origin != z:
                    for job in chosen:
                        job.forward(z, origin, 0)

        def start(z):
            forward(z, side_jobs[:1])
            for job in side_jobs[1:]:
                job.start(z, 0)
            for k in targets(side[1], z):
                spread_job.start_one(k, 0)

        at_each_line(side, start)
        plan.run(grid, order, edges[2], edges[3])

        def end_small(z):
            side_jobs[0].finish(z)
            own(z, 0).wait()

        at_each_line(side, end_small)
        count = small.shape[0]
        total = small_all[pl.ds(0, count), :]
        for s in range(1, shards):
            total = total + small_all[pl.ds(s * count, count), :]
        small_parts[...] = total
        plan.run(grid, order, edges[3], edges[4])

        def spread_on(z):
            for k in targets(side[1], z)[:-1]:
                spread_job.reduce_one(z, k, 0)
            forward(z, side_jobs[1:])

        at_each_line(side, spread_on)
        plan.run(grid, order, edges[4], 1e9)

        def end(z):
            for job in jobs:
                job.finish(z)

        at_each_line(grid, end)

        def put_spread(at, total):
            spread_out[at, :] = total

        def end_rows(z):
            spread_job.total(z, 0, put_spread)
            spread_job.finish(z)
            for i in range(1, m):
                side_jobs[i].finish(z)
                own(z, i).wait()

        at_each_line(side, end_rows)

    scratch = [
        pltpu.VMEM((shards * small.shape[0], small.shape[1]), small.dtype),
        pltpu.VMEM(small.shape, small.dtype),
        pltpu.SemaphoreType.DMA((m,)),
    ]
    for a, kind in zip(values, kinds):
        scratch += Reduce.scratch(grid, a.shape[0], a.shape[1], a.dtype, *kind)
    spread_rows = spread.shape[0] // shards
    scratch += Scatter.buffers(side, spread_rows, spread.shape[1], BF) + Scatter.sems(side, 1)
    for _ in range(m):
        scratch += Gather.sems(side, 1)
    out = pl.pallas_call(
        kernel,
        out_shape=[jax.ShapeDtypeStruct(a.shape, a.dtype) for a in values]
        + [jax.ShapeDtypeStruct((shards * a.shape[0], a.shape[1]), a.dtype) for a in rows]
        + [jax.ShapeDtypeStruct((spread_rows, spread.shape[1]), F32)],
        in_specs=[vmem()] * 3 + [hbm()] * m,
        out_specs=[hbm()] * (2 + m) + [vmem()],
        scratch_shapes=scratch,
        compiler_params=params(number),
        name="sum_and_gather",
    )(across_first, line_first, spread, small, *rows)
    return out[:3], out[3:-1], out[-1]


CHUNK_US = 4.0
PAIR_US = 1.5
HEAD_US = 5.5
TILE_US = 1.5
EXTRA = 128


def share_of(columns):
    return 4 * columns // 5 // 256 * 256


def expert_rows(normed, cot, gates, weights_rel, own, number):
    grid, side = grid_of("expert"), grid_of("shard")
    _, lines, width, _ = grid
    size = lines * width
    shards = side[1] * side[2]
    experts, hidden, columns = weights_rel[0].shape
    full = shards * hidden
    both = 2 * full
    total_rows = normed.shape[0]
    count = total_rows // size
    pair = width * count
    tile = 256
    half = 512
    wide = 2 * hidden
    extra = EXTRA
    orders = [targets(lines, z) for z in range(lines)]
    out_tiles = columns // tile
    grad_tiles = experts * 3 * full // wide
    out_us, grad_us = 1.3, 2.3

    def kernel(*refs):
        take = Taker(refs)
        normed_hbm, cot_hbm, gates_ref = take.take(3)
        gate_hbm, up_hbm, down_hbm = take.take(shards), take.take(shards), take.take(shards)
        residual_hbm, own_gates, router, norm_gain = take.take(4)
        d_residual, d_logits, norm_gain_grad, d_attn = take.take(4)
        out_hbm = take.one()
        grad_hbm = take.take(3)
        normed_v, cot_v, weights, down = take.take(4)
        grads_low, act_low, parts = take.take(3)
        buffers = take.take(3)
        out_stage, grad_stage, d_gates_ref = take.take(3)
        sum_ref, residual, d_low = take.take(3)
        load_sems, weight_sems, out_sems, grad_sems = take.take(4)
        rows_job = Gather(side, d_low, d_attn, 2, take.take(4))
        job = Scatter(grid, parts, buffers, 1, take.take(6))
        me, z, _ = position(grid)

        def put(at, total):
            sum_ref[at, :] = total

        plan = Plan(lines)
        plan_scatter(
            plan, job, 0, put, None, [(i + 1) * CHUNK_US for i in range(lines)], False
        )
        order = plan.order()
        shard = lax.axis_index("shard")
        near = shard + 1 - 2 * (shard % 2)
        places = [shard, near, (shard + 2) % shards, (near + 2) % shards]

        loads = [
            pltpu.make_async_copy(normed_hbm, normed_v, load_sems.at[0]),
            pltpu.make_async_copy(cot_hbm, cot_v, load_sems.at[1]),
        ]
        residual_load = pltpu.make_async_copy(residual_hbm, residual, load_sems.at[2])
        weight_loads = [[] for _ in range(experts)]
        for j in range(experts):
            for r in range(shards):
                for w, (source, target) in enumerate(
                    (
                        (gate_hbm[r].at[j], weights.at[pl.ds(j * both + r * hidden, hidden)]),
                        (up_hbm[r].at[j], weights.at[pl.ds(j * both + full + r * hidden, hidden)]),
                        (down_hbm[r].at[j], down.at[pl.ds(j * full + r * hidden, hidden)]),
                    )
                ):
                    weight_loads[j].append(
                        pltpu.make_async_copy(source, target, weight_sems.at[j, r, w])
                    )
        for c in loads + weight_loads[0]:
            c.start()
        for j in range(1, experts):
            for c in weight_loads[j]:
                c.start()
        residual_load.start()
        greet([grid, side])
        for c in loads:
            c.wait()

        for j in range(experts):
            for c in weight_loads[j]:
                c.wait()

            @pl.loop(0, total_rows // half)
            def _(m):
                rows = pl.ds(pl.multiple_of(m * half, half), half)

                @pl.loop(0, full // tile)
                def _(t):
                    at = t * tile

                    def lines_of(base):
                        return pl.ds(pl.multiple_of(base + at, tile), tile)

                    x = normed_v[rows, :]
                    gate_pre = dot_nt(x, weights[lines_of(j * both), :])
                    up_pre = dot_nt(x, weights[lines_of(j * both + full), :])
                    back = dot_nt(cot_v[rows, :], down[lines_of(j * full), :])
                    probs = gates_ref[rows, j : j + 1]
                    sig = 0.5 + 0.5 * jnp.tanh(0.5 * gate_pre)
                    silu = gate_pre * sig
                    act = silu * up_pre
                    act_low[rows, lines_of(j * full)] = (act * probs).astype(BF)
                    d_act = back * probs
                    d_gate = d_act * up_pre * (sig * (1.0 + gate_pre * (1.0 - sig)))
                    grads_low[rows, lines_of(j * both)] = d_gate.astype(BF)
                    grads_low[rows, lines_of(j * both + full)] = (d_act * silu).astype(BF)
                    part = jnp.sum(act * back, axis=1, keepdims=True)

                    @pl.when(t == 0)
                    def _():
                        d_gates_ref[rows, j : j + 1] = part

                    @pl.when(t > 0)
                    def _():
                        d_gates_ref[rows, j : j + 1] = d_gates_ref[rows, j : j + 1] + part

        lane = lax.broadcasted_iota(jnp.int32, (count, extra), 1)

        @pl.loop(0, size)
        def _(e):
            rows = pl.ds(pl.multiple_of(e * count, count), count)
            block = jnp.zeros((count, extra), F32)
            for j in range(experts):
                value = d_gates_ref[rows, j : j + 1]
                high = value.astype(BF).astype(F32)
                mine = me * experts + j
                block = jnp.where(lane == mine, high, block)
                block = jnp.where(lane == mine + size * experts, value - high, block)
            parts[rows, columns:] = block.astype(BF)

        @pl.loop(0, lines)
        def _(i):
            k = jnp.int32(0)
            for at in range(lines):
                for step in range(lines):
                    k = jnp.where(jnp.logical_and(z == at, i == step), orders[at][step], k)
            rows = pl.ds(pl.multiple_of(k * pair, pair), pair)

            @pl.loop(0, columns // tile)
            def _(t):
                cols = pl.ds(pl.multiple_of(t * tile, tile), tile)
                value = dot(grads_low[rows, :], weights[:, cols])
                parts[rows, cols] = value.astype(BF)

            job.start_one(k, 0)

        begin = lines * CHUNK_US

        def out_copy(t, slot):
            cols = pl.ds(pl.multiple_of(t * tile, tile), tile)
            return pltpu.make_async_copy(
                out_stage.at[slot], out_hbm.at[:, cols], out_sems.at[slot]
            )

        plan.run(grid, order, -1.0, begin)

        @pl.loop(0, out_tiles)
        def _(t):
            slot = t % 2

            @pl.when(t >= 2)
            def _():
                out_copy(t - 2, slot).wait()

            cols = pl.ds(pl.multiple_of(t * tile, tile), tile)
            out_stage[slot, :, :] = dot(act_low[...], down[:, cols]).astype(BF)
            out_copy(t, slot).start()
            plan.run_step(grid, order, t, begin, out_us, out_tiles)

        begin = begin + out_tiles * out_us

        def grad_copies(kind, j, r, slot):
            copies = []
            for h in range(2):
                place = places[h]
                for step in range(1, shards // 2):
                    place = jnp.where(r == step, places[2 * step + h], place)
                copies.append(
                    pltpu.make_async_copy(
                        grad_stage.at[slot, pl.ds(h * hidden, hidden)],
                        grad_hbm[kind].at[place, j],
                        grad_sems.at[slot, h],
                    )
                )
            return copies

        per = full // wide

        def norm_backward():
            ext = sum_ref[:, columns:]
            d_gates = ext + pltpu.roll(ext, extra - size * experts, 1)
            probs = own_gates[...]
            inner = jnp.sum(probs * d_gates, axis=-1, keepdims=True)
            low = (probs * (d_gates - inner)).astype(BF)
            d_logits[...] = low
            for q in range(columns // half):
                cols = pl.ds(q * half, half)
                sum_ref[:, cols] = sum_ref[:, cols] + dot_nt(low, router[cols, :])
            norm_gain_grad[...] = jnp.zeros_like(norm_gain_grad)
            residual_load.wait()

            @pl.loop(0, count // 16)
            def _(i):
                rows = pl.ds(pl.multiple_of(i * 16, 16), 16)
                grad = sum_ref[rows, :columns]
                value = residual[rows, :]
                inverse = lax.rsqrt(jnp.mean(value * value, axis=-1, keepdims=True) + EPS)
                norm_gain_grad[0:1, :] = norm_gain_grad[0:1, :] + jnp.sum(
                    grad * value * inverse, axis=0, keepdims=True
                )
                back = rms_backward(value, inverse, norm_gain[...], grad)
                back = back + cot_v[pl.ds(pl.multiple_of(me * count + i * 16, 16), 16), :].astype(F32)
                d_residual[rows, :] = back
                d_low[rows, :] = back.astype(BF)

            def start(z):
                for p in range(2):
                    rows_job.start(z, p)

            at_each_line(side, start)

        def rows_forward(z):
            for p in range(2):
                for origin in range(side[1]):
                    if origin != z:
                        rows_job.forward(z, origin, p)

        def rows_end(z):
            own_rows = pltpu.make_async_copy(d_low, rows_job.own_slot(z), load_sems.at[3])
            own_rows.start()
            rows_job.finish(z)
            own_rows.wait()

        for kind in range(3):
            if kind == 2:
                plan.run(grid, order, begin, 1e9)
                norm_backward()

            @pl.loop(0, experts * per)
            def _(i):
                j, r = i // per, i % per
                slot = i % 2
                if kind == 2:
                    low, base, rows_v = act_low, j * full, cot_v
                else:
                    low, base, rows_v = grads_low, j * both + kind * full, normed_v
                lanes = pl.ds(pl.multiple_of(base + r * wide, wide), wide)

                @pl.when(i >= 2)
                def _():
                    for c in grad_copies(kind, (i - 2) // per, (i - 2) % per, slot):
                        c.wait()

                for q in range(2):
                    cols = pl.ds(q * columns // 2, columns // 2)
                    value = dot_tn(low[:, lanes], rows_v[:, cols])
                    grad_stage[slot, :, cols] = value.astype(BF)
                for c in grad_copies(kind, j, r, slot):
                    c.start()
                if kind < 2:
                    plan.run_step(grid, order, i, begin, grad_us, experts * per)

            for i in range(max(0, experts * per - 2), experts * per):
                for c in grad_copies(kind, i // per, i % per, i % 2):
                    c.wait()
            begin = begin + experts * per * grad_us

        at_each_line(side, rows_forward)
        for t in range(max(0, out_tiles - 2), out_tiles):
            out_copy(t, t % 2).wait()
        at_each_line(side, rows_end)
        at_each_line(grid, job.finish)

    dma = pltpu.SemaphoreType.DMA
    weight_shape = jax.ShapeDtypeStruct((shards, experts, hidden, columns), BF)
    return pl.pallas_call(
        kernel,
        out_shape=[
            jax.ShapeDtypeStruct((count, columns), F32),
            jax.ShapeDtypeStruct((count, extra), BF),
            jax.ShapeDtypeStruct((8, columns), F32),
            jax.ShapeDtypeStruct((shards * count, columns), BF),
            jax.ShapeDtypeStruct((total_rows, columns), BF),
            weight_shape,
            weight_shape,
            weight_shape,
        ],
        in_specs=[hbm()] * 2 + [vmem()] + [hbm()] * (3 * shards) + [hbm()] + [vmem()] * 3,
        out_specs=[vmem()] * 3 + [hbm()] * 5,
        scratch_shapes=[
            pltpu.VMEM((total_rows, columns), BF),
            pltpu.VMEM((total_rows, columns), BF),
            pltpu.VMEM((experts * both, columns), BF),
            pltpu.VMEM((experts * full, columns), BF),
            pltpu.VMEM((total_rows, experts * both), BF),
            pltpu.VMEM((total_rows, experts * full), BF),
            pltpu.VMEM((total_rows, columns + extra), BF),
        ]
        + Scatter.buffers(grid, count, columns + extra, BF)
        + [
            pltpu.VMEM((2, total_rows, tile), BF),
            pltpu.VMEM((2, wide, columns), BF),
            pltpu.VMEM((total_rows, experts), F32),
            pltpu.VMEM((count, columns + extra), F32),
            pltpu.VMEM((count, columns), F32),
            pltpu.VMEM((count, columns), BF),
            dma((4,)),
            dma((experts, shards, 3)),
            dma((2,)),
            dma((2, 2)),
        ]
        + Gather.sems(side, 2)
        + Scatter.sems(grid, 1),
        compiler_params=params(number, 63),
        name="expert_rows",
    )(normed, cot, gates, *weights_rel, *own)


def rms_forward(vector, gain):
    inverse = lax.rsqrt(jnp.mean(vector * vector, axis=-1, keepdims=True) + EPS)
    return vector * inverse * gain, inverse


def rms_backward(vector, inverse, gain, grad):
    scaled = grad * gain
    inner = jnp.mean(scaled * vector, axis=-1, keepdims=True)
    return inverse * scaled - vector * (inverse * inverse * inverse * inner)


def attention_backward(arrays, heads, number):
    grid, side = grid_of("expert"), grid_of("shard")
    _, lines, width, _ = grid
    size = lines * width
    shards = side[1] * side[2]
    names = list(arrays)
    tokens, columns = arrays["d_attn"].shape
    own_rows = tokens // shards
    inner = arrays["mixed"].shape[1]
    head = inner // heads
    count = inner // size
    pair = width * count
    tile = 256
    scale = head ** (-0.5)
    block = min(256, tokens)
    orders = [targets(lines, z) for z in range(lines)]
    split = [share_of(columns), columns - share_of(columns)]
    kinds = [(2, False), (1, True)]
    share = share_of(inner + 2 * head)

    def kernel(*refs):
        take = Taker(refs)
        hbm_refs = take.take(len(names))
        grad_refs = take.take(2)
        input_grad_ref, norm_gain_ref, gains_ref = take.take(3)
        sum_refs = take.take(2)
        v = dict(zip(names, take.take(len(names))))
        d_mixed, bias, dk, dv, lines_ref, d_norm_ref = take.take(6)
        parts = take.take(2)
        jobs = [
            Reduce(grid, parts[i], sum_refs[i], take.take(Reduce.refs(kinds[i][1])), *kinds[i])
            for i in range(2)
        ]
        side_parts = take.one()
        side_buffers = take.take(3)
        load_sems = take.one()
        side_job = Scatter(side, side_parts, side_buffers, 2, take.take(6))
        me, z, _ = position(grid)
        plan = Plan(lines)
        for job in jobs:
            job.plan(plan, [(i + 1) * PAIR_US for i in range(lines)], False)
        order = plan.order()

        loads = [
            pltpu.make_async_copy(ref, v[name], load_sems.at[i])
            for i, (name, ref) in enumerate(zip(names, hbm_refs))
        ]
        for c in loads:
            c.start()
        greet([grid, side])

        for c in loads[:2]:
            c.wait()
        d_attn = v["d_attn"]

        @pl.loop(0, lines)
        def _(i):
            k = jnp.int32(0)
            for at in range(lines):
                for step in range(lines):
                    k = jnp.where(jnp.logical_and(z == at, i == step), orders[at][step], k)
            lanes = pl.ds(pl.multiple_of(k * pair, pair), pair)

            rows = pl.ds(pl.multiple_of(k * pair, pair), pair)
            first = 0
            for n in range(2):

                value = dot_tn(v["mixed"][:, lanes], d_attn[:, first : first + split[n]])
                parts[n][rows, :] = value.astype(BF)
                first += split[n]
                for p in range(kinds[n][0]):
                    jobs[n].start_one(k, p)

        for c in loads[2:]:
            c.wait()
        rows_at = lax.broadcasted_iota(jnp.int32, (tokens, tokens), 0)
        cols_at = lax.broadcasted_iota(jnp.int32, (tokens, tokens), 1)
        allowed = jnp.logical_and(v["doc_col"][...] == v["doc_row"][...], rows_at >= cols_at)
        bias[...] = jnp.where(allowed, 0.0, -1e30)
        dk[...] = jnp.zeros_like(dk)
        dv[...] = jnp.zeros_like(dv)
        gains_ref[...] = jnp.zeros_like(gains_ref)

        @pl.loop(0, inner // tile)
        def _(t):
            rows = pl.ds(pl.multiple_of(t * tile, tile), tile)
            d_mixed[:, rows] = dot_nt(d_attn[...], v["out_weight"][rows, :]).astype(BF)

        def unturn(grad):
            turned = pltpu.roll(grad * v["sine"][...], head // 2, 1)
            return grad * v["cosine"][...] + turned

        def unnorm(grad, linear, gain, row):
            inverse = lax.rsqrt(jnp.mean(linear * linear, axis=-1, keepdims=True) + EPS)
            gains_ref[row : row + 1, :] = gains_ref[row : row + 1, :] + jnp.sum(
                grad * linear * inverse, axis=0, keepdims=True
            )
            return rms_backward(linear, inverse, gain, grad)

        begin = lines * PAIR_US + 3.0

        @pl.loop(0, heads)
        def _(h):
            lanes = pl.ds(pl.multiple_of(h * head, head), head)
            grads = []
            for first in range(0, tokens, block):
                rows = pl.ds(first, block)
                keys = pl.ds(0, first + block)
                query = v["query"][rows, lanes]
                scores = dot_nt(query, v["key"][keys, :])
                probs = jnp.exp(scores * scale + bias[rows, keys] - v["log_total"][h, rows, :])
                back = d_mixed[rows, lanes]
                d_probs = dot_nt(back, v["value"][keys, :])
                inner_sum = jnp.sum(probs * d_probs, axis=-1, keepdims=True)
                d_scores = (probs * (d_probs - inner_sum)).astype(BF)
                dv[keys, :] = dv[keys, :] + dot_tn(probs.astype(BF), back)
                dk[keys, :] = dk[keys, :] + dot_tn(d_scores, query)
                grads.append(dot(d_scores, v["key"][keys, :]))
            grad = jnp.concatenate(grads, axis=0) * scale
            grad = unnorm(unturn(grad), v["query_lin"][:, lanes], v["query_gain"][...], 0)
            lines_ref[:, lanes] = grad.astype(BF)
            plan.run_step(grid, order, h, begin, HEAD_US, heads, True)

        grad = unnorm(unturn(dk[...] * scale), v["key_lin"][...], v["key_gain"][...], 1)
        lines_ref[:, inner : inner + head] = grad.astype(BF)
        lines_ref[:, inner + head : inner + 2 * head] = dv[...].astype(BF)

        @pl.loop(0, columns // tile)
        def _(t):
            rows = pl.ds(pl.multiple_of(t * tile, tile), tile)
            value = dot_nt(lines_ref[:, :inner], v["query_weight"][rows, :])
            value = value + dot_nt(lines_ref[:, inner : inner + head], v["key_weight"][rows, :])
            value = value + dot_nt(lines_ref[:, inner + head :], v["value_weight"][rows, :])
            side_parts[:, rows] = value.astype(BF)

        def put_norm(at, total):
            d_norm_ref[at, :] = total

        side_plan = Plan(side[1])
        for p in range(2):
            plan_scatter(side_plan, side_job, p, put_norm)
        side_order = side_plan.order()

        def side_begin(z):
            for _, act in side_order[z][:-2]:
                act()

        def side_end(z):
            for _, act in side_order[z][-2:]:
                act()

        at_each_line(side, side_begin)
        middle = begin + heads * HEAD_US
        tiles = columns // tile

        @pl.loop(0, tiles)
        def _(t):
            rows = pl.ds(pl.multiple_of(t * tile, tile), tile)
            value = dot_tn(v["normed"][:, rows], lines_ref[...])
            grad_refs[0][rows, :] = value[:, :share].astype(BF)
            grad_refs[1][rows, :] = value[:, share:].astype(BF)
            plan.run_step(grid, order, t, middle, TILE_US, tiles)

        at_each_line(side, side_end)
        plan.run(grid, order, middle + tiles * TILE_US, middle + tiles * TILE_US + 6.0)

        norm_gain_ref[...] = jnp.zeros_like(norm_gain_ref)

        @pl.loop(0, own_rows // 16)
        def _(i):
            rows = pl.ds(pl.multiple_of(i * 16, 16), 16)
            value = v["input_own"][rows, :].astype(F32)
            grad = d_norm_ref[rows, :]
            inverse = lax.rsqrt(jnp.mean(value * value, axis=-1, keepdims=True) + EPS)
            norm_gain_ref[0:1, :] = norm_gain_ref[0:1, :] + jnp.sum(
                grad * value * inverse, axis=0, keepdims=True
            )
            back = rms_backward(value, inverse, v["norm_gain"][...], grad)
            input_grad_ref[rows, :] = (v["d_residual"][rows, :] + back).astype(BF)

        plan.run(grid, order, middle + tiles * TILE_US + 6.0, 1e9)

        def end(z):
            for job in jobs:
                job.finish(z)

        at_each_line(grid, end)
        at_each_line(side, side_job.finish)

    dma = pltpu.SemaphoreType.DMA
    values = [arrays[name] for name in names]
    out = pl.pallas_call(
        kernel,
        out_shape=[
            jax.ShapeDtypeStruct((columns, share), BF),
            jax.ShapeDtypeStruct((columns, inner + 2 * head - share), BF),
            jax.ShapeDtypeStruct((own_rows, columns), BF),
            jax.ShapeDtypeStruct((8, columns), F32),
            jax.ShapeDtypeStruct((8, head), F32),
            jax.ShapeDtypeStruct((inner, split[0]), BF),
            jax.ShapeDtypeStruct((inner, split[1]), BF),
        ],
        in_specs=[hbm()] * len(names),
        out_specs=[vmem()] * 5 + [hbm()] * 2,
        scratch_shapes=[pltpu.VMEM(a.shape, a.dtype) for a in values]
        + [
            pltpu.VMEM((tokens, inner), BF),
            pltpu.VMEM((tokens, tokens), F32),
            pltpu.VMEM((tokens, head), F32),
            pltpu.VMEM((tokens, head), F32),
            pltpu.VMEM((tokens, inner + 2 * head), BF),
            pltpu.VMEM((own_rows, columns), F32),
            pltpu.VMEM((inner, split[0]), BF),
            pltpu.VMEM((inner, split[1]), BF),
        ]
        + Reduce.scratch(grid, inner, split[0], BF, *kinds[0])
        + Reduce.scratch(grid, inner, split[1], BF, *kinds[1])
        + [pltpu.VMEM((tokens, columns), BF)]
        + Scatter.buffers(side, own_rows, columns, BF)
        + [dma((len(names),))]
        + Scatter.sems(side, 2),
        compiler_params=params(number),
        name="attention_backward",
    )(*values)
    first, second, input_grad, norm_gain, gains, *out_sums = out
    out_sum = jnp.concatenate(out_sums, axis=1)
    return (first, second), input_grad, norm_gain[0], gains[0], gains[1], out_sum


def rope_tables(positions, head_size):
    half_size = head_size // 2
    frequency = THETA ** (-2.0 * jnp.arange(half_size, dtype=F32) / head_size)
    angles = positions.astype(F32)[:, None] * frequency[None, :]
    return (jnp.cos(angles), jnp.sin(angles))


def apply_rotary(vector, cosine_table, sine_values):
    half_size = vector.shape[-1] // 2
    first_half = vector[..., :half_size]
    second_half = vector[..., half_size:]
    cos_rows = cosine_table[:, None, :]
    sin_rows = sine_values[:, None, :]
    return jnp.concatenate(
        [
            first_half * cos_rows - second_half * sin_rows,
            second_half * cos_rows + first_half * sin_rows,
        ],
        axis=-1,
    )


def root_mean_norm_forward(vector, gain):
    return rms_forward(vector, gain)[0]


def doc_positions(doc_ids):
    row_index = jnp.arange(doc_ids.shape[0], dtype=jnp.int32)
    doc_starts = jnp.concatenate([jnp.ones((1,), jnp.bool_), doc_ids[1:] != doc_ids[:-1]])
    first_row = lax.cummax(jnp.where(doc_starts, row_index, 0), axis=0)
    return row_index - first_row


def from_near(rows, count):
    return lax.ppermute(rows, "shard", [(s, s + 1 - 2 * (s % 2)) for s in range(count)])


def from_far(rows, count):
    return lax.ppermute(rows, "shard", [(s, (s + 2) % count) for s in range(count)])


def local(
    layer_input,
    doc_ids,
    routes,
    norm1_gain,
    query_weight,
    key_matrix,
    value_matrix,
    query_norm_gain,
    key_norm_gain,
    out_weight,
    norm2_gain,
    router_weight,
    gate_weight,
    up_weight,
    down_weight,
    cotangent,
):
    tokens_here, model_width = layer_input.shape
    head_size = query_norm_gain.shape[0]
    heads_here = query_weight.shape[1] // head_size
    kv_here = key_matrix.shape[1] // head_size
    group_size = heads_here // kv_here
    experts_all = router_weight.shape[1]
    local_experts, _, hidden_here = gate_weight.shape
    expert_peers = lax.axis_size("expert")
    shard_count = lax.axis_size("shard")
    rows_here = tokens_here // shard_count
    shard_index = lax.axis_index("shard")
    expert_index = lax.axis_index("expert")
    score_scale = head_size ** (-0.5)
    hidden_all = shard_count * local_experts * hidden_here

    def own(rows):
        return lax.dynamic_slice_in_dim(rows, shard_index * rows_here, rows_here, axis=0)

    def gather_weight(weight):
        return lax.all_gather(weight, "shard", axis=0).reshape(hidden_all, model_width)

    fused = expert_peers * rows_here <= VMEM_ROWS
    cot_own = own(cotangent)
    cot_all = lax.all_gather(cot_own, "expert", axis=0, tiled=True)
    routes_own = own(routes)
    experts = jnp.arange(experts_all, dtype=jnp.int32)
    chosen_own = jnp.any(routes_own[:, :, None] == experts[None, None, :], axis=1)
    gate_weight = jnp.swapaxes(gate_weight, 1, 2)
    up_weight = jnp.swapaxes(up_weight, 1, 2)
    if fused:
        gate_far = from_far(gate_weight, shard_count)
        gate_near = from_near(gate_weight, shard_count)
    else:
        down_all = gather_weight(down_weight)
        gate_all = gather_weight(gate_weight)
        up_all = gather_weight(up_weight)

    inputs = layer_input.astype(F32)
    norm_one, _ = rms_forward(inputs, norm1_gain)
    first_normed_input = norm_one.astype(BF)
    query_linear = dot(first_normed_input, query_weight).reshape(
        tokens_here, heads_here, head_size
    )
    key_linear = dot(first_normed_input, key_matrix).reshape(tokens_here, kv_here, head_size)
    value_token_rows = (
        dot(first_normed_input, value_matrix).astype(BF).reshape(tokens_here, kv_here, head_size)
    )
    positions = doc_positions(doc_ids)
    cosine_table, sine_values = rope_tables(positions, head_size)

    def head_prep(linear, gain):
        return apply_rotary(root_mean_norm_forward(linear, gain), cosine_table, sine_values)

    query_rotated = head_prep(query_linear, query_norm_gain)
    key_rotated = head_prep(key_linear, key_norm_gain)
    query_low = query_rotated.astype(BF).reshape(tokens_here, kv_here, group_size, head_size)
    key_low = key_rotated.astype(BF)
    row_index = jnp.arange(tokens_here)
    allowed = (doc_ids[:, None] == doc_ids[None, :]) & (row_index[:, None] >= row_index[None, :])

    def masked_scores():
        raw_scores = (
            jnp.einsum("tkgd,skd->kgts", query_low, key_low, preferred_element_type=F32)
            * score_scale
        )
        return jnp.where(allowed, raw_scores, -1e30)

    scores = masked_scores()
    row_max = jnp.max(scores, axis=-1, keepdims=True)
    exp_scores = jnp.exp(scores - row_max)
    row_total = jnp.sum(exp_scores, axis=-1, keepdims=True)
    log_total = row_max + jnp.log(row_total)
    probs_low = (exp_scores / row_total).astype(BF)
    mixture = jnp.einsum(
        "kgts,skd->tkgd", probs_low, value_token_rows, preferred_element_type=F32
    )
    mixed = mixture.astype(BF).reshape(tokens_here, heads_here * head_size)
    attn_part = dot(mixed, out_weight)
    attn_part = attn_part.astype(BF)
    if fused:
        gate_far, attn_part = lax.optimization_barrier((gate_far, attn_part))
    attn_own = scatter_rows(attn_part, "shard", 1, 2)

    if fused:
        up_late, down_late, attn_own = lax.optimization_barrier((up_weight, down_weight, attn_own))
        up_far, down_far = from_far(up_late, shard_count), from_far(down_late, shard_count)
        up_near, down_near = from_near(up_late, shard_count), from_near(down_late, shard_count)
    inputs_own = own(layer_input).astype(F32)
    residual = inputs_own + attn_own
    norm_two, inverse_two = rms_forward(residual, norm2_gain)
    normed_two = norm_two.astype(BF)
    normed_all, chosen_all = gather_rows(
        [normed_two, chosen_own.T.astype(F32)], [], 2, (2, 1)
    )
    if fused:
        up_far, down_far, normed_all = lax.optimization_barrier((up_far, down_far, normed_all))
        weights_rel = []
        for own_one, near, far in (
            (gate_weight, gate_near, gate_far),
            (up_weight, up_near, up_far),
            (down_weight, down_near, down_far),
        ):
            weights_rel += [own_one, near, far, from_near(far, shard_count)]
    chosen_all = chosen_all.reshape(expert_peers, experts_all, rows_here).transpose(0, 2, 1)
    chosen_all = chosen_all.reshape(expert_peers * rows_here, experts_all) > 0.5

    def gate_table(rows, chosen):
        logits = jnp.where(chosen, dot(rows, router_weight), -jnp.inf)
        top = jnp.max(logits, axis=-1, keepdims=True)
        powers = jnp.exp(logits - top)
        return powers / jnp.sum(powers, axis=-1, keepdims=True)

    gates_all = gate_table(normed_all, chosen_all)
    gates_here = lax.dynamic_slice_in_dim(
        gates_all, expert_index * local_experts, local_experts, axis=1
    )
    gates_own = gate_table(normed_two, chosen_own)
    inner = heads_here * head_size
    backward = dict(
        mixed=mixed,
        out_weight=out_weight,
        query=query_low.reshape(tokens_here, inner),
        key=key_low.reshape(tokens_here, head_size),
        value=value_token_rows.reshape(tokens_here, head_size),
        query_lin=query_linear.reshape(tokens_here, inner),
        key_lin=key_linear.reshape(tokens_here, head_size),
        log_total=log_total.reshape(heads_here, tokens_here, 1),
        cosine=jnp.concatenate([cosine_table, cosine_table], axis=1),
        sine=jnp.concatenate([-sine_values, sine_values], axis=1),
        query_gain=query_norm_gain[None, :],
        key_gain=key_norm_gain[None, :],
        doc_col=doc_ids[:, None],
        doc_row=doc_ids[None, :],
        query_weight=query_weight,
        key_weight=key_matrix,
        value_weight=value_matrix,
        normed=first_normed_input,
        input_own=own(layer_input),
        norm_gain=norm1_gain[None, :],
    )
    names = list(backward)
    gates_here, gates_own, *values = lax.optimization_barrier(
        (gates_here, gates_own, *backward.values())
    )
    backward = dict(zip(names, values))

    if fused:
        wide = ((0, 0), (0, EXTRA - experts_all))
        own_arrays = (
            residual,
            jnp.pad(gates_own, wide),
            jnp.pad(router_weight, wide),
            norm2_gain[None, :],
        )
        d_residual, d_logits_low, norm2_grad, d_attn, out_part, *grad_parts = expert_rows(
            normed_all, cot_all, gates_here, weights_rel, own_arrays, 3
        )
        d_logits_low, norm2_grad = d_logits_low[:, :experts_all], norm2_grad[0]
        gate_part, up_part, down_part = grad_parts
    else:
        column_expert = (jnp.arange(hidden_all, dtype=jnp.int32) // hidden_here) % local_experts
        gate_columns = jnp.zeros((1, 1), F32)
        for j in range(local_experts):
            gate_columns = jnp.where(column_expert[None, :] == j, gates_here[:, j : j + 1], gate_columns)

        d_act_raw = dot_nt(cot_all, down_all)
        gate_pre = dot_nt(normed_all, gate_all)
        up_pre = dot_nt(normed_all, up_all)
        sig = jax.nn.sigmoid(gate_pre)
        silu = gate_pre * sig
        act = silu * up_pre
        act_gated = (act * gate_columns).astype(BF)
        d_act = d_act_raw * gate_columns
        d_gate_low = (d_act * up_pre * sig * (1.0 + gate_pre * (1.0 - sig))).astype(BF)
        d_up_low = (d_act * silu).astype(BF)
        act_back = act * d_act_raw
        d_gates_here = jnp.stack(
            [
                jnp.sum(jnp.where(column_expert[None, :] == j, act_back, 0.0), axis=1)
                for j in range(local_experts)
            ],
            axis=-1,
        )
        d_rows = dot(d_gate_low, gate_all) + dot(d_up_low, up_all)
        d_rows_own = scatter_rows(d_rows.astype(BF), "expert", 3, 2)
        out_part = dot(act_gated, down_all).astype(BF)

        def split(grad):
            return grad.astype(BF).reshape(shard_count, local_experts, hidden_here, model_width)

        gate_part = split(dot_tn(d_gate_low, normed_all))
        up_part = split(dot_tn(d_up_low, normed_all))
        down_part = split(dot_tn(act_gated, cot_all))

        d_gates_own = lax.all_to_all(
            d_gates_here.reshape(expert_peers, rows_here, local_experts),
            "expert",
            split_axis=0,
            concat_axis=0,
            tiled=True,
        )
        d_gates_own = jnp.swapaxes(d_gates_own, 0, 1).reshape(rows_here, experts_all)

        d_logits = gates_own * (
            d_gates_own - jnp.sum(gates_own * d_gates_own, axis=-1, keepdims=True)
        )
        d_logits_low = d_logits.astype(BF)
        d_normed_two = d_rows_own + dot_nt(d_logits_low, router_weight)
        norm2_grad = jnp.sum(d_normed_two * residual * inverse_two, axis=0)
        d_residual = cot_own.astype(F32) + rms_backward(
            residual, inverse_two, norm2_gain, d_normed_two
        )
        d_attn = gather_rows([], [d_residual.astype(BF)], 7, (2,))[0]
    router_grad = dot_tn(normed_two, d_logits_low)
    backward = dict(mixed=backward.pop("mixed"), d_attn=d_attn, **backward, d_residual=d_residual)
    out_own = lax.psum_scatter(out_part, "expert", scatter_dimension=0, tiled=True)
    def scatter_grad(grad):
        return lax.psum_scatter(grad, "shard", scatter_dimension=0, tiled=False)

    gate_grad = jnp.swapaxes(scatter_grad(gate_part).astype(F32), 1, 2)
    up_grad = jnp.swapaxes(scatter_grad(up_part).astype(F32), 1, 2)

    line_grads, input_grad_own, norm1_grad, d_query_gain, d_key_gain, out_sum = (
        attention_backward(backward, heads_here, 4)
    )
    share = share_of(inner + 2 * head_size)
    out_own, _ = lax.optimization_barrier((out_own, norm1_grad))
    layer_out_own = (residual + out_own).astype(BF)

    flat = jnp.concatenate(
        [router_grad.T.reshape(-1), norm2_grad, norm1_grad, d_query_gain, d_key_gain]
    )
    small_rows = 8 * expert_peers
    small_columns = -(-flat.shape[0] // (128 * small_rows)) * 128
    small = jnp.pad(flat, (0, small_rows * small_columns - flat.shape[0]))
    (line_first, line_second, small), (input_grad, layer_out), down_sum = sum_and_gather(
        *line_grads,
        small.reshape(small_rows, small_columns),
        (input_grad_own, layer_out_own),
        down_part.reshape(hidden_all, model_width),
        5,
    )
    down_grad = down_sum.reshape(local_experts, hidden_here, model_width)
    query_cols = inner - share
    query_sum = jnp.concatenate([line_first, line_second[:, :query_cols]], axis=1)
    key_sum = line_second[:, query_cols : query_cols + head_size]
    value_sum = line_second[:, query_cols + head_size :]
    small = small.reshape(-1)
    bounds = [experts_all * model_width, model_width, model_width, head_size, head_size]
    taken = []
    at = 0
    for bound in bounds:
        taken.append(small[at : at + bound])
        at += bound
    router_sum, norm2_sum, norm1_sum, query_gain_sum, key_gain_sum = taken
    router_sum = router_sum.reshape(experts_all, model_width).T
    return (
        layer_out,
        input_grad,
        norm1_sum,
        query_sum.astype(F32),
        key_sum.astype(F32),
        value_sum.astype(F32),
        query_gain_sum,
        key_gain_sum,
        out_sum.astype(F32),
        norm2_sum,
        router_sum,
        gate_grad,
        up_grad,
        down_grad,
    )


def solution(mesh):
    return jax.shard_map(
        local,
        mesh=mesh,
        in_specs=(
            P("expert", None),
            P("expert"),
            P("expert", None),
            P(),
            P(None, "shard"),
            P(None, "shard"),
            P(None, "shard"),
            P(),
            P(),
            P("shard", None),
            P(),
            P(),
            P("expert", None, "shard"),
            P("expert", None, "shard"),
            P("expert", "shard", None),
            P("expert", None),
        ),
        out_specs=(
            P("expert", None),
            P("expert", None),
            P(),
            P(None, "shard"),
            P(None, "shard"),
            P(None, "shard"),
            P(),
            P(),
            P("shard", None),
            P(),
            P(),
            P("expert", None, "shard"),
            P("expert", None, "shard"),
            P("expert", "shard", None),
        ),
        check_vma=False,
    )
```

time: 2280 us -> 606 us (0.27)
  waiting for transfers between devices: 1590 us -> 11.8 us
  Pallas kernels: 0 us -> 466 us
  matrix products: 220 us -> 23 us
  blocking collectives: 170 us -> 0 us
  local copies, waits for them, and re-layouts: 153 us -> 33.1 us
  other arithmetic: 98.1 us -> 48.7 us
    all_to_all x3 -> x0, waiting for transfers between devices: 1130 us -> none  [the longest x2 996 us: send_owners(): lax.all_to_all(table, 'expert', split_axis=0, concat_axis=0, tiled=True)]
    pallas_call x0 -> x5, Pallas kernels: none -> 466 us  [the longest x1 142 us: attention_backward(): pl.pallas_call(kernel, out_shape=[jax.ShapeDtypeStruct((columns, share),...]
    psum x3 -> x0, waiting for transfers between devices: 319 us -> none  [the longest x1 269 us: local(): lax.psum(query_grad.astype(jnp.bfloat16), 'expert').astype(jnp.float32)]
    dot_general x29 -> x8, matrix products: 218 us -> 19.5 us  [the longest x6 17.1 us: dot(): return jnp.dot(a, b, preferred_element_type=F32)]
    all_to_all x1 -> x0, blocking collectives: 143 us -> none  [send_tokens(): lax.all_to_all(table, 'expert', split_axis=0, concat_axis=0, tiled=True)]
    reduce_scatter x2 -> x3, waiting for transfers between devices: 134 us -> 0.01 us  [the longest x2 0.01 us: scatter_grad(): return lax.psum_scatter(grad, 'shard', scatter_dimension=0, tiled=False)]
    scatter x2 -> x0, local copies, waits for them, and re-layouts: 76.1 us -> none  [the longest x1 38.1 us: local(): jnp.zeros((experts_all * capacity, model_width), jnp.bfloat16)]
    gather x2 -> x0, local copies, waits for them, and re-layouts: 42.5 us -> none  [the longest x1 21.4 us: local(): output_cols = returned[flat_place].reshape(tokens_here, top_count, -1)]
  transfers between devices with their start and end apart: 10 -> 13, of which waited for: 8 -> 1; matrix products, arithmetic and copies ran while one was open for 13% -> 15% of each run, Pallas kernels for 0% -> 59%
where the time goes in v1:
time: 606 us; the launch traced here: 602 us
  Pallas kernels  466 us (77%)
  other arithmetic  48.7 us (8%)
  local copies, waits for them, and re-layouts  33.1 us (5%)
  matrix products  23 us (4%)
  between operations  14.5 us (2%)
  waiting for transfers between devices  11.8 us (2%)
    pallas_call x1, Pallas kernels, attention_backward(): pl.pallas_call(kernel, out_shape=[jax.ShapeDtypeStruct((columns, share),...  142 us
    pallas_call x1, Pallas kernels, sum_and_gather(): pl.pallas_call(kernel, out_shape=[jax.ShapeDtypeStruct(a.shape, a.dtype)...  140 us
    pallas_call x1, Pallas kernels, expert_rows(): pl.pallas_call(kernel, out_shape=[jax.ShapeDtypeStruct((count, columns),...  113 us
    pallas_call x1, Pallas kernels, gather_rows(): pl.pallas_call(kernel, out_shape=[jax.ShapeDtypeStruct((g[1] * g[2] * a.s...  50.3 us
    pallas_call x1, Pallas kernels, scatter_rows(): pl.pallas_call(kernel, out_shape=jax.ShapeDtypeStruct((count, columns), F...  20.2 us
    dot_general x6, matrix products, dot(): return jnp.dot(a, b, preferred_element_type=F32)  17.1 us
    unnamed x84, local copies, waits for them, and re-layouts  13.6 us
  transfers between devices with their start and end apart: 13, of which 1 were waited for; matrix products, arithmetic and copies ran while one was open for 15% of the time, Pallas kernels for 59%

profile of v1, /device:TPU:8, one launch (start us, length us, event | category | flops | bytes accessed | tf_op | source)
XLA Modules:
  0.0 601.7 jit_solution(3315040255600843933)
XLA Ops:
  7.3 1.6 collective-permute-start
  8.8 1.9 constant_dynamic-slice_fusion
  11.8 1.0 fusion.12
  12.7 2.1 fusion.2
  17.6 1.9 fusion.25
  19.6 2.5 fusion.24
  22.2 4.5 fusion.40.refs_6_
  29.3 1.3 add_rsqrt_fusion
  31.4 1.2 pad_maximum_fusion.2.refs_4_
  32.6 1.8 fusion.39.refs_5_
  35.9 2.2 fusion.1
  38.1 1.8 fusion
  39.9 3.5 fusion.9
  43.4 2.5 copy.109.refs_0_
  45.9 1.0 copy.100
  46.9 2.1 pad.13.refs_17_
  49.0 1.5 copy_bitcast_fusion.refs_3_
  50.5 5.1 convolution_convert_fusion.parts_ref
  55.6 20.2 %scatter_shard.1 = f32[128,2048]{1,0:T(8,128)} custom-call(bf16[512,2048]{1,0:T(8,128)(2,1)} %convolution_convert_fusion.parts_ref), custom_call_target="tpu_custom_call" | custom-call | tf_op jit(solution)/shard_map/scatter_shard/pallas_call | solution.py:626
  75.8 1.6 collective-permute-start.1
  77.9 1.0 pad_maximum_fusion
  80.1 2.3 multiply_reduce_fusion.1
  82.4 1.0 copy-done.5
  83.4 1.0 multiply_convert_fusion.refs_0_
  84.3 50.3 %gather_rows.1 = (bf16[1024,2048]{1,0:T(8,128)(2,1)}, f32[128,128]{1,0:T(8,128)}) custom-call(bf16[128,2048]{1,0:T(8,128)(2,1)} %multiply_convert_fusion.refs_0_, f32[16,128]{1,0:T(8,128)} %convert_bitcast_fusion.4.refs_1_), custom_call_target="tpu_custom_call" | custom-call | tf_op jit(solution)/shard_map/gather_rows/pallas_call | solution.py:594
  134.8 10.5 %collective-permute-done.2.refs_13_ = bf16[2,192,2048]{2,1,0:T(8,128)(2,1)S(1)} collective-permute-done((bf16[2,192,2048]{2,1,0:T(8,128)(2,1)S(1)}, bf16[2,192,2048]{2,1,0:T(8,128)(2,1)S(1)}, u32[]{:S(2)}, u32[]{:S(2)}) %collective-permute-start.2) | collective-permute-done | bytes 1572896 | tf_op jit(solution)/shard_map/ppermute | solution.py:1367
  146.9 1.4 fusion.37
  148.6 3.5 fusion.36
  152.5 1.1 dynamic-slice_divide_fusion.refs_2_
  154.3 1.1 copy-done.18
  155.4 1.1 copy-done.19
  156.6 113.3 %expert_rows.1 = (f32[128,2048]{1,0:T(8,128)}, bf16[128,128]{1,0:T(8,128)(2,1)}, f32[8,2048]{1,0:T(8,128)}, bf16[512,2048]{1,0:T(8,128)(2,1)}, bf16[1024,2048]{1...) custom-call(bf16[1024,2048]{1,0:T(8,128)(2,1)} %get-tuple-element.74, ...), custom_call_target="tpu_custom_call" | custom-call | tf_op jit(solution)/shard_map/expert_rows/pallas_call | solution.py:1046
  271.2 2.0 copy.102.refs_8_
  274.9 141.7 %attention_backward.1 = (bf16[2048,1024]{1,0:T(8,128)(2,1)}, bf16[2048,256]{1,0:T(8,128)(2,1)}, bf16[128,2048]{1,0:T(8,128)(2,1)}, f32[8,2048]{1,0:T(8,128)}, f3...) custom-call(bf16[512,1024]{1,0:T(8,128)(2,1)} %copy.109.refs_0_, ...), custom_call_target="tpu_custom_call" | custom-call | tf_op jit(solution)/shard_map/attention_backward/pallas_call | solution.py:1291
  416.6 0.9 slice.74
  420.8 6.5 %maximum_convert_fusion = f32[1024,2048]{1,0:T(8,128)} fusion(bf16[1024,512]{1,0:T(8,128)(2,1)S(1)} %copy-done.21, bf16[1024,1536]{1,0:T(8,128)(2,1)} %get-tuple-element.117), kind=kLoop, calls=%fused_computation.10 | loop fusion | flops 8388608 | bytes 12582912 | tf_op jit(solution)/shard_map/convert_element_type | solution.py:1653
  427.3 1.9 add_convert_fusion.refs_5_
  429.3 140.1 %sum_and_gather.1 = (bf16[2048,1024]{1,0:T(8,128)(2,1)}, bf16[2048,256]{1,0:T(8,128)(2,1)}, f32[64,640]{1,0:T(8,128)}, bf16[512,2048]{1,0:T(8,128)(2,1)}, bf16[5...) custom-call(bf16[2048,1024]{1,0:T(8,128)(2,1)} %get-tuple-element.102.refs_0_, bf16[2048,256]{1,0:T(8,128)(2,1)} %get-tuple-element.103.refs_1_, ...), custom_call_target="tpu_custom_call" | custom-call | tf_op jit(solution)/shard_map/sum_and_gather/pallas_call | solution.py:746
  569.4 1.0 slice.83
  571.3 6.7 %convert_element_type.105 = f32[2048,1024]{1,0:T(8,128)} convert(bf16[2048,1024]{1,0:T(8,128)(2,1)} %get-tuple-element.115) | non-fusion elementwise | flops 2097152 | bytes 12582912 | tf_op jit(solution)/shard_map/convert_element_type | solution.py:1648
  579.8 1.5 slice_convert_fusion
  581.3 3.4 convert_bitcast_fusion
  584.7 3.6 convert_bitcast_fusion.1
  588.3 1.3 copy.125
  589.6 1.0 copy-done.12
  590.7 1.3 copy.126
  592.0 1.3 copy-done.10
  593.3 1.7 copy.127
  (143 shorter events, 22.4 us)
Async XLA Ops:
  7.2 23.5 %copy-start = (s32[512,8]{0,1:T(8,128)S(1)}, s32[512,8]{0,1:T(8,128)}, u32[]{:S(2)}) copy-start(s32[512,8]{0,1:T(8,128)} %param.18) | copy-start | bytes 49156
  7.2 7.6 %copy-start.28 = (f32[2048]{0:T(1024)S(1)}, f32[2048]{0:T(1024)}, u32[]{:S(2)}) copy-start(f32[2048]{0:T(1024)} %param.19) | copy-start | bytes 24580
  7.2 149.4 %all-gather.2.cloned.1.call-start = ((), (), s32[]{:S(2)}) async-start(), calls=%async_computation.3 | async-start | bytes 4718592 | tf_op jit(solution)/shard_map/all_gather | solution.py:1411
  7.3 48.3 %collective-permute-start = (bf16[2,192,2048]{2,1,0:T(8,128)(2,1)}, bf16[2,192,2048]{2,1,0:T(8,128)(2,1)}, u32[]{:S(2)}, u32[]{:S(2)}) collective-permute-start(bf16[2,192,2048]{2,1,0:T(8,128)(2,1)} %bitcast.117), channel_id=1, source_target_pairs={{0,2},{1,3},{2,0},{3,1},{4,6},{5,7},{6,4},{7,5},{8,10},{9,11},{10,... | collective-permute-start | bytes 4718600 | tf_op jit(solution)/shard_map/ppermute | solution.py:1367
  8.8 136.5 %collective-permute-start.3 = (bf16[2,192,2048]{2,1,0:T(8,128)(2,1)}, bf16[2,192,2048]{2,1,0:T(8,128)(2,1)}, u32[]{:S(2)}, u32[]{:S(2)}) collective-permute-start(bf16[2,192,2048]{2,1,0:T(8,128)(2,1)} %bitcast.118), channel_id=1, source_target_pairs={{0,1},{1,0},{2,3},{3,2},{4,5},{5,4},{6,7},{7,6},{8,9},{9,8},{10,11... | collective-permute-start | bytes 4718600 | tf_op jit(solution)/shard_map/ppermute | solution.py:1363
  10.8 416.5 %reduce-scatter.4.cloned.1.call-start = ((), (), s32[]{:S(2)}) async-start(), calls=%async_computation.4 | async-start | bytes 4718592 | tf_op jit(solution)/shard_map/reduce_scatter | solution.py:1603
  10.8 4.0 copy-start.7
  10.9 6.7 %copy-start.36 = (f32[64]{0:T(128)}, f32[64]{0:T(128)S(1)}, u32[]{:S(2)}) copy-start(f32[64]{0:T(128)S(1)} %multiply_power_fusion) | copy-start | bytes 772
  14.9 1.0 copy-start.11
  15.9 16.7 %copy-start.2 = (bf16[512,2048]{1,0:T(8,128)(2,1)}, bf16[512,2048]{1,0:T(8,128)(2,1)S(1)}, u32[]{:S(2)}) copy-start(bf16[512,2048]{1,0:T(8,128)(2,1)S(1)} %fusion.4.refs_18_) | copy-start | bytes 6291460
  15.9 3.6 copy-start.34
  26.7 1.3 copy-start.3
  30.7 3.7 copy-start.26
  31.4 3.0 copy-start.4
  31.4 3.0 copy-start.35
  32.6 3.4 copy-start.20
  34.4 5.5 copy-start.24
  43.4 2.5 copy-start.27
  46.9 3.6 copy-start.9
  50.5 27.4 %copy-start.23 = (f32[512,64]{1,0:T(8,128)S(1)}, f32[512,64]{1,0:T(8,128)}, u32[]{:S(2)}) copy-start(f32[512,64]{1,0:T(8,128)} %get-tuple-element.137) | copy-start | bytes 393220
  55.6 20.2 %copy-start.14 = (bf16[2,2048,192]{1,2,0:T(8,128)(2,1)S(1)}, bf16[2,2048,192]{1,2,0:T(8,128)(2,1)}, u32[]{:S(2)}) copy-start(bf16[2,2048,192]{1,2,0:T(8,128)(2,1)} %param.29) | copy-start | bytes 4718596
  55.6 21.9 %copy-start.15 = (bf16[2,192,2048]{2,1,0:T(8,128)(2,1)S(1)}, bf16[2,192,2048]{2,1,0:T(8,128)(2,1)}, u32[]{:S(2)}) copy-start(bf16[2,192,2048]{2,1,0:T(8,128)(2,1)} %refs_11_.1) | copy-start | bytes 4718596
  55.6 23.3 %copy-start.32 = (pred[128,16]{0,1:T(8,128)(4,1)S(1)}, pred[128,16]{0,1:T(8,128)(4,1)}, u32[]{:S(2)}) copy-start(pred[128,16]{0,1:T(8,128)(4,1)} %copy-done.31) | copy-start | bytes 6148
  75.8 58.9 %collective-permute-start.1 = (bf16[2,192,2048]{2,1,0:T(8,128)(2,1)S(1)}, bf16[2,192,2048]{2,1,0:T(8,128)(2,1)S(1)}, u32[]{:S(2)}, u32[]{:S(2)}) collective-permute-start(bf16[2,192,2048]{2,1,0:T(8,128)(2,1)S(1)} %bitcast.121), channel_id=1, source_target_pairs={{0,2},{1,3},{2,0},{3,1},{4,6},{5,7},{6,4},{7,5},{8,10},{9,11},{10,... | collective-permute-start | bytes 4718600 | tf_op jit(solution)/shard_map/ppermute | solution.py:1367
  77.4 67.9 %collective-permute-start.2 = (bf16[2,192,2048]{2,1,0:T(8,128)(2,1)S(1)}, bf16[2,192,2048]{2,1,0:T(8,128)(2,1)S(1)}, u32[]{:S(2)}, u32[]{:S(2)}) collective-permute-start(bf16[2,192,2048]{2,1,0:T(8,128)(2,1)S(1)} %copy-done.15), channel_id=1, source_target_pairs={{0,2},{1,3},{2,0},{3,1},{4,6},{5,7},{6,4},{7,5},{8,10},{9,11},{10,... | collective-permute-start | bytes 4718600 | tf_op jit(solution)/shard_map/ppermute | solution.py:1367
  77.9 5.5 copy-start.30
  79.5 67.4 %copy-start.33 = (pred[128,16]{1,0:T(32,128)(4,1)S(1)}, pred[128,16]{1,0:T(32,128)(4,1)}, u32[]{:S(2)}) copy-start(pred[128,16]{1,0:T(32,128)(4,1)} %copy.97) | copy-start | bytes 6148
  79.5 74.7 %collective-permute-start.5 = (bf16[2,192,2048]{2,1,0:T(8,128)(2,1)S(1)}, bf16[2,192,2048]{2,1,0:T(8,128)(2,1)}, u32[]{:S(2)}, u32[]{:S(2)}) collective-permute-start(bf16[2,192,2048]{2,1,0:T(8,128)(2,1)S(1)} %bitcast.122), channel_id=1, source_target_pairs={{0,1},{1,0},{2,3},{3,2},{4,5},{5,4},{6,7},{7,6},{8,9},{9,8},{10,11... | collective-permute-start | bytes 4718600 | tf_op jit(solution)/shard_map/ppermute | solution.py:1363
  79.6 74.6 %collective-permute-start.7 = (bf16[2,192,2048]{2,1,0:T(8,128)(2,1)S(1)}, bf16[2,192,2048]{2,1,0:T(8,128)(2,1)}, u32[]{:S(2)}, u32[]{:S(2)}) collective-permute-start(bf16[2,192,2048]{2,1,0:T(8,128)(2,1)S(1)} %copy-done.15), channel_id=1, source_target_pairs={{0,1},{1,0},{2,3},{3,2},{4,5},{5,4},{6,7},{7,6},{8,9},{9,8},{10,11... | collective-permute-start | bytes 4718600 | tf_op jit(solution)/shard_map/ppermute | solution.py:1363
  134.7 17.4 %copy-start.16 = (bf16[2,192,2048]{2,1,0:T(8,128)(2,1)}, bf16[2,192,2048]{2,1,0:T(8,128)(2,1)S(1)}, u32[]{:S(2)}) copy-start(bf16[2,192,2048]{2,1,0:T(8,128)(2,1)S(1)} %collective-permute-done.1.refs_9_) | copy-start | bytes 4718596
  134.7 19.6 %collective-permute-start.4 = (bf16[2,192,2048]{2,1,0:T(8,128)(2,1)}, bf16[2,192,2048]{2,1,0:T(8,128)(2,1)S(1)}, u32[]{:S(2)}, u32[]{:S(2)}) collective-permute-start(bf16[2,192,2048]{2,1,0:T(8,128)(2,1)} %collective-permute-done.refs_5_), channel_id=1, source_target_pairs={{0,1},{1,0},{2,3},{3,2},{4,5},{5,4},{6,7},{7,6},{8,9},{9,8},{10,11... | collective-permute-start | bytes 4718600 | tf_op jit(solution)/shard_map/ppermute | solution.py:1363
  145.3 6.8 %copy-start.17 = (bf16[2,192,2048]{2,1,0:T(8,128)(2,1)}, bf16[2,192,2048]{2,1,0:T(8,128)(2,1)S(1)}, u32[]{:S(2)}) copy-start(bf16[2,192,2048]{2,1,0:T(8,128)(2,1)S(1)} %collective-permute-done.2.refs_13_) | copy-start | bytes 4718596
  145.3 9.0 %collective-permute-start.6 = (bf16[2,192,2048]{2,1,0:T(8,128)(2,1)S(1)}, bf16[2,192,2048]{2,1,0:T(8,128)(2,1)S(1)}, u32[]{:S(2)}, u32[]{:S(2)}) collective-permute-start(bf16[2,192,2048]{2,1,0:T(8,128)(2,1)S(1)} %collective-permute-done.1.refs_9_), channel_id=1, source_target_pairs={{0,1},{1,0},{2,3},{3,2},{4,5},{5,4},{6,7},{7,6},{8,9},{9,8},{10,11... | collective-permute-start | bytes 4718600 | tf_op jit(solution)/shard_map/ppermute | solution.py:1363
  145.3 11.3 %collective-permute-start.8 = (bf16[2,192,2048]{2,1,0:T(8,128)(2,1)S(1)}, bf16[2,192,2048]{2,1,0:T(8,128)(2,1)}, u32[]{:S(2)}, u32[]{:S(2)}) collective-permute-start(bf16[2,192,2048]{2,1,0:T(8,128)(2,1)S(1)} %collective-permute-done.2.refs_13_), channel_id=1, source_target_pairs={{0,1},{1,0},{2,3},{3,2},{4,5},{5,4},{6,7},{7,6},{8,9},{9,8},{10,11... | collective-permute-start | bytes 4718600 | tf_op jit(solution)/shard_map/ppermute | solution.py:1363
  154.3 1.1 copy-start.18
  155.4 1.1 copy-start.19
  269.9 311.4 %reduce-scatter.8.cloned.1.call-start = ((), (), s32[]{:S(2)}) async-start(), calls=%async_computation.6 | async-start | bytes 7864320 | tf_op jit(solution)/shard_map/reduce_scatter | solution.py:1605
  270.6 314.1 %reduce-scatter.6.cloned.1.call-start = ((), (), s32[]{:S(2)}) async-start(), calls=%async_computation.5 | async-start | bytes 7864320 | tf_op jit(solution)/shard_map/reduce_scatter | solution.py:1605
  271.2 2.8 copy-start.25
  274.9 142.7 %copy-start.8 = (bf16[128,2048]{1,0:T(8,128)(2,1)S(1)}, bf16[128,2048]{1,0:T(8,128)(2,1)}, u32[]{:S(2)}) copy-start(bf16[128,2048]{1,0:T(8,128)(2,1)} %multiply_convert_fusion.refs_0_) | copy-start | bytes 1572868
  274.9 142.7 %copy-start.29 = (bf16[128,128]{1,0:T(8,128)(2,1)S(1)}, bf16[128,128]{1,0:T(8,128)(2,1)}, u32[]{:S(2)}) copy-start(bf16[128,128]{1,0:T(8,128)(2,1)} %get-tuple-element.105) | copy-start | bytes 98308
  416.6 4.2 copy-start.21
  420.8 6.5 %copy-start.6 = (f32[128,2048]{1,0:T(8,128)S(1)}, f32[128,2048]{1,0:T(8,128)}, u32[]{:S(2)}) copy-start(f32[128,2048]{1,0:T(8,128)} %copy-done.5) | copy-start | bytes 3145732
  571.3 8.5 %copy-start.22 = (bf16[2048,256]{1,0:T(8,128)(2,1)S(1)}, bf16[2048,256]{1,0:T(8,128)(2,1)}, u32[]{:S(2)}) copy-start(bf16[2048,256]{1,0:T(8,128)(2,1)} %get-tuple-element.116) | copy-start | bytes 3145732
  584.7 3.6 copy-start.13
  588.3 2.3 copy-start.12
  590.7 2.6 copy-start.10
  590.7 4.3 copy-start.1
  (2 other events, 1.7 us)
Sparse Core Ops, SparseCore 0:
  10.9 73.1 all-gather.1
  270.0 127.4 reduce-scatter.3
  400.2 72.2 reduce-scatter.7
  474.9 91.4 reduce-scatter.5

commit v2 on v1

--- a/solution.py
+++ b/solution.py
@@ -768,11 +768,10 @@
     return 4 * columns // 5 // 256 * 256
 
 
-def expert_rows(normed, cot, gates, weights_rel, own, number):
-    grid, side = grid_of("expert"), grid_of("shard")
+def expert_rows(normed, cot, gates, weights_rel, shards, number):
+    grid = grid_of("expert")
     _, lines, width, _ = grid
     size = lines * width
-    shards = side[1] * side[2]
     experts, hidden, columns = weights_rel[0].shape
     full = shards * hidden
     both = 2 * full
@@ -792,17 +791,13 @@
         take = Taker(refs)
         normed_hbm, cot_hbm, gates_ref = take.take(3)
         gate_hbm, up_hbm, down_hbm = take.take(shards), take.take(shards), take.take(shards)
-        residual_hbm, own_gates, router, norm_gain = take.take(4)
-        d_residual, d_logits, norm_gain_grad, d_attn = take.take(4)
-        out_hbm = take.one()
+        sum_ref, out_hbm = take.take(2)
         grad_hbm = take.take(3)
         normed_v, cot_v, weights, down = take.take(4)
         grads_low, act_low, parts = take.take(3)
         buffers = take.take(3)
         out_stage, grad_stage, d_gates_ref = take.take(3)
-        sum_ref, residual, d_low = take.take(3)
         load_sems, weight_sems, out_sems, grad_sems = take.take(4)
-        rows_job = Gather(side, d_low, d_attn, 2, take.take(4))
         job = Scatter(grid, parts, buffers, 1, take.take(6))
         me, z, _ = position(grid)
 
@@ -822,7 +817,6 @@
             pltpu.make_async_copy(normed_hbm, normed_v, load_sems.at[0]),
             pltpu.make_async_copy(cot_hbm, cot_v, load_sems.at[1]),
         ]
-        residual_load = pltpu.make_async_copy(residual_hbm, residual, load_sems.at[2])
         weight_loads = [[] for _ in range(experts)]
         for j in range(experts):
             for r in range(shards):
@@ -841,8 +835,7 @@
         for j in range(1, experts):
             for c in weight_loads[j]:
                 c.start()
-        residual_load.start()
-        greet([grid, side])
+        greet([grid])
         for c in loads:
             c.wait()
 
@@ -866,7 +859,7 @@
                     up_pre = dot_nt(x, weights[lines_of(j * both + full), :])
                     back = dot_nt(cot_v[rows, :], down[lines_of(j * full), :])
                     probs = gates_ref[rows, j : j + 1]
-                    sig = 0.5 + 0.5 * jnp.tanh(0.5 * gate_pre)
+                    sig = 1.0 / (1.0 + jnp.exp(-gate_pre))
                     silu = gate_pre * sig
                     act = silu * up_pre
                     act_low[rows, lines_of(j * full)] = (act * probs).astype(BF)
@@ -955,56 +948,7 @@
             return copies
 
         per = full // wide
-
-        def norm_backward():
-            ext = sum_ref[:, columns:]
-            d_gates = ext + pltpu.roll(ext, extra - size * experts, 1)
-            probs = own_gates[...]
-            inner = jnp.sum(probs * d_gates, axis=-1, keepdims=True)
-            low = (probs * (d_gates - inner)).astype(BF)
-            d_logits[...] = low
-            for q in range(columns // half):
-                cols = pl.ds(q * half, half)
-                sum_ref[:, cols] = sum_ref[:, cols] + dot_nt(low, router[cols, :])
-            norm_gain_grad[...] = jnp.zeros_like(norm_gain_grad)
-            residual_load.wait()
-
-            @pl.loop(0, count // 16)
-            def _(i):
-                rows = pl.ds(pl.multiple_of(i * 16, 16), 16)
-                grad = sum_ref[rows, :columns]
-                value = residual[rows, :]
-                inverse = lax.rsqrt(jnp.mean(value * value, axis=-1, keepdims=True) + EPS)
-                norm_gain_grad[0:1, :] = norm_gain_grad[0:1, :] + jnp.sum(
-                    grad * value * inverse, axis=0, keepdims=True
-                )
-                back = rms_backward(value, inverse, norm_gain[...], grad)
-                back = back + cot_v[pl.ds(pl.multiple_of(me * count + i * 16, 16), 16), :].astype(F32)
-                d_residual[rows, :] = back
-                d_low[rows, :] = back.astype(BF)
-
-            def start(z):
-                for p in range(2):
-                    rows_job.start(z, p)
-
-            at_each_line(side, start)
-
-        def rows_forward(z):
-            for p in range(2):
-                for origin in range(side[1]):
-                    if origin != z:
-                        rows_job.forward(z, origin, p)
-
-        def rows_end(z):
-            own_rows = pltpu.make_async_copy(d_low, rows_job.own_slot(z), load_sems.at[3])
-            own_rows.start()
-            rows_job.finish(z)
-            own_rows.wait()
-
         for kind in range(3):
-            if kind == 2:
-                plan.run(grid, order, begin, 1e9)
-                norm_backward()
 
             @pl.loop(0, experts * per)
             def _(i):
@@ -1027,18 +971,17 @@
                     grad_stage[slot, :, cols] = value.astype(BF)
                 for c in grad_copies(kind, j, r, slot):
                     c.start()
-                if kind < 2:
-                    plan.run_step(grid, order, i, begin, grad_us, experts * per)
+                plan.run_step(grid, order, i, begin, grad_us, experts * per)
 
             for i in range(max(0, experts * per - 2), experts * per):
                 for c in grad_copies(kind, i // per, i % per, i % 2):
                     c.wait()
             begin = begin + experts * per * grad_us
 
-        at_each_line(side, rows_forward)
+        plan.run(grid, order, begin, 1e9)
+
         for t in range(max(0, out_tiles - 2), out_tiles):
             out_copy(t, t % 2).wait()
-        at_each_line(side, rows_end)
         at_each_line(grid, job.finish)
 
     dma = pltpu.SemaphoreType.DMA
@@ -1046,17 +989,14 @@
     return pl.pallas_call(
         kernel,
         out_shape=[
-            jax.ShapeDtypeStruct((count, columns), F32),
-            jax.ShapeDtypeStruct((count, extra), BF),
-            jax.ShapeDtypeStruct((8, columns), F32),
-            jax.ShapeDtypeStruct((shards * count, columns), BF),
+            jax.ShapeDtypeStruct((count, columns + extra), F32),
             jax.ShapeDtypeStruct((total_rows, columns), BF),
             weight_shape,
             weight_shape,
             weight_shape,
         ],
-        in_specs=[hbm()] * 2 + [vmem()] + [hbm()] * (3 * shards) + [hbm()] + [vmem()] * 3,
-        out_specs=[vmem()] * 3 + [hbm()] * 5,
+        in_specs=[hbm()] * 2 + [vmem()] + [hbm()] * (3 * shards),
+        out_specs=[vmem()] + [hbm()] * 4,
         scratch_shapes=[
             pltpu.VMEM((total_rows, columns), BF),
             pltpu.VMEM((total_rows, columns), BF),
@@ -1071,19 +1011,15 @@
             pltpu.VMEM((2, total_rows, tile), BF),
             pltpu.VMEM((2, wide, columns), BF),
             pltpu.VMEM((total_rows, experts), F32),
-            pltpu.VMEM((count, columns + extra), F32),
-            pltpu.VMEM((count, columns), F32),
-            pltpu.VMEM((count, columns), BF),
-            dma((4,)),
+            dma((2,)),
             dma((experts, shards, 3)),
             dma((2,)),
             dma((2, 2)),
         ]
-        + Gather.sems(side, 2)
         + Scatter.sems(grid, 1),
-        compiler_params=params(number, 63),
+        compiler_params=params(number, 62),
         name="expert_rows",
-    )(normed, cot, gates, *weights_rel, *own)
+    )(normed, cot, gates, *weights_rel)
 
 
 def rms_forward(vector, gain):
@@ -1097,14 +1033,143 @@
     return inverse * scaled - vector * (inverse * inverse * inverse * inner)
 
 
-def attention_backward(arrays, heads, number):
+def attention_forward(arrays, heads, number):
+    side = grid_of("shard")
+    shards = side[1] * side[2]
+    names = list(arrays)
+    tokens, columns = arrays["rows"].shape
+    inner = arrays["query_weight"].shape[1]
+    head = inner // heads
+    own_rows = tokens // shards
+    tile = 256
+    scale = head ** (-0.5)
+    block = min(256, tokens)
+
+    def kernel(*refs):
+        take = Taker(refs)
+        hbm_refs = take.take(len(names))
+        normed, query_lin, key_lin, query, key, value, mixed, log_total = take.take(8)
+        residual, normed_two = take.take(2)
+        v = dict(zip(names, take.take(len(names))))
+        bias, parts, summed = take.take(3)
+        buffers = take.take(3)
+        load_sems = take.one()
+        job = Scatter(side, parts, buffers, 2, take.take(6))
+        shard = lax.axis_index("shard")
+        loads = [
+            pltpu.make_async_copy(ref, v[name], load_sems.at[i])
+            for i, (name, ref) in enumerate(zip(names, hbm_refs))
+        ]
+        for c in loads:
+            c.start()
+        greet([side])
+        for c in loads[:-1]:
+            c.wait()
+
+        def norm(value, gain):
+            return value * lax.rsqrt(jnp.mean(value * value, axis=-1, keepdims=True) + EPS) * gain
+
+        @pl.loop(0, tokens // 32)
+        def _(i):
+            rows = pl.ds(pl.multiple_of(i * 32, 32), 32)
+            normed[rows, :] = norm(v["rows"][rows, :].astype(F32), v["norm_gain"][...]).astype(BF)
+
+        @pl.loop(0, inner // tile)
+        def _(t):
+            cols = pl.ds(pl.multiple_of(t * tile, tile), tile)
+            query_lin[:, cols] = dot(normed[...], v["query_weight"][:, cols])
+
+        key_lin[...] = dot(normed[...], v["key_weight"][...])
+        value[...] = dot(normed[...], v["value_weight"][...]).astype(BF)
+
+        def turn(rows):
+            return rows * v["cosine"][...] + pltpu.roll(rows, head // 2, 1) * v["sine"][...]
+
+        key[...] = turn(norm(key_lin[...], v["key_gain"][...])).astype(BF)
+        rows_at = lax.broadcasted_iota(jnp.int32, (tokens, tokens), 0)
+        cols_at = lax.broadcasted_iota(jnp.int32, (tokens, tokens), 1)
+        allowed = jnp.logical_and(v["doc_col"][...] == v["doc_row"][...], rows_at >= cols_at)
+        bias[...] = jnp.where(allowed, 0.0, -1e30)
+
+        @pl.loop(0, heads)
+        def _(h):
+            lanes = pl.ds(pl.multiple_of(h * head, head), head)
+            query[:, lanes] = turn(norm(query_lin[:, lanes], v["query_gain"][...])).astype(BF)
+            for first in range(0, tokens, block):
+                rows = pl.ds(first, block)
+                keys = pl.ds(0, first + block)
+                scores = dot_nt(query[rows, lanes], key[keys, :]) * scale + bias[rows, keys]
+                top = jnp.max(scores, axis=-1, keepdims=True)
+                powers = jnp.exp(scores - top)
+                total = jnp.sum(powers, axis=-1, keepdims=True)
+                log_total[h, rows, :] = top + jnp.log(total)
+                probs = (powers * (1.0 / total)).astype(BF)
+                mixed[rows, lanes] = dot(probs, value[keys, :]).astype(BF)
+
+        loads[-1].wait()
+
+        @pl.loop(0, columns // tile)
+        def _(t):
+            cols = pl.ds(pl.multiple_of(t * tile, tile), tile)
+            parts[:, cols] = dot(mixed[...], v["out_weight"][:, cols]).astype(BF)
+
+        def put(at, total):
+            summed[at, :] = total
+
+        plan = Plan(side[1])
+        for p in range(2):
+            plan_scatter(plan, job, p, put)
+        plan.run(side, plan.order(), *ALWAYS)
+
+        @pl.loop(0, own_rows // 16)
+        def _(i):
+            rows = pl.ds(pl.multiple_of(i * 16, 16), 16)
+            from_rows = pl.ds(pl.multiple_of(shard * own_rows + i * 16, 16), 16)
+            total = v["rows"][from_rows, :].astype(F32) + summed[rows, :]
+            residual[rows, :] = total
+            normed_two[rows, :] = norm(total, v["norm_two_gain"][...]).astype(BF)
+
+        at_each_line(side, job.finish)
+
+    values = [arrays[name] for name in names]
+    shape = jax.ShapeDtypeStruct
+    return pl.pallas_call(
+        kernel,
+        out_shape=[
+            shape((tokens, columns), BF),
+            shape((tokens, inner), F32),
+            shape((tokens, head), F32),
+            shape((tokens, inner), BF),
+            shape((tokens, head), BF),
+            shape((tokens, head), BF),
+            shape((tokens, inner), BF),
+            shape((heads, tokens, 1), F32),
+            shape((own_rows, columns), F32),
+            shape((own_rows, columns), BF),
+        ],
+        in_specs=[hbm()] * len(names),
+        out_specs=[vmem()] * 10,
+        scratch_shapes=[pltpu.VMEM(a.shape, a.dtype) for a in values]
+        + [
+            pltpu.VMEM((tokens, tokens), F32),
+            pltpu.VMEM((tokens, columns), BF),
+            pltpu.VMEM((own_rows, columns), F32),
+        ]
+        + Scatter.buffers(side, own_rows, columns, BF)
+        + [pltpu.SemaphoreType.DMA((len(names),))]
+        + Scatter.sems(side, 2),
+        compiler_params=params(number),
+        name="attention_forward",
+    )(*values)
+
+
+def attention_backward(arrays, d_own, heads, number):
     grid, side = grid_of("expert"), grid_of("shard")
     _, lines, width, _ = grid
     size = lines * width
     shards = side[1] * side[2]
     names = list(arrays)
-    tokens, columns = arrays["d_attn"].shape
-    own_rows = tokens // shards
+    tokens, columns = shards * d_own.shape[0], d_own.shape[1]
     inner = arrays["mixed"].shape[1]
     head = inner // heads
     count = inner // size
@@ -1119,12 +1184,12 @@
 
     def kernel(*refs):
         take = Taker(refs)
-        hbm_refs = take.take(len(names))
+        hbm_refs, d_own_ref = take.take(len(names)), take.one()
         grad_refs = take.take(2)
         input_grad_ref, norm_gain_ref, gains_ref = take.take(3)
         sum_refs = take.take(2)
         v = dict(zip(names, take.take(len(names))))
-        d_mixed, bias, dk, dv, lines_ref, d_norm_ref = take.take(6)
+        d_attn, d_mixed, bias, dk, dv, lines_ref, d_norm_ref = take.take(7)
         parts = take.take(2)
         jobs = [
             Reduce(grid, parts[i], sum_refs[i], take.take(Reduce.refs(kinds[i][1])), *kinds[i])
@@ -1132,7 +1197,8 @@
         ]
         side_parts = take.one()
         side_buffers = take.take(3)
-        load_sems = take.one()
+        load_sems, own_sems = take.take(2)
+        gather = Gather(side, d_own_ref, d_attn, 2, take.take(4))
         side_job = Scatter(side, side_parts, side_buffers, 2, take.take(6))
         me, z, _ = position(grid)
         plan = Plan(lines)
@@ -1140,6 +1206,10 @@
             job.plan(plan, [(i + 1) * PAIR_US for i in range(lines)], False)
         order = plan.order()
 
+        def own(z):
+            return pltpu.make_async_copy(d_own_ref, gather.own_slot(z), own_sems.at[0])
+
+        at_each_line(side, lambda z: own(z).start())
         loads = [
             pltpu.make_async_copy(ref, v[name], load_sems.at[i])
             for i, (name, ref) in enumerate(zip(names, hbm_refs))
@@ -1148,9 +1218,31 @@
             c.start()
         greet([grid, side])
 
-        for c in loads[:2]:
+        def gather_start(z):
+            for p in range(2):
+                gather.start(z, p)
+            for p in range(2):
+                for origin in range(side[1]):
+                    if origin != z:
+                        gather.forward(z, origin, p)
+
+        at_each_line(side, gather_start)
+        for c in loads:
             c.wait()
-        d_attn = v["d_attn"]
+
+        rows_at = lax.broadcasted_iota(jnp.int32, (tokens, tokens), 0)
+        cols_at = lax.broadcasted_iota(jnp.int32, (tokens, tokens), 1)
+        allowed = jnp.logical_and(v["doc_col"][...] == v["doc_row"][...], rows_at >= cols_at)
+        bias[...] = jnp.where(allowed, 0.0, -1e30)
+        dk[...] = jnp.zeros_like(dk)
+        dv[...] = jnp.zeros_like(dv)
+        gains_ref[...] = jnp.zeros_like(gains_ref)
+
+        def gather_end(z):
+            gather.finish(z)
+            own(z).wait()
+
+        at_each_line(side, gather_end)
 
         @pl.loop(0, lines)
         def _(i):
@@ -1169,16 +1261,6 @@
                 first += split[n]
                 for p in range(kinds[n][0]):
                     jobs[n].start_one(k, p)
-
-        for c in loads[2:]:
-            c.wait()
-        rows_at = lax.broadcasted_iota(jnp.int32, (tokens, tokens), 0)
-        cols_at = lax.broadcasted_iota(jnp.int32, (tokens, tokens), 1)
-        allowed = jnp.logical_and(v["doc_col"][...] == v["doc_row"][...], rows_at >= cols_at)
-        bias[...] = jnp.where(allowed, 0.0, -1e30)
-        dk[...] = jnp.zeros_like(dk)
-        dv[...] = jnp.zeros_like(dv)
-        gains_ref[...] = jnp.zeros_like(gains_ref)
 
         @pl.loop(0, inner // tile)
         def _(t):
@@ -1265,7 +1347,7 @@
 
         norm_gain_ref[...] = jnp.zeros_like(norm_gain_ref)
 
-        @pl.loop(0, own_rows // 16)
+        @pl.loop(0, d_own.shape[0] // 16)
         def _(i):
             rows = pl.ds(pl.multiple_of(i * 16, 16), 16)
             value = v["input_own"][rows, :].astype(F32)
@@ -1293,34 +1375,36 @@
         out_shape=[
             jax.ShapeDtypeStruct((columns, share), BF),
             jax.ShapeDtypeStruct((columns, inner + 2 * head - share), BF),
-            jax.ShapeDtypeStruct((own_rows, columns), BF),
+            jax.ShapeDtypeStruct(d_own.shape, BF),
             jax.ShapeDtypeStruct((8, columns), F32),
             jax.ShapeDtypeStruct((8, head), F32),
             jax.ShapeDtypeStruct((inner, split[0]), BF),
             jax.ShapeDtypeStruct((inner, split[1]), BF),
         ],
-        in_specs=[hbm()] * len(names),
+        in_specs=[hbm()] * (len(names) + 1),
         out_specs=[vmem()] * 5 + [hbm()] * 2,
         scratch_shapes=[pltpu.VMEM(a.shape, a.dtype) for a in values]
         + [
+            pltpu.VMEM((tokens, columns), BF),
             pltpu.VMEM((tokens, inner), BF),
             pltpu.VMEM((tokens, tokens), F32),
             pltpu.VMEM((tokens, head), F32),
             pltpu.VMEM((tokens, head), F32),
             pltpu.VMEM((tokens, inner + 2 * head), BF),
-            pltpu.VMEM((own_rows, columns), F32),
+            pltpu.VMEM(d_own.shape, F32),
             pltpu.VMEM((inner, split[0]), BF),
             pltpu.VMEM((inner, split[1]), BF),
         ]
         + Reduce.scratch(grid, inner, split[0], BF, *kinds[0])
         + Reduce.scratch(grid, inner, split[1], BF, *kinds[1])
         + [pltpu.VMEM((tokens, columns), BF)]
-        + Scatter.buffers(side, own_rows, columns, BF)
-        + [dma((len(names),))]
+        + Scatter.buffers(side, d_own.shape[0], columns, BF)
+        + [dma((len(names),)), dma((1,))]
+        + Gather.sems(side, 2)
         + Scatter.sems(side, 2),
         compiler_params=params(number),
         name="attention_backward",
-    )(*values)
+    )(*values, d_own)
     first, second, input_grad, norm_gain, gains, *out_sums = out
     out_sum = jnp.concatenate(out_sums, axis=1)
     return (first, second), input_grad, norm_gain[0], gains[0], gains[1], out_sum
@@ -1331,25 +1415,6 @@
     frequency = THETA ** (-2.0 * jnp.arange(half_size, dtype=F32) / head_size)
     angles = positions.astype(F32)[:, None] * frequency[None, :]
     return (jnp.cos(angles), jnp.sin(angles))
-
-
-def apply_rotary(vector, cosine_table, sine_values):
-    half_size = vector.shape[-1] // 2
-    first_half = vector[..., :half_size]
-    second_half = vector[..., half_size:]
-    cos_rows = cosine_table[:, None, :]
-    sin_rows = sine_values[:, None, :]
-    return jnp.concatenate(
-        [
-            first_half * cos_rows - second_half * sin_rows,
-            second_half * cos_rows + first_half * sin_rows,
-        ],
-        axis=-1,
-    )
-
-
-def root_mean_norm_forward(vector, gain):
-    return rms_forward(vector, gain)[0]
 
 
 def doc_positions(doc_ids):
@@ -1388,8 +1453,6 @@
     tokens_here, model_width = layer_input.shape
     head_size = query_norm_gain.shape[0]
     heads_here = query_weight.shape[1] // head_size
-    kv_here = key_matrix.shape[1] // head_size
-    group_size = heads_here // kv_here
     experts_all = router_weight.shape[1]
     local_experts, _, hidden_here = gate_weight.shape
     expert_peers = lax.axis_size("expert")
@@ -1397,7 +1460,6 @@
     rows_here = tokens_here // shard_count
     shard_index = lax.axis_index("shard")
     expert_index = lax.axis_index("expert")
-    score_scale = head_size ** (-0.5)
     hidden_all = shard_count * local_experts * hidden_here
 
     def own(rows):
@@ -1422,60 +1484,39 @@
         gate_all = gather_weight(gate_weight)
         up_all = gather_weight(up_weight)
 
-    inputs = layer_input.astype(F32)
-    norm_one, _ = rms_forward(inputs, norm1_gain)
-    first_normed_input = norm_one.astype(BF)
-    query_linear = dot(first_normed_input, query_weight).reshape(
-        tokens_here, heads_here, head_size
-    )
-    key_linear = dot(first_normed_input, key_matrix).reshape(tokens_here, kv_here, head_size)
-    value_token_rows = (
-        dot(first_normed_input, value_matrix).astype(BF).reshape(tokens_here, kv_here, head_size)
-    )
     positions = doc_positions(doc_ids)
     cosine_table, sine_values = rope_tables(positions, head_size)
-
-    def head_prep(linear, gain):
-        return apply_rotary(root_mean_norm_forward(linear, gain), cosine_table, sine_values)
-
-    query_rotated = head_prep(query_linear, query_norm_gain)
-    key_rotated = head_prep(key_linear, key_norm_gain)
-    query_low = query_rotated.astype(BF).reshape(tokens_here, kv_here, group_size, head_size)
-    key_low = key_rotated.astype(BF)
-    row_index = jnp.arange(tokens_here)
-    allowed = (doc_ids[:, None] == doc_ids[None, :]) & (row_index[:, None] >= row_index[None, :])
-
-    def masked_scores():
-        raw_scores = (
-            jnp.einsum("tkgd,skd->kgts", query_low, key_low, preferred_element_type=F32)
-            * score_scale
+    inner = heads_here * head_size
+    shared = dict(
+        cosine=jnp.concatenate([cosine_table, cosine_table], axis=1),
+        sine=jnp.concatenate([-sine_values, sine_values], axis=1),
+        query_gain=query_norm_gain[None, :],
+        key_gain=key_norm_gain[None, :],
+        doc_col=doc_ids[:, None],
+        doc_row=doc_ids[None, :],
+        query_weight=query_weight,
+        key_weight=key_matrix,
+        value_weight=value_matrix,
+        norm_gain=norm1_gain[None, :],
+    )
+    forward = dict(
+        rows=layer_input, norm_two_gain=norm2_gain[None, :], **shared, out_weight=out_weight
+    )
+    normed_one, query_lin, key_lin, query, key, value, mixed, log_total, residual, normed_two = (
+        attention_forward(forward, heads_here, 1)
+    )
+    if fused:
+        gate_far, residual, normed_two = lax.optimization_barrier(
+            (gate_far, residual, normed_two)
         )
-        return jnp.where(allowed, raw_scores, -1e30)
-
-    scores = masked_scores()
-    row_max = jnp.max(scores, axis=-1, keepdims=True)
-    exp_scores = jnp.exp(scores - row_max)
-    row_total = jnp.sum(exp_scores, axis=-1, keepdims=True)
-    log_total = row_max + jnp.log(row_total)
-    probs_low = (exp_scores / row_total).astype(BF)
-    mixture = jnp.einsum(
-        "kgts,skd->tkgd", probs_low, value_token_rows, preferred_element_type=F32
-    )
-    mixed = mixture.astype(BF).reshape(tokens_here, heads_here * head_size)
-    attn_part = dot(mixed, out_weight)
-    attn_part = attn_part.astype(BF)
+
     if fused:
-        gate_far, attn_part = lax.optimization_barrier((gate_far, attn_part))
-    attn_own = scatter_rows(attn_part, "shard", 1, 2)
-
-    if fused:
-        up_late, down_late, attn_own = lax.optimization_barrier((up_weight, down_weight, attn_own))
+        up_late, down_late, normed_two = lax.optimization_barrier(
+            (up_weight, down_weight, normed_two)
+        )
         up_far, down_far = from_far(up_late, shard_count), from_far(down_late, shard_count)
         up_near, down_near = from_near(up_late, shard_count), from_near(down_late, shard_count)
-    inputs_own = own(layer_input).astype(F32)
-    residual = inputs_own + attn_own
-    norm_two, inverse_two = rms_forward(residual, norm2_gain)
-    normed_two = norm_two.astype(BF)
+    _, inverse_two = rms_forward(residual, norm2_gain)
     normed_all, chosen_all = gather_rows(
         [normed_two, chosen_own.T.astype(F32)], [], 2, (2, 1)
     )
@@ -1501,49 +1542,15 @@
     gates_here = lax.dynamic_slice_in_dim(
         gates_all, expert_index * local_experts, local_experts, axis=1
     )
-    gates_own = gate_table(normed_two, chosen_own)
-    inner = heads_here * head_size
-    backward = dict(
-        mixed=mixed,
-        out_weight=out_weight,
-        query=query_low.reshape(tokens_here, inner),
-        key=key_low.reshape(tokens_here, head_size),
-        value=value_token_rows.reshape(tokens_here, head_size),
-        query_lin=query_linear.reshape(tokens_here, inner),
-        key_lin=key_linear.reshape(tokens_here, head_size),
-        log_total=log_total.reshape(heads_here, tokens_here, 1),
-        cosine=jnp.concatenate([cosine_table, cosine_table], axis=1),
-        sine=jnp.concatenate([-sine_values, sine_values], axis=1),
-        query_gain=query_norm_gain[None, :],
-        key_gain=key_norm_gain[None, :],
-        doc_col=doc_ids[:, None],
-        doc_row=doc_ids[None, :],
-        query_weight=query_weight,
-        key_weight=key_matrix,
-        value_weight=value_matrix,
-        normed=first_normed_input,
-        input_own=own(layer_input),
-        norm_gain=norm1_gain[None, :],
-    )
-    names = list(backward)
-    gates_here, gates_own, *values = lax.optimization_barrier(
-        (gates_here, gates_own, *backward.values())
-    )
-    backward = dict(zip(names, values))
-
     if fused:
-        wide = ((0, 0), (0, EXTRA - experts_all))
-        own_arrays = (
-            residual,
-            jnp.pad(gates_own, wide),
-            jnp.pad(router_weight, wide),
-            norm2_gain[None, :],
+        summed, out_part, gate_part, up_part, down_part = expert_rows(
+            normed_all, cot_all, gates_here, weights_rel, shard_count, 3
         )
-        d_residual, d_logits_low, norm2_grad, d_attn, out_part, *grad_parts = expert_rows(
-            normed_all, cot_all, gates_here, weights_rel, own_arrays, 3
+        d_rows_own = summed[:, :model_width]
+        d_gates_own = (
+            summed[:, model_width : model_width + experts_all]
+            + summed[:, model_width + experts_all : model_width + 2 * experts_all]
         )
-        d_logits_low, norm2_grad = d_logits_low[:, :experts_all], norm2_grad[0]
-        gate_part, up_part, down_part = grad_parts
     else:
         column_expert = (jnp.arange(hidden_all, dtype=jnp.int32) // hidden_here) % local_experts
         gate_columns = jnp.zeros((1, 1), F32)
@@ -1587,19 +1594,6 @@
             tiled=True,
         )
         d_gates_own = jnp.swapaxes(d_gates_own, 0, 1).reshape(rows_here, experts_all)
-
-        d_logits = gates_own * (
-            d_gates_own - jnp.sum(gates_own * d_gates_own, axis=-1, keepdims=True)
-        )
-        d_logits_low = d_logits.astype(BF)
-        d_normed_two = d_rows_own + dot_nt(d_logits_low, router_weight)
-        norm2_grad = jnp.sum(d_normed_two * residual * inverse_two, axis=0)
-        d_residual = cot_own.astype(F32) + rms_backward(
-            residual, inverse_two, norm2_gain, d_normed_two
-        )
-        d_attn = gather_rows([], [d_residual.astype(BF)], 7, (2,))[0]
-    router_grad = dot_tn(normed_two, d_logits_low)
-    backward = dict(mixed=backward.pop("mixed"), d_attn=d_attn, **backward, d_residual=d_residual)
     out_own = lax.psum_scatter(out_part, "expert", scatter_dimension=0, tiled=True)
     def scatter_grad(grad):
         return lax.psum_scatter(grad, "shard", scatter_dimension=0, tiled=False)
@@ -1607,8 +1601,33 @@
     gate_grad = jnp.swapaxes(scatter_grad(gate_part).astype(F32), 1, 2)
     up_grad = jnp.swapaxes(scatter_grad(up_part).astype(F32), 1, 2)
 
+    gates_own = gate_table(normed_two, chosen_own)
+    d_logits = gates_own * (
+        d_gates_own - jnp.sum(gates_own * d_gates_own, axis=-1, keepdims=True)
+    )
+    d_logits_low = d_logits.astype(BF)
+    router_grad = dot_tn(normed_two, d_logits_low)
+    d_normed_two = d_rows_own + dot_nt(d_logits_low, router_weight)
+    norm2_grad = jnp.sum(d_normed_two * residual * inverse_two, axis=0)
+    d_residual = cot_own.astype(F32) + rms_backward(
+        residual, inverse_two, norm2_gain, d_normed_two
+    )
+    backward = dict(
+        mixed=mixed,
+        query=query,
+        key=key,
+        value=value,
+        query_lin=query_lin,
+        key_lin=key_lin,
+        log_total=log_total,
+        out_weight=out_weight,
+        normed=normed_one,
+        input_own=own(layer_input),
+        d_residual=d_residual,
+        **shared,
+    )
     line_grads, input_grad_own, norm1_grad, d_query_gain, d_key_gain, out_sum = (
-        attention_backward(backward, heads_here, 4)
+        attention_backward(backward, d_residual.astype(BF), heads_here, 4)
     )
     share = share_of(inner + 2 * head_size)
     out_own, _ = lax.optimization_barrier((out_own, norm1_grad))

time: 606 us -> 555 us (0.916)
  matrix products: 23 us -> 4.72 us
  other arithmetic: 48.7 us -> 33 us
  local copies, waits for them, and re-layouts: 33.1 us -> 22.3 us
    pallas_call x1, Pallas kernels: 140 us -> 126 us  [sum_and_gather(): pl.pallas_call(kernel, out_shape=[jax.ShapeDtypeStruct(a.shape, a.dtype)...]
    dot_general x6 -> x2, matrix products: 17.1 us -> 3.84 us  [dot(): return jnp.dot(a, b, preferred_element_type=F32)]
    pallas_call x2, Pallas kernels: 133 us -> 146 us  [the longest x1 97.6 us: expert_rows(): pl.pallas_call(kernel, out_shape=[jax.ShapeDtypeStruct((count, columns +...]
    unnamed x84 -> x36, local copies, waits for them, and re-layouts: 13.6 us -> 9.69 us
  transfers between devices with their start and end apart: 13 -> 13, of which waited for: 1 -> 1; matrix products, arithmetic and copies ran while one was open for 15% -> 8% of each run, Pallas kernels for 59% -> 66%
where the time goes in v2:
time: 555 us
  Pallas kernels  461 us (83%)
  other arithmetic  33 us (6%)
  local copies, waits for them, and re-layouts  22.3 us (4%)
  waiting for transfers between devices  14.2 us (3%)
  between operations  14.1 us (3%)
    pallas_call x1, Pallas kernels, attention_backward(): pl.pallas_call(kernel, out_shape=[jax.ShapeDtypeStruct((columns, share),...  138 us
    pallas_call x1, Pallas kernels, sum_and_gather(): pl.pallas_call(kernel, out_shape=[jax.ShapeDtypeStruct(a.shape, a.dtype)...  126 us
    pallas_call x1, Pallas kernels, expert_rows(): pl.pallas_call(kernel, out_shape=[jax.ShapeDtypeStruct((count, columns +...  97.6 us
    pallas_call x1, Pallas kernels, gather_rows(): pl.pallas_call(kernel, out_shape=[jax.ShapeDtypeStruct((g[1] * g[2] * a.s...  52 us
    pallas_call x1, Pallas kernels, attention_forward(): pl.pallas_call(kernel, out_shape=[shape((tokens, columns), BF), shape((to...  48.1 us
    ppermute x3, waiting for transfers between devices, from_far(): lax.ppermute(rows, 'shard', [(s, (s + 2) % count) for s in range(count)])  13 us
  transfers between devices with their start and end apart: 13, of which 1 were waited for; matrix products, arithmetic and copies ran while one was open for 8% of the time, Pallas kernels for 66%

profile of v2, /device:TPU:8, one launch (start us, length us, event | category | flops | bytes accessed | tf_op | source)
XLA Modules:
  0.0 554.7 jit_solution(10725644304329114544)
XLA Ops:
  7.2 1.9 constant_dynamic-slice_fusion.1
  9.2 1.6 collective-permute-start
  10.8 0.8 slice_compare_fusion
  12.1 1.5 copy.42.refs_6_.refs_15_
  13.9 1.0 fusion
  14.9 1.0 pad_maximum_fusion
  15.9 48.1 %attention_forward.1 = (bf16[512,2048]{1,0:T(8,128)(2,1)}, f32[512,1024]{1,0:T(8,128)}, f32[512,128]{1,0:T(8,128)}, bf16[512,1024]{1,0:T(8,128)(2,1)}, bf16[512,...) custom-call(bf16[512,2048]{1,0:T(8,128)(2,1)} %refs_0_.1, ...), custom_call_target="tpu_custom_call" | custom-call | tf_op jit(solution)/shard_map/attention_forward/pallas_call | solution.py:1136
  63.9 0.6 collective-permute-start.1
  64.5 1.5 collective-permute-start.2
  66.0 0.7 constant_dynamic-slice_fusion
  66.8 0.6 convert_bitcast_fusion.2.refs_1_
  67.4 0.5 collective-permute-start.5
  67.9 52.0 %gather_rows.1 = (bf16[1024,2048]{1,0:T(8,128)(2,1)}, f32[128,128]{1,0:T(8,128)}) custom-call(bf16[128,2048]{1,0:T(8,128)(2,1)} %get-tuple-element.68.refs_0_, f32[16,128]{1,0:T(8,128)} %convert_bitcast_fusion.2.refs_1_), custom_call_target="tpu_custom_call" | custom-call | tf_op jit(solution)/shard_map/gather_rows/pallas_call | solution.py:594
  119.9 12.9 %collective-permute-done.2.refs_13_ = bf16[2,192,2048]{2,1,0:T(8,128)(2,1)} collective-permute-done((bf16[2,192,2048]{2,1,0:T(8,128)(2,1)}, bf16[2,192,2048]{2,1,0:T(8,128)(2,1)}, u32[]{:S(2)}, u32[]{:S(2)}) %collective-permute-start.2) | collective-permute-done | bytes 1572896 | tf_op jit(solution)/shard_map/ppermute | solution.py:1432
  132.9 1.1 copy-done.8
  134.0 0.5 collective-permute-start.8
  134.5 0.8 broadcast_compare_fusion
  135.6 3.5 fusion.10
  139.5 1.1 dynamic-slice_divide_fusion.refs_2_
  140.7 1.1 copy-done.9
  141.8 97.6 %expert_rows.1 = (f32[128,2176]{1,0:T(8,128)}, bf16[1024,2048]{1,0:T(8,128)(2,1)}, bf16[4,2,192,2048]{3,2,1,0:T(8,128)(2,1)}, bf16[4,2,192,2048]{3,2,1,0:T(8,128)(2,1)}, bf16[4,2,192,2048]{3,2,1,0:T(8,128)(2,1)}) custom-call(bf16[1024,2048]{1,0:T(8,128)(2,1)} %get-tuple-element.70.refs_0_, bf16[1024,2048]{1,0:T(8,128)(2,1)} %all-gather.2.cloned.1.call-done.refs_1_, ...), custom_call_target="tpu_custom_call" | custom-call | tf_op jit(solution)/shard_map/expert_rows/pallas_call | solution.py:989
  239.5 0.7 reduce-scatter.8.cloned.1.call-update
  240.2 0.5 reduce-scatter.6.cloned.1.call-update
  240.9 2.0 constant_dynamic-slice_fusion.2.refs_9_
  243.8 0.6 multiply_reduce_fusion
  244.4 2.5 fusion.6
  246.9 138.2 %attention_backward.1 = (bf16[2048,1024]{1,0:T(8,128)(2,1)}, bf16[2048,256]{1,0:T(8,128)(2,1)}, bf16[128,2048]{1,0:T(8,128)(2,1)}, f32[8,2048]{1,0:T(8,128)}, f3...) custom-call(bf16[512,1024]{1,0:T(8,128)(2,1)} %get-tuple-element.54.refs_0_, ...), custom_call_target="tpu_custom_call" | custom-call | tf_op jit(solution)/shard_map/attention_backward/pallas_call | solution.py:1373
  385.2 0.9 slice.62
  386.5 0.7 constant_dynamic-update-slice_fusion.1
  387.2 0.7 constant_dynamic-update-slice_fusion
  387.9 0.7 reshape.120.refs_3_
  388.6 6.5 %maximum_convert_fusion = f32[1024,2048]{1,0:T(8,128)} fusion(bf16[1024,512]{1,0:T(8,128)(2,1)S(1)} %copy-done.11, bf16[1024,1536]{1,0:T(8,128)(2,1)} %get-tuple-element.89), kind=kLoop, calls=%fused_computation | loop fusion | flops 8388608 | bytes 12582912 | tf_op jit(solution)/shard_map/convert_element_type | solution.py:1672
  395.1 1.9 add_convert_fusion.refs_5_
  397.0 125.5 %sum_and_gather.1 = (bf16[2048,1024]{1,0:T(8,128)(2,1)}, bf16[2048,256]{1,0:T(8,128)(2,1)}, f32[64,640]{1,0:T(8,128)}, bf16[512,2048]{1,0:T(8,128)(2,1)}, bf16[5...) custom-call(bf16[2048,1024]{1,0:T(8,128)(2,1)} %get-tuple-element.76.refs_0_, bf16[2048,256]{1,0:T(8,128)(2,1)} %get-tuple-element.77.refs_1_, ...), custom_call_target="tpu_custom_call" | custom-call | tf_op jit(solution)/shard_map/sum_and_gather/pallas_call | solution.py:746
  522.6 1.0 slice.71
  523.5 0.9 reshape.121
  524.5 6.7 %convert_element_type.57 = f32[2048,1024]{1,0:T(8,128)} convert(bf16[2048,1024]{1,0:T(8,128)(2,1)} %get-tuple-element.87) | non-fusion elementwise | flops 2097152 | bytes 12582912 | tf_op jit(solution)/shard_map/convert_element_type | solution.py:1667
  531.2 0.5 fusion.9
  531.7 0.6 fusion.8
  532.3 0.7 slice_bitcast_fusion
  533.0 1.5 slice_convert_fusion
  534.4 3.4 convert_bitcast_fusion
  537.9 3.6 convert_bitcast_fusion.1
  541.5 1.3 copy.60
  542.8 1.0 copy-done.4
  543.8 1.3 copy.61
  545.1 1.3 copy-done.3
  546.5 1.7 copy.62
  (69 shorter events, 3.1 us)
Async XLA Ops:
  7.2 128.4 %copy-start = (bf16[2048,16]{0,1:T(8,128)(2,1)S(1)}, bf16[2048,16]{0,1:T(8,128)(2,1)}, u32[]{:S(2)}) copy-start(bf16[2048,16]{0,1:T(8,128)(2,1)} %param.27) | copy-start | bytes 196612
  7.2 133.5 %all-gather.2.cloned.1.call-start = ((), (), s32[]{:S(2)}) async-start(), calls=%async_computation.3 | async-start | bytes 4718592 | tf_op jit(solution)/shard_map/all_gather | solution.py:1473
  9.2 385.9 %reduce-scatter.4.cloned.1.call-start = ((), (), s32[]{:S(2)}) async-start(), calls=%async_computation.4 | async-start | bytes 4718592 | tf_op jit(solution)/shard_map/reduce_scatter | solution.py:1597
  9.2 54.7 %collective-permute-start = (bf16[2,192,2048]{2,1,0:T(8,128)(2,1)}, bf16[2,192,2048]{2,1,0:T(8,128)(2,1)}, u32[]{:S(2)}, u32[]{:S(2)}) collective-permute-start(bf16[2,192,2048]{2,1,0:T(8,128)(2,1)} %bitcast.52), channel_id=1, source_target_pairs={{0,2},{1,3},{2,0},{3,1},{4,6},{5,7},{6,4},{7,5},{8,10},{9,11},{10,... | collective-permute-start | bytes 4718600 | tf_op jit(solution)/shard_map/ppermute | solution.py:1432
  15.9 50.2 %copy-start.7 = (bf16[2,2048,192]{1,2,0:T(8,128)(2,1)S(1)}, bf16[2,2048,192]{1,2,0:T(8,128)(2,1)}, u32[]{:S(2)}) copy-start(bf16[2,2048,192]{1,2,0:T(8,128)(2,1)} %param.28) | copy-start | bytes 4718596
  63.9 55.9 %collective-permute-start.1 = (bf16[2,192,2048]{2,1,0:T(8,128)(2,1)}, bf16[2,192,2048]{2,1,0:T(8,128)(2,1)}, u32[]{:S(2)}, u32[]{:S(2)}) collective-permute-start(bf16[2,192,2048]{2,1,0:T(8,128)(2,1)} %bitcast.9.refs_7_), channel_id=1, source_target_pairs={{0,2},{1,3},{2,0},{3,1},{4,6},{5,7},{6,4},{7,5},{8,10},{9,11},{10,... | collective-permute-start | bytes 4718600 | tf_op jit(solution)/shard_map/ppermute | solution.py:1432
  64.5 68.3 %collective-permute-start.2 = (bf16[2,192,2048]{2,1,0:T(8,128)(2,1)}, bf16[2,192,2048]{2,1,0:T(8,128)(2,1)}, u32[]{:S(2)}, u32[]{:S(2)}) collective-permute-start(bf16[2,192,2048]{2,1,0:T(8,128)(2,1)} %refs_11_.1), channel_id=1, source_target_pairs={{0,2},{1,3},{2,0},{3,1},{4,6},{5,7},{6,4},{7,5},{8,10},{9,11},{10,... | collective-permute-start | bytes 4718600 | tf_op jit(solution)/shard_map/ppermute | solution.py:1432
  66.0 66.8 %collective-permute-start.3 = (bf16[2,192,2048]{2,1,0:T(8,128)(2,1)S(1)}, bf16[2,192,2048]{2,1,0:T(8,128)(2,1)S(1)}, u32[]{:S(2)}, u32[]{:S(2)}) collective-permute-start(bf16[2,192,2048]{2,1,0:T(8,128)(2,1)S(1)} %bitcast.54), channel_id=1, source_target_pairs={{0,1},{1,0},{2,3},{3,2},{4,5},{5,4},{6,7},{7,6},{8,9},{9,8},{10,11... | collective-permute-start | bytes 4718600 | tf_op jit(solution)/shard_map/ppermute | solution.py:1428
  67.4 73.2 %collective-permute-start.5 = (bf16[2,192,2048]{2,1,0:T(8,128)(2,1)}, bf16[2,192,2048]{2,1,0:T(8,128)(2,1)}, u32[]{:S(2)}, u32[]{:S(2)}) collective-permute-start(bf16[2,192,2048]{2,1,0:T(8,128)(2,1)} %bitcast.9.refs_7_), channel_id=1, source_target_pairs={{0,1},{1,0},{2,3},{3,2},{4,5},{5,4},{6,7},{7,6},{8,9},{9,8},{10,11... | collective-permute-start | bytes 4718600 | tf_op jit(solution)/shard_map/ppermute | solution.py:1428
  67.9 72.7 %collective-permute-start.7 = (bf16[2,192,2048]{2,1,0:T(8,128)(2,1)}, bf16[2,192,2048]{2,1,0:T(8,128)(2,1)}, u32[]{:S(2)}, u32[]{:S(2)}) collective-permute-start(bf16[2,192,2048]{2,1,0:T(8,128)(2,1)} %refs_11_.1), channel_id=1, source_target_pairs={{0,1},{1,0},{2,3},{3,2},{4,5},{5,4},{6,7},{7,6},{8,9},{9,8},{10,11... | collective-permute-start | bytes 4718600 | tf_op jit(solution)/shard_map/ppermute | solution.py:1428
  119.8 20.8 %collective-permute-start.4 = (bf16[2,192,2048]{2,1,0:T(8,128)(2,1)}, bf16[2,192,2048]{2,1,0:T(8,128)(2,1)}, u32[]{:S(2)}, u32[]{:S(2)}) collective-permute-start(bf16[2,192,2048]{2,1,0:T(8,128)(2,1)} %collective-permute-done.refs_5_), channel_id=1, source_target_pairs={{0,1},{1,0},{2,3},{3,2},{4,5},{5,4},{6,7},{7,6},{8,9},{9,8},{10,11... | collective-permute-start | bytes 4718600 | tf_op jit(solution)/shard_map/ppermute | solution.py:1428
  132.9 7.7 %collective-permute-start.6 = (bf16[2,192,2048]{2,1,0:T(8,128)(2,1)}, bf16[2,192,2048]{2,1,0:T(8,128)(2,1)}, u32[]{:S(2)}, u32[]{:S(2)}) collective-permute-start(bf16[2,192,2048]{2,1,0:T(8,128)(2,1)} %collective-permute-done.1.refs_9_), channel_id=1, source_target_pairs={{0,1},{1,0},{2,3},{3,2},{4,5},{5,4},{6,7},{7,6},{8,9},{9,8},{10,11... | collective-permute-start | bytes 4718600 | tf_op jit(solution)/shard_map/ppermute | solution.py:1428
  132.9 1.1 copy-start.8
  134.0 6.6 %collective-permute-start.8 = (bf16[2,192,2048]{2,1,0:T(8,128)(2,1)}, bf16[2,192,2048]{2,1,0:T(8,128)(2,1)S(1)}, u32[]{:S(2)}, u32[]{:S(2)}) collective-permute-start(bf16[2,192,2048]{2,1,0:T(8,128)(2,1)} %collective-permute-done.2.refs_13_), channel_id=1, source_target_pairs={{0,1},{1,0},{2,3},{3,2},{4,5},{5,4},{6,7},{7,6},{8,9},{9,8},{10,11... | collective-permute-start | bytes 4718600 | tf_op jit(solution)/shard_map/ppermute | solution.py:1428
  140.6 1.1 copy-start.9
  239.4 295.0 %reduce-scatter.8.cloned.1.call-start = ((), (), s32[]{:S(2)}) async-start(), calls=%async_computation.6 | async-start | bytes 7864320 | tf_op jit(solution)/shard_map/reduce_scatter | solution.py:1599
  240.1 297.7 %reduce-scatter.6.cloned.1.call-start = ((), (), s32[]{:S(2)}) async-start(), calls=%async_computation.5 | async-start | bytes 7864320 | tf_op jit(solution)/shard_map/reduce_scatter | solution.py:1599
  240.2 2.7 copy-start.6
  240.7 2.7 copy-start.2
  240.7 2.9 copy-start.10
  240.7 3.1 copy-start.13
  385.2 3.5 copy-start.11
  524.4 8.5 %copy-start.12 = (bf16[2048,256]{1,0:T(8,128)(2,1)S(1)}, bf16[2048,256]{1,0:T(8,128)(2,1)}, u32[]{:S(2)}) copy-start(bf16[2048,256]{1,0:T(8,128)(2,1)} %get-tuple-element.88) | copy-start | bytes 3145732
  537.9 3.6 copy-start.5
  541.5 2.3 copy-start.4
  543.8 2.6 copy-start.3
  543.8 4.3 copy-start.1
Sparse Core Ops, SparseCore 0:
  10.7 83.5 all-gather.1
  239.5 118.4 reduce-scatter.3
  360.7 61.5 reduce-scatter.7
  424.7 74.6 reduce-scatter.5

commit v3 on v2

--- a/solution.py
+++ b/solution.py
@@ -761,6 +761,7 @@
 PAIR_US = 1.5
 HEAD_US = 5.5
 TILE_US = 1.5
+FORWARD_US = 3.0
 EXTRA = 128
 
 
@@ -768,11 +769,12 @@
     return 4 * columns // 5 // 256 * 256
 
 
-def expert_rows(normed, cot, gates, weights_rel, shards, number):
+def expert_rows(normed, cot, chosen, router, gate_rel, up_first, up_rel, down_rel, number):
     grid = grid_of("expert")
     _, lines, width, _ = grid
     size = lines * width
-    experts, hidden, columns = weights_rel[0].shape
+    experts, hidden, columns = gate_rel[0].shape
+    shards = len(gate_rel)
     full = shards * hidden
     both = 2 * full
     total_rows = normed.shape[0]
@@ -789,14 +791,16 @@
 
     def kernel(*refs):
         take = Taker(refs)
-        normed_hbm, cot_hbm, gates_ref = take.take(3)
-        gate_hbm, up_hbm, down_hbm = take.take(shards), take.take(shards), take.take(shards)
+        normed_hbm, cot_hbm, chosen_hbm, router_ref = take.take(4)
+        gate_hbm, up_first_hbm = take.take(shards), take.one()
+        up_hbm, down_hbm = take.take(shards), take.take(shards)
         sum_ref, out_hbm = take.take(2)
         grad_hbm = take.take(3)
         normed_v, cot_v, weights, down = take.take(4)
         grads_low, act_low, parts = take.take(3)
         buffers = take.take(3)
         out_stage, grad_stage, d_gates_ref = take.take(3)
+        gates_ref, chosen_v = take.take(2)
         load_sems, weight_sems, out_sems, grad_sems = take.take(4)
         job = Scatter(grid, parts, buffers, 1, take.take(6))
         me, z, _ = position(grid)
@@ -815,6 +819,7 @@
 
         loads = [
             pltpu.make_async_copy(normed_hbm, normed_v, load_sems.at[0]),
+            pltpu.make_async_copy(chosen_hbm, chosen_v, load_sems.at[2]),
             pltpu.make_async_copy(cot_hbm, cot_v, load_sems.at[1]),
         ]
         weight_loads = [[] for _ in range(experts)]
@@ -823,7 +828,12 @@
                 for w, (source, target) in enumerate(
                     (
                         (gate_hbm[r].at[j], weights.at[pl.ds(j * both + r * hidden, hidden)]),
-                        (up_hbm[r].at[j], weights.at[pl.ds(j * both + full + r * hidden, hidden)]),
+                        (
+                            up_hbm[r].at[j - 1]
+                            if j
+                            else slice_of(up_first_hbm, places[r] * hidden, hidden),
+                            weights.at[pl.ds(j * both + full + r * hidden, hidden)],
+                        ),
                         (down_hbm[r].at[j], down.at[pl.ds(j * full + r * hidden, hidden)]),
                     )
                 ):
@@ -839,6 +849,21 @@
         for c in loads:
             c.wait()
 
+        lane = lax.broadcasted_iota(jnp.int32, (half, EXTRA), 1)
+
+        @pl.loop(0, total_rows // half)
+        def _(m):
+            rows = pl.ds(pl.multiple_of(m * half, half), half)
+            named = chosen_v[rows, :].astype(F32) > 0.5
+            logits = jnp.where(named, dot(normed_v[rows, :], router_ref[...]), -1e30)
+            top = jnp.max(logits, axis=-1, keepdims=True)
+            powers = jnp.where(named, jnp.exp(logits - top), 0.0)
+            probs = powers / jnp.sum(powers, axis=-1, keepdims=True)
+            for j in range(experts):
+                gates_ref[rows, j : j + 1] = jnp.sum(
+                    jnp.where(lane == me * experts + j, probs, 0.0), axis=-1, keepdims=True
+                )
+
         for j in range(experts):
             for c in weight_loads[j]:
                 c.wait()
@@ -995,7 +1020,7 @@
             weight_shape,
             weight_shape,
         ],
-        in_specs=[hbm()] * 2 + [vmem()] + [hbm()] * (3 * shards),
+        in_specs=[hbm()] * 3 + [vmem()] + [hbm()] * (3 * shards + 1),
         out_specs=[vmem()] + [hbm()] * 4,
         scratch_shapes=[
             pltpu.VMEM((total_rows, columns), BF),
@@ -1011,15 +1036,17 @@
             pltpu.VMEM((2, total_rows, tile), BF),
             pltpu.VMEM((2, wide, columns), BF),
             pltpu.VMEM((total_rows, experts), F32),
-            dma((2,)),
+            pltpu.VMEM((total_rows, experts), F32),
+            pltpu.VMEM((total_rows, EXTRA), BF),
+            dma((3,)),
             dma((experts, shards, 3)),
             dma((2,)),
             dma((2, 2)),
         ]
         + Scatter.sems(grid, 1),
-        compiler_params=params(number, 62),
+        compiler_params=params(number, 63),
         name="expert_rows",
-    )(normed, cot, gates, *weights_rel)
+    )(normed, cot, chosen, router, *gate_rel, up_first, *up_rel, *down_rel)
 
 
 def rms_forward(vector, gain):
@@ -1033,9 +1060,9 @@
     return inverse * scaled - vector * (inverse * inverse * inverse * inner)
 
 
-def attention_forward(arrays, heads, number):
-    side = grid_of("shard")
-    shards = side[1] * side[2]
+def attention_forward(arrays, cot_own, up_own, heads, number):
+    grid, side = grid_of("expert"), grid_of("shard")
+    size, shards = grid[1] * grid[2], side[1] * side[2]
     names = list(arrays)
     tokens, columns = arrays["rows"].shape
     inner = arrays["query_weight"].shape[1]
@@ -1048,21 +1075,40 @@
     def kernel(*refs):
         take = Taker(refs)
         hbm_refs = take.take(len(names))
+        cot_ref, up_ref = take.take(2)
         normed, query_lin, key_lin, query, key, value, mixed, log_total = take.take(8)
         residual, normed_two = take.take(2)
+        cot_all, up_all = take.take(2)
         v = dict(zip(names, take.take(len(names))))
         bias, parts, summed = take.take(3)
         buffers = take.take(3)
-        load_sems = take.one()
+        load_sems, own_sems = take.take(2)
         job = Scatter(side, parts, buffers, 2, take.take(6))
+        cot_job = Gather(grid, cot_ref, cot_all, 2, take.take(4))
+        up_job = Gather(side, up_ref, up_all, 1, take.take(4))
         shard = lax.axis_index("shard")
+        cot_plan = Plan(grid[1])
+        for p in range(2):
+            plan_gather(cot_plan, cot_job, p, 0.0)
+        cot_order = cot_plan.order()
+
+        def own_cot(z):
+            return pltpu.make_async_copy(cot_ref, cot_job.own_slot(z), own_sems.at[0])
+
+        def own_up(z):
+            return pltpu.make_async_copy(up_ref, up_job.own_slot(z), own_sems.at[1])
+
         loads = [
             pltpu.make_async_copy(ref, v[name], load_sems.at[i])
             for i, (name, ref) in enumerate(zip(names, hbm_refs))
         ]
         for c in loads:
             c.start()
-        greet([side])
+        at_each_line(grid, lambda z: own_cot(z).start())
+        at_each_line(side, lambda z: own_up(z).start())
+        greet([grid, side])
+        cot_plan.run(grid, cot_order, 0.0, 2.0)
+        at_each_line(side, lambda z: up_job.start(z, 0))
         for c in loads[:-1]:
             c.wait()
 
@@ -1090,6 +1136,8 @@
         cols_at = lax.broadcasted_iota(jnp.int32, (tokens, tokens), 1)
         allowed = jnp.logical_and(v["doc_col"][...] == v["doc_row"][...], rows_at >= cols_at)
         bias[...] = jnp.where(allowed, 0.0, -1e30)
+
+        cot_order_late = [[s for s in steps if s[0] >= 2.0] for steps in cot_order]
 
         @pl.loop(0, heads)
         def _(h):
@@ -1105,6 +1153,7 @@
                 log_total[h, rows, :] = top + jnp.log(total)
                 probs = (powers * (1.0 / total)).astype(BF)
                 mixed[rows, lanes] = dot(probs, value[keys, :]).astype(BF)
+            cot_plan.run_step(grid, cot_order_late, h, 10.0, FORWARD_US, heads, True)
 
         loads[-1].wait()
 
@@ -1120,6 +1169,14 @@
         for p in range(2):
             plan_scatter(plan, job, p, put)
         plan.run(side, plan.order(), *ALWAYS)
+        cot_plan.run(grid, cot_order, 10.0 + heads * FORWARD_US, 1e9)
+
+        def forward_up(z):
+            for origin in range(side[1]):
+                if origin != z:
+                    up_job.forward(z, origin, 0)
+
+        at_each_line(side, forward_up)
 
         @pl.loop(0, own_rows // 16)
         def _(i):
@@ -1130,6 +1187,17 @@
             normed_two[rows, :] = norm(total, v["norm_two_gain"][...]).astype(BF)
 
         at_each_line(side, job.finish)
+
+        def end_cot(z):
+            cot_job.finish(z)
+            own_cot(z).wait()
+
+        def end_up(z):
+            up_job.finish(z)
+            own_up(z).wait()
+
+        at_each_line(side, end_up)
+        at_each_line(grid, end_cot)
 
     values = [arrays[name] for name in names]
     shape = jax.ShapeDtypeStruct
@@ -1146,9 +1214,11 @@
             shape((heads, tokens, 1), F32),
             shape((own_rows, columns), F32),
             shape((own_rows, columns), BF),
+            shape((size * own_rows, columns), BF),
+            shape((shards * up_own.shape[0], columns), BF),
         ],
-        in_specs=[hbm()] * len(names),
-        out_specs=[vmem()] * 10,
+        in_specs=[hbm()] * (len(names) + 2),
+        out_specs=[vmem()] * 10 + [hbm()] * 2,
         scratch_shapes=[pltpu.VMEM(a.shape, a.dtype) for a in values]
         + [
             pltpu.VMEM((tokens, tokens), F32),
@@ -1156,11 +1226,13 @@
             pltpu.VMEM((own_rows, columns), F32),
         ]
         + Scatter.buffers(side, own_rows, columns, BF)
-        + [pltpu.SemaphoreType.DMA((len(names),))]
-        + Scatter.sems(side, 2),
+        + [pltpu.SemaphoreType.DMA((len(names),)), pltpu.SemaphoreType.DMA((2,))]
+        + Scatter.sems(side, 2)
+        + Gather.sems(grid, 2)
+        + Gather.sems(side, 1),
         compiler_params=params(number),
         name="attention_forward",
-    )(*values)
+    )(*values, cot_own, up_own)
 
 
 def attention_backward(arrays, d_own, heads, number):
@@ -1470,7 +1542,6 @@
 
     fused = expert_peers * rows_here <= VMEM_ROWS
     cot_own = own(cotangent)
-    cot_all = lax.all_gather(cot_own, "expert", axis=0, tiled=True)
     routes_own = own(routes)
     experts = jnp.arange(experts_all, dtype=jnp.int32)
     chosen_own = jnp.any(routes_own[:, :, None] == experts[None, None, :], axis=1)
@@ -1502,9 +1573,10 @@
     forward = dict(
         rows=layer_input, norm_two_gain=norm2_gain[None, :], **shared, out_weight=out_weight
     )
-    normed_one, query_lin, key_lin, query, key, value, mixed, log_total, residual, normed_two = (
-        attention_forward(forward, heads_here, 1)
+    normed_one, query_lin, key_lin, query, key, value, mixed, log_total, *rest = (
+        attention_forward(forward, cot_own, up_weight[0], heads_here, 1)
     )
+    residual, normed_two, cot_all, up_first = rest
     if fused:
         gate_far, residual, normed_two = lax.optimization_barrier(
             (gate_far, residual, normed_two)
@@ -1512,25 +1584,22 @@
 
     if fused:
         up_late, down_late, normed_two = lax.optimization_barrier(
-            (up_weight, down_weight, normed_two)
+            (up_weight[1:], down_weight, normed_two)
         )
         up_far, down_far = from_far(up_late, shard_count), from_far(down_late, shard_count)
         up_near, down_near = from_near(up_late, shard_count), from_near(down_late, shard_count)
     _, inverse_two = rms_forward(residual, norm2_gain)
-    normed_all, chosen_all = gather_rows(
-        [normed_two, chosen_own.T.astype(F32)], [], 2, (2, 1)
-    )
+    chosen_wide = jnp.pad(chosen_own.astype(BF), ((0, 0), (0, EXTRA - experts_all)))
+    normed_all, chosen_all = gather_rows([normed_two, chosen_wide], [], 2, (2, 1))
     if fused:
         up_far, down_far, normed_all = lax.optimization_barrier((up_far, down_far, normed_all))
-        weights_rel = []
+        rel = []
         for own_one, near, far in (
             (gate_weight, gate_near, gate_far),
-            (up_weight, up_near, up_far),
-            (down_weight, down_near, down_far),
+            (up_late, up_near, up_far),
+            (down_late, down_near, down_far),
         ):
-            weights_rel += [own_one, near, far, from_near(far, shard_count)]
-    chosen_all = chosen_all.reshape(expert_peers, experts_all, rows_here).transpose(0, 2, 1)
-    chosen_all = chosen_all.reshape(expert_peers * rows_here, experts_all) > 0.5
+            rel.append([own_one, near, far, from_near(far, shard_count)])
 
     def gate_table(rows, chosen):
         logits = jnp.where(chosen, dot(rows, router_weight), -jnp.inf)
@@ -1538,13 +1607,10 @@
         powers = jnp.exp(logits - top)
         return powers / jnp.sum(powers, axis=-1, keepdims=True)
 
-    gates_all = gate_table(normed_all, chosen_all)
-    gates_here = lax.dynamic_slice_in_dim(
-        gates_all, expert_index * local_experts, local_experts, axis=1
-    )
     if fused:
+        router_wide = jnp.pad(router_weight, ((0, 0), (0, EXTRA - experts_all)))
         summed, out_part, gate_part, up_part, down_part = expert_rows(
-            normed_all, cot_all, gates_here, weights_rel, shard_count, 3
+            normed_all, cot_all, chosen_all, router_wide, rel[0], up_first, rel[1], rel[2], 3
         )
         d_rows_own = summed[:, :model_width]
         d_gates_own = (
@@ -1552,6 +1618,12 @@
             + summed[:, model_width + experts_all : model_width + 2 * experts_all]
         )
     else:
+        gates_here = lax.dynamic_slice_in_dim(
+            gate_table(normed_all, chosen_all[:, :experts_all] > 0.5),
+            expert_index * local_experts,
+            local_experts,
+            axis=1,
+        )
         column_expert = (jnp.arange(hidden_all, dtype=jnp.int32) // hidden_here) % local_experts
         gate_columns = jnp.zeros((1, 1), F32)
         for j in range(local_experts):

time: 555 us -> 558 us (level)
  Pallas kernels: 461 us -> 480 us
  waiting for transfers between devices: 14.2 us -> 4.26 us
    pallas_call x1, Pallas kernels: 48.1 us -> 63.7 us  [attention_forward(): pl.pallas_call(kernel, out_shape=[shape((tokens, columns), BF), shape((to...]
    ppermute x3, waiting for transfers between devices: 13 us -> 0.01 us  [from_far(): lax.ppermute(rows, 'shard', [(s, (s + 2) % count) for s in range(count)])]
  transfers between devices with their start and end apart: 13 -> 12, of which waited for: 1 -> 2; matrix products, arithmetic and copies ran while one was open for 8% -> 8% of each run, Pallas kernels for 66% -> 68%
where the time goes in v3:
time: 558 us
  Pallas kernels  480 us (86%)
  other arithmetic  30.7 us (6%)
  local copies, waits for them, and re-layouts  22.9 us (4%)
  between operations  14 us (3%)
    pallas_call x1, Pallas kernels, attention_backward(): pl.pallas_call(kernel, out_shape=[jax.ShapeDtypeStruct((columns, share),...  138 us
    pallas_call x1, Pallas kernels, sum_and_gather(): pl.pallas_call(kernel, out_shape=[jax.ShapeDtypeStruct(a.shape, a.dtype)...  126 us
    pallas_call x1, Pallas kernels, expert_rows(): pl.pallas_call(kernel, out_shape=[jax.ShapeDtypeStruct((count, columns +...  99.4 us
    pallas_call x1, Pallas kernels, attention_forward(): pl.pallas_call(kernel, out_shape=[shape((tokens, columns), BF), shape((to...  63.7 us
    pallas_call x1, Pallas kernels, gather_rows(): pl.pallas_call(kernel, out_shape=[jax.ShapeDtypeStruct((g[1] * g[2] * a.s...  52.8 us
  transfers between devices with their start and end apart: 12, of which 2 were waited for; matrix products, arithmetic and copies ran while one was open for 8% of the time, Pallas kernels for 68%

profile of v3, /device:TPU:8, one launch (start us, length us, event | category | flops | bytes accessed | tf_op | source)
XLA Modules:
  0.0 557.6 jit_solution(2183961750755951740)
XLA Ops:
  7.3 1.6 collective-permute-start
  8.8 0.8 slice_compare_fusion
  10.2 1.5 copy.38.refs_6_.refs_15_
  11.9 1.0 fusion
  12.9 1.0 pad_maximum_fusion
  13.9 1.9 constant_dynamic-slice_fusion.2.refs_13_
  15.8 1.0 fusion.7
  16.8 63.7 %attention_forward.1 = (bf16[512,2048]{1,0:T(8,128)(2,1)}, f32[512,1024]{1,0:T(8,128)}, f32[512,128]{1,0:T(8,128)}, bf16[512,1024]{1,0:T(8,128)(2,1)}, bf16[512,...) custom-call(bf16[512,2048]{1,0:T(8,128)(2,1)} %refs_0_.1, ...), custom_call_target="tpu_custom_call" | custom-call | tf_op jit(solution)/shard_map/attention_forward/pallas_call | solution.py:1204
  80.5 0.7 collective-permute-start.2
  81.2 1.4 collective-permute-start.1
  82.8 0.6 pad_convert_fusion.refs_1_
  83.4 0.5 collective-permute-start.7
  83.9 52.8 %gather_rows.1 = (bf16[1024,2048]{1,0:T(8,128)(2,1)}, bf16[1024,128]{1,0:T(8,128)(2,1)}) custom-call(bf16[128,2048]{1,0:T(8,128)(2,1)} %get-tuple-element.70.refs_0_, bf16[128,128]{1,0:T(8,128)(2,1)} %pad_convert_fusion.refs_1_), custom_call_target="tpu_custom_call" | custom-call | tf_op jit(solution)/shard_map/gather_rows/pallas_call | solution.py:594
  136.9 0.5 collective-permute-start.5
  137.4 1.1 copy-done.10
  138.9 0.9 pad.16.refs_3_
  139.8 2.4 collective-permute-done.5.refs_10_
  142.2 0.5 collective-permute-done.6.refs_12_
  142.7 0.4 copy-done.15
  143.0 99.4 %expert_rows.1 = (f32[128,2176]{1,0:T(8,128)}, bf16[1024,2048]{1,0:T(8,128)(2,1)}, bf16[4,2,192,2048]{3,2,1,0:T(8,128)(2,1)}, bf16[4,2,192,2048]{3,2,1,0:T(8,128)(2,1)}, bf16[4,2,192,2048]{3,2,1,0:T(8,128)(2,1)}) custom-call(bf16[1024,2048]{1,0:T(8,128)(2,1)} %get-tuple-element.72.refs_0_, bf16[1024,2048]{1,0:T(8,128)(2,1)} %get-tuple-element.73.refs_1_, ...), custom_call_target="tpu_custom_call" | custom-call | tf_op jit(solution)/shard_map/expert_rows/pallas_call | solution.py:1014
  242.5 0.7 reduce-scatter.8.cloned.1.call-update
  243.3 0.7 reduce-scatter.6.cloned.1.call-update
  244.0 2.0 constant_dynamic-slice_fusion.1.refs_9_
  246.0 0.4 fusion.10
  246.9 0.6 multiply_reduce_fusion
  247.5 2.5 fusion.6
  250.0 137.7 %attention_backward.1 = (bf16[2048,1024]{1,0:T(8,128)(2,1)}, bf16[2048,256]{1,0:T(8,128)(2,1)}, bf16[128,2048]{1,0:T(8,128)(2,1)}, f32[8,2048]{1,0:T(8,128)}, f3...) custom-call(bf16[512,1024]{1,0:T(8,128)(2,1)} %get-tuple-element.56.refs_0_, ...), custom_call_target="tpu_custom_call" | custom-call | tf_op jit(solution)/shard_map/attention_backward/pallas_call | solution.py:1445
  387.8 0.9 slice.70
  389.1 0.7 constant_dynamic-update-slice_fusion.1
  389.8 0.7 constant_dynamic-update-slice_fusion
  390.5 0.7 reshape.112.refs_3_
  391.2 6.5 %maximum_convert_fusion = f32[1024,2048]{1,0:T(8,128)} fusion(bf16[1024,512]{1,0:T(8,128)(2,1)S(1)} %copy-done.12, bf16[1024,1536]{1,0:T(8,128)(2,1)} %get-tuple-element.93), kind=kLoop, calls=%fused_computation | loop fusion | flops 8388608 | bytes 12582912 | tf_op jit(solution)/shard_map/convert_element_type | solution.py:1744
  397.7 1.9 add_convert_fusion.refs_5_
  399.6 125.9 %sum_and_gather.1 = (bf16[2048,1024]{1,0:T(8,128)(2,1)}, bf16[2048,256]{1,0:T(8,128)(2,1)}, f32[64,640]{1,0:T(8,128)}, bf16[512,2048]{1,0:T(8,128)(2,1)}, bf16[5...) custom-call(bf16[2048,1024]{1,0:T(8,128)(2,1)} %get-tuple-element.80.refs_0_, bf16[2048,256]{1,0:T(8,128)(2,1)} %get-tuple-element.81.refs_1_, ...), custom_call_target="tpu_custom_call" | custom-call | tf_op jit(solution)/shard_map/sum_and_gather/pallas_call | solution.py:746
  525.5 1.0 slice.79
  526.5 0.9 reshape.113
  527.4 6.7 %convert_element_type.55 = f32[2048,1024]{1,0:T(8,128)} convert(bf16[2048,1024]{1,0:T(8,128)(2,1)} %get-tuple-element.91) | non-fusion elementwise | flops 2097152 | bytes 12582912 | tf_op jit(solution)/shard_map/convert_element_type | solution.py:1739
  534.1 0.5 fusion.9
  534.7 0.6 fusion.8
  535.3 0.7 slice_bitcast_fusion.1
  535.9 1.5 slice_convert_fusion
  537.4 3.4 convert_bitcast_fusion
  540.8 3.6 convert_bitcast_fusion.1
  544.4 1.3 copy.55
  545.8 1.0 copy-done.5
  546.8 1.3 copy.56
  548.1 1.3 copy-done.4
  549.4 1.7 copy.57
  (72 shorter events, 2.5 us)
Async XLA Ops:
  7.2 75.5 %copy-start = (s32[512,8]{0,1:T(8,128)S(1)}, s32[512,8]{0,1:T(8,128)}, u32[]{:S(2)}) copy-start(s32[512,8]{0,1:T(8,128)} %param.18) | copy-start | bytes 49156
  7.2 8.6 %copy-start.8 = (bf16[2,2048,192]{1,2,0:T(8,128)(2,1)S(1)}, bf16[2,2048,192]{1,2,0:T(8,128)(2,1)}, u32[]{:S(2)}) copy-start(bf16[2,2048,192]{1,2,0:T(8,128)(2,1)} %param.29) | copy-start | bytes 4718596
  7.2 390.5 %reduce-scatter.4.cloned.1.call-start = ((), (), s32[]{:S(2)}) async-start(), calls=%async_computation.3 | async-start | bytes 4718592 | tf_op jit(solution)/shard_map/reduce_scatter | solution.py:1669
  7.3 73.3 %collective-permute-start = (bf16[2,192,2048]{2,1,0:T(8,128)(2,1)}, bf16[2,192,2048]{2,1,0:T(8,128)(2,1)}, u32[]{:S(2)}, u32[]{:S(2)}) collective-permute-start(bf16[2,192,2048]{2,1,0:T(8,128)(2,1)} %bitcast.47), channel_id=1, source_target_pairs={{0,2},{1,3},{2,0},{3,1},{4,6},{5,7},{6,4},{7,5},{8,10},{9,11},{10,... | collective-permute-start | bytes 4718600 | tf_op jit(solution)/shard_map/ppermute | solution.py:1504
  16.8 120.1 %copy-start.3 = (bf16[1,192,2048]{2,1,0:T(8,128)(2,1)}, bf16[1,192,2048]{2,1,0:T(8,128)(2,1)S(1)}, u32[]{:S(2)}) copy-start(bf16[1,192,2048]{2,1,0:T(8,128)(2,1)S(1)} %get-tuple-element.68.refs_9_) | copy-start | bytes 2359300
  16.8 65.8 %copy-start.9 = (bf16[2,2048,192]{1,2,0:T(8,128)(2,1)S(1)}, bf16[2,2048,192]{1,2,0:T(8,128)(2,1)}, u32[]{:S(2)}) copy-start(bf16[2,2048,192]{1,2,0:T(8,128)(2,1)} %param.28) | copy-start | bytes 4718596
  16.8 121.8 %copy-start.16 = (bf16[2048,16]{0,1:T(8,128)(2,1)S(1)}, bf16[2048,16]{0,1:T(8,128)(2,1)}, u32[]{:S(2)}) copy-start(bf16[2048,16]{0,1:T(8,128)(2,1)} %param.27) | copy-start | bytes 196612
  80.5 56.3 %collective-permute-start.2 = (bf16[2,192,2048]{2,1,0:T(8,128)(2,1)}, bf16[2,192,2048]{2,1,0:T(8,128)(2,1)}, u32[]{:S(2)}, u32[]{:S(2)}) collective-permute-start(bf16[2,192,2048]{2,1,0:T(8,128)(2,1)} %refs_13_), channel_id=1, source_target_pairs={{0,2},{1,3},{2,0},{3,1},{4,6},{5,7},{6,4},{7,5},{8,10},{9,11},{10,... | collective-permute-start | bytes 4718600 | tf_op jit(solution)/shard_map/ppermute | solution.py:1504
  81.2 55.5 %collective-permute-start.1 = (bf16[1,192,2048]{2,1,0:T(8,128)(2,1)S(1)}, bf16[1,192,2048]{2,1,0:T(8,128)(2,1)S(1)}, u32[]{:S(2)}, u32[]{:S(2)}) collective-permute-start(bf16[1,192,2048]{2,1,0:T(8,128)(2,1)S(1)} %get-tuple-element.68.refs_9_), channel_id=1, source_target_pairs={{0,2},{1,3},{2,0},{3,1},{4,6},{5,7},{6,4},{7,5},{8,10},{9,11},{10,... | collective-permute-start | bytes 2359304 | tf_op jit(solution)/shard_map/ppermute | solution.py:1504
  82.6 54.7 %collective-permute-start.3 = (bf16[2,192,2048]{2,1,0:T(8,128)(2,1)S(1)}, bf16[2,192,2048]{2,1,0:T(8,128)(2,1)S(1)}, u32[]{:S(2)}, u32[]{:S(2)}) collective-permute-start(bf16[2,192,2048]{2,1,0:T(8,128)(2,1)S(1)} %bitcast.49), channel_id=1, source_target_pairs={{0,1},{1,0},{2,3},{3,2},{4,5},{5,4},{6,7},{7,6},{8,9},{9,8},{10,11... | collective-permute-start | bytes 4718600 | tf_op jit(solution)/shard_map/ppermute | solution.py:1500
  83.4 58.7 %collective-permute-start.7 = (bf16[2,192,2048]{2,1,0:T(8,128)(2,1)}, bf16[2,192,2048]{2,1,0:T(8,128)(2,1)}, u32[]{:S(2)}, u32[]{:S(2)}) collective-permute-start(bf16[2,192,2048]{2,1,0:T(8,128)(2,1)} %refs_13_), channel_id=1, source_target_pairs={{0,1},{1,0},{2,3},{3,2},{4,5},{5,4},{6,7},{7,6},{8,9},{9,8},{10,11... | collective-permute-start | bytes 4718600 | tf_op jit(solution)/shard_map/ppermute | solution.py:1500
  83.9 58.2 %collective-permute-start.4 = (bf16[2,192,2048]{2,1,0:T(8,128)(2,1)}, bf16[2,192,2048]{2,1,0:T(8,128)(2,1)}, u32[]{:S(2)}, u32[]{:S(2)}) collective-permute-start(bf16[2,192,2048]{2,1,0:T(8,128)(2,1)} %collective-permute-done.refs_6_), channel_id=1, source_target_pairs={{0,1},{1,0},{2,3},{3,2},{4,5},{5,4},{6,7},{7,6},{8,9},{9,8},{10,11... | collective-permute-start | bytes 4718600 | tf_op jit(solution)/shard_map/ppermute | solution.py:1500
  136.8 6.3 %copy-start.14 = (bf16[1,192,2048]{2,1,0:T(8,128)(2,1)}, bf16[1,192,2048]{2,1,0:T(8,128)(2,1)S(1)}, u32[]{:S(2)}) copy-start(bf16[1,192,2048]{2,1,0:T(8,128)(2,1)S(1)} %collective-permute-done.1.refs_11_) | copy-start | bytes 2359300
  136.8 6.2 %collective-permute-start.8 = (bf16[2,192,2048]{2,1,0:T(8,128)(2,1)}, bf16[2,192,2048]{2,1,0:T(8,128)(2,1)}, u32[]{:S(2)}, u32[]{:S(2)}) collective-permute-start(bf16[2,192,2048]{2,1,0:T(8,128)(2,1)} %collective-permute-done.2.refs_15_), channel_id=1, source_target_pairs={{0,1},{1,0},{2,3},{3,2},{4,5},{5,4},{6,7},{7,6},{8,9},{9,8},{10,11... | collective-permute-start | bytes 4718600 | tf_op jit(solution)/shard_map/ppermute | solution.py:1500
  136.9 5.3 collective-permute-start.5
  137.4 1.1 copy-start.10
  138.5 4.1 collective-permute-start.6
  142.2 0.9 copy-start.15
  242.4 294.9 %reduce-scatter.8.cloned.1.call-start = ((), (), s32[]{:S(2)}) async-start(), calls=%async_computation.5 | async-start | bytes 7864320 | tf_op jit(solution)/shard_map/reduce_scatter | solution.py:1671
  243.2 297.6 %reduce-scatter.6.cloned.1.call-start = ((), (), s32[]{:S(2)}) async-start(), calls=%async_computation.4 | async-start | bytes 7864320 | tf_op jit(solution)/shard_map/reduce_scatter | solution.py:1671
  243.2 2.8 copy-start.7
  243.9 2.6 copy-start.2
  243.9 2.8 copy-start.11
  244.0 3.0 copy-start.17
  387.8 3.5 copy-start.12
  527.4 8.5 %copy-start.13 = (bf16[2048,256]{1,0:T(8,128)(2,1)S(1)}, bf16[2048,256]{1,0:T(8,128)(2,1)}, u32[]{:S(2)}) copy-start(bf16[2048,256]{1,0:T(8,128)(2,1)} %get-tuple-element.92) | copy-start | bytes 3145732
  540.8 3.6 copy-start.6
  544.4 2.3 copy-start.5
  546.8 2.6 copy-start.4
  546.8 4.3 copy-start.1
Sparse Core Ops, SparseCore 0:
  242.6 118.4 reduce-scatter.3
  363.7 61.5 reduce-scatter.7
  427.9 73.8 reduce-scatter.5

commit v4 on v3

--- a/solution.py
+++ b/solution.py
@@ -792,7 +792,7 @@
     def kernel(*refs):
         take = Taker(refs)
         normed_hbm, cot_hbm, chosen_hbm, router_ref = take.take(4)
-        gate_hbm, up_first_hbm = take.take(shards), take.one()
+        gate_hbm, up_first_hbm = take.take(shards), take.take(shards)
         up_hbm, down_hbm = take.take(shards), take.take(shards)
         sum_ref, out_hbm = take.take(2)
         grad_hbm = take.take(3)
@@ -831,7 +831,7 @@
                         (
                             up_hbm[r].at[j - 1]
                             if j
-                            else slice_of(up_first_hbm, places[r] * hidden, hidden),
+                            else up_first_hbm[r].at[0],
                             weights.at[pl.ds(j * both + full + r * hidden, hidden)],
                         ),
                         (down_hbm[r].at[j], down.at[pl.ds(j * full + r * hidden, hidden)]),
@@ -1020,7 +1020,7 @@
             weight_shape,
             weight_shape,
         ],
-        in_specs=[hbm()] * 3 + [vmem()] + [hbm()] * (3 * shards + 1),
+        in_specs=[hbm()] * 3 + [vmem()] + [hbm()] * (4 * shards),
         out_specs=[vmem()] + [hbm()] * 4,
         scratch_shapes=[
             pltpu.VMEM((total_rows, columns), BF),
@@ -1046,7 +1046,7 @@
         + Scatter.sems(grid, 1),
         compiler_params=params(number, 63),
         name="expert_rows",
-    )(normed, cot, chosen, router, *gate_rel, up_first, *up_rel, *down_rel)
+    )(normed, cot, chosen, router, *gate_rel, *up_first, *up_rel, *down_rel)
 
 
 def rms_forward(vector, gain):
@@ -1060,7 +1060,7 @@
     return inverse * scaled - vector * (inverse * inverse * inverse * inner)
 
 
-def attention_forward(arrays, cot_own, up_own, heads, number):
+def attention_forward(arrays, cot_own, heads, number):
     grid, side = grid_of("expert"), grid_of("shard")
     size, shards = grid[1] * grid[2], side[1] * side[2]
     names = list(arrays)
@@ -1075,17 +1075,16 @@
     def kernel(*refs):
         take = Taker(refs)
         hbm_refs = take.take(len(names))
-        cot_ref, up_ref = take.take(2)
+        cot_ref = take.one()
         normed, query_lin, key_lin, query, key, value, mixed, log_total = take.take(8)
         residual, normed_two = take.take(2)
-        cot_all, up_all = take.take(2)
+        cot_all = take.one()
         v = dict(zip(names, take.take(len(names))))
         bias, parts, summed = take.take(3)
         buffers = take.take(3)
         load_sems, own_sems = take.take(2)
         job = Scatter(side, parts, buffers, 2, take.take(6))
         cot_job = Gather(grid, cot_ref, cot_all, 2, take.take(4))
-        up_job = Gather(side, up_ref, up_all, 1, take.take(4))
         shard = lax.axis_index("shard")
         cot_plan = Plan(grid[1])
         for p in range(2):
@@ -1094,9 +1093,6 @@
 
         def own_cot(z):
             return pltpu.make_async_copy(cot_ref, cot_job.own_slot(z), own_sems.at[0])
-
-        def own_up(z):
-            return pltpu.make_async_copy(up_ref, up_job.own_slot(z), own_sems.at[1])
 
         loads = [
             pltpu.make_async_copy(ref, v[name], load_sems.at[i])
@@ -1105,10 +1101,8 @@
         for c in loads:
             c.start()
         at_each_line(grid, lambda z: own_cot(z).start())
-        at_each_line(side, lambda z: own_up(z).start())
         greet([grid, side])
         cot_plan.run(grid, cot_order, 0.0, 2.0)
-        at_each_line(side, lambda z: up_job.start(z, 0))
         for c in loads[:-1]:
             c.wait()
 
@@ -1171,13 +1165,6 @@
         plan.run(side, plan.order(), *ALWAYS)
         cot_plan.run(grid, cot_order, 10.0 + heads * FORWARD_US, 1e9)
 
-        def forward_up(z):
-            for origin in range(side[1]):
-                if origin != z:
-                    up_job.forward(z, origin, 0)
-
-        at_each_line(side, forward_up)
-
         @pl.loop(0, own_rows // 16)
         def _(i):
             rows = pl.ds(pl.multiple_of(i * 16, 16), 16)
@@ -1192,11 +1179,6 @@
             cot_job.finish(z)
             own_cot(z).wait()
 
-        def end_up(z):
-            up_job.finish(z)
-            own_up(z).wait()
-
-        at_each_line(side, end_up)
         at_each_line(grid, end_cot)
 
     values = [arrays[name] for name in names]
@@ -1215,10 +1197,9 @@
             shape((own_rows, columns), F32),
             shape((own_rows, columns), BF),
             shape((size * own_rows, columns), BF),
-            shape((shards * up_own.shape[0], columns), BF),
         ],
-        in_specs=[hbm()] * (len(names) + 2),
-        out_specs=[vmem()] * 10 + [hbm()] * 2,
+        in_specs=[hbm()] * (len(names) + 1),
+        out_specs=[vmem()] * 10 + [hbm()],
         scratch_shapes=[pltpu.VMEM(a.shape, a.dtype) for a in values]
         + [
             pltpu.VMEM((tokens, tokens), F32),
@@ -1226,13 +1207,12 @@
             pltpu.VMEM((own_rows, columns), F32),
         ]
         + Scatter.buffers(side, own_rows, columns, BF)
-        + [pltpu.SemaphoreType.DMA((len(names),)), pltpu.SemaphoreType.DMA((2,))]
+        + [pltpu.SemaphoreType.DMA((len(names),)), pltpu.SemaphoreType.DMA((1,))]
         + Scatter.sems(side, 2)
-        + Gather.sems(grid, 2)
-        + Gather.sems(side, 1),
+        + Gather.sems(grid, 2),
         compiler_params=params(number),
         name="attention_forward",
-    )(*values, cot_own, up_own)
+    )(*values, cot_own)
 
 
 def attention_backward(arrays, d_own, heads, number):
@@ -1550,6 +1530,8 @@
     if fused:
         gate_far = from_far(gate_weight, shard_count)
         gate_near = from_near(gate_weight, shard_count)
+        first_far = from_far(up_weight[:1], shard_count)
+        first_near = from_near(up_weight[:1], shard_count)
     else:
         down_all = gather_weight(down_weight)
         gate_all = gather_weight(gate_weight)
@@ -1574,12 +1556,12 @@
         rows=layer_input, norm_two_gain=norm2_gain[None, :], **shared, out_weight=out_weight
     )
     normed_one, query_lin, key_lin, query, key, value, mixed, log_total, *rest = (
-        attention_forward(forward, cot_own, up_weight[0], heads_here, 1)
+        attention_forward(forward, cot_own, heads_here, 1)
     )
-    residual, normed_two, cot_all, up_first = rest
+    residual, normed_two, cot_all = rest
     if fused:
-        gate_far, residual, normed_two = lax.optimization_barrier(
-            (gate_far, residual, normed_two)
+        gate_far, first_far, residual, normed_two = lax.optimization_barrier(
+            (gate_far, first_far, residual, normed_two)
         )
 
     if fused:
@@ -1596,6 +1578,7 @@
         rel = []
         for own_one, near, far in (
             (gate_weight, gate_near, gate_far),
+            (up_weight[:1], first_near, first_far),
             (up_late, up_near, up_far),
             (down_late, down_near, down_far),
         ):
@@ -1610,7 +1593,7 @@
     if fused:
         router_wide = jnp.pad(router_weight, ((0, 0), (0, EXTRA - experts_all)))
         summed, out_part, gate_part, up_part, down_part = expert_rows(
-            normed_all, cot_all, chosen_all, router_wide, rel[0], up_first, rel[1], rel[2], 3
+            normed_all, cot_all, chosen_all, router_wide, *rel, 3
         )
         d_rows_own = summed[:, :model_width]
         d_gates_own = (

time: 558 us -> 560 us (level)
  transfers between devices with their start and end apart: 12 -> 15, of which waited for: 2 -> 4; matrix products, arithmetic and copies ran while one was open for 8% -> 8% of each run, Pallas kernels for 68% -> 68%
where the time goes in v4:
time: 560 us; the launch traced here: 559 us
  Pallas kernels  478 us (85%)
  other arithmetic  29.9 us (5%)
  local copies, waits for them, and re-layouts  22.9 us (4%)
  between operations  14.1 us (3%)
  waiting for transfers between devices  6.66 us (1%)
  starting transfers between devices  6.15 us (1%)
    pallas_call x1, Pallas kernels, attention_backward(): pl.pallas_call(kernel, out_shape=[jax.ShapeDtypeStruct((columns, share),...  138 us
    pallas_call x1, Pallas kernels, sum_and_gather(): pl.pallas_call(kernel, out_shape=[jax.ShapeDtypeStruct(a.shape, a.dtype)...  126 us
    pallas_call x1, Pallas kernels, expert_rows(): pl.pallas_call(kernel, out_shape=[jax.ShapeDtypeStruct((count, columns +...  98.8 us
    pallas_call x1, Pallas kernels, attention_forward(): pl.pallas_call(kernel, out_shape=[shape((tokens, columns), BF), shape((to...  62.7 us
    pallas_call x1, Pallas kernels, gather_rows(): pl.pallas_call(kernel, out_shape=[jax.ShapeDtypeStruct((g[1] * g[2] * a.s...  52.8 us
  transfers between devices with their start and end apart: 15, of which 4 were waited for; matrix products, arithmetic and copies ran while one was open for 8% of the time, Pallas kernels for 68%

profile of v4, /device:TPU:8, one launch (start us, length us, event | category | flops | bytes accessed | tf_op | source)
XLA Modules:
  0.0 559.5 jit_solution(8551394732468240725)
XLA Ops:
  7.3 1.6 collective-permute-start
  8.8 1.5 fusion.7
  10.3 0.6 collective-permute-start.1
  11.5 0.8 copy.38.refs_6_.refs_15_
  12.5 1.0 fusion
  13.5 1.0 pad_maximum_fusion
  14.5 1.9 constant_dynamic-slice_fusion.2.refs_13_
  16.4 62.7 %attention_forward.1 = (bf16[512,2048]{1,0:T(8,128)(2,1)}, f32[512,1024]{1,0:T(8,128)}, f32[512,128]{1,0:T(8,128)}, bf16[512,1024]{1,0:T(8,128)(2,1)}, bf16[512,...) custom-call(bf16[512,2048]{1,0:T(8,128)(2,1)} %refs_0_.1, ...), custom_call_target="tpu_custom_call" | custom-call | tf_op jit(solution)/shard_map/attention_forward/pallas_call | solution.py:1186
  79.2 0.6 collective-permute-start.3
  79.8 1.5 collective-permute-start.2
  81.3 0.5 collective-permute-start.6
  82.0 0.6 pad_convert_fusion.refs_1_
  82.7 52.8 %gather_rows.1 = (bf16[1024,2048]{1,0:T(8,128)(2,1)}, bf16[1024,128]{1,0:T(8,128)(2,1)}) custom-call(bf16[128,2048]{1,0:T(8,128)(2,1)} %get-tuple-element.70.refs_0_, bf16[128,128]{1,0:T(8,128)(2,1)} %pad_convert_fusion.refs_1_), custom_call_target="tpu_custom_call" | custom-call | tf_op jit(solution)/shard_map/gather_rows/pallas_call | solution.py:594
  135.6 0.5 collective-permute-start.5
  136.2 0.4 collective-permute-start.7
  136.6 1.5 collective-permute-done.8.refs_13_
  138.1 0.9 copy-done.16
  139.4 0.9 pad.16.refs_3_
  140.5 0.9 copy-done.17
  141.6 3.4 collective-permute-done.9.refs_15_
  144.9 98.8 %expert_rows.1 = (f32[128,2176]{1,0:T(8,128)}, bf16[1024,2048]{1,0:T(8,128)(2,1)}, bf16[4,2,192,2048]{3,2,1,0:T(8,128)(2,1)}, bf16[4,2,192,2048]{3,2,1,0:T(8,128)(2,1)}, bf16[4,2,192,2048]{3,2,1,0:T(8,128)(2,1)}) custom-call(bf16[1024,2048]{1,0:T(8,128)(2,1)} %get-tuple-element.72.refs_0_, bf16[1024,2048]{1,0:T(8,128)(2,1)} %get-tuple-element.73.refs_1_, ...), custom_call_target="tpu_custom_call" | custom-call | tf_op jit(solution)/shard_map/expert_rows/pallas_call | solution.py:1014
  243.8 0.7 reduce-scatter.8.cloned.1.call-update
  244.6 0.7 reduce-scatter.6.cloned.1.call-update
  245.3 2.0 constant_dynamic-slice_fusion.1.refs_9_
  248.3 0.6 multiply_reduce_fusion
  248.8 2.5 fusion.6
  251.4 138.2 %attention_backward.1 = (bf16[2048,1024]{1,0:T(8,128)(2,1)}, bf16[2048,256]{1,0:T(8,128)(2,1)}, bf16[128,2048]{1,0:T(8,128)(2,1)}, f32[8,2048]{1,0:T(8,128)}, f3...) custom-call(bf16[512,1024]{1,0:T(8,128)(2,1)} %get-tuple-element.56.refs_0_, ...), custom_call_target="tpu_custom_call" | custom-call | tf_op jit(solution)/shard_map/attention_backward/pallas_call | solution.py:1425
  389.6 0.9 slice.72
  390.9 0.7 constant_dynamic-update-slice_fusion.1
  391.6 0.7 constant_dynamic-update-slice_fusion
  392.3 0.7 reshape.112.refs_3_
  393.0 6.5 %maximum_convert_fusion = f32[1024,2048]{1,0:T(8,128)} fusion(bf16[1024,512]{1,0:T(8,128)(2,1)S(1)} %copy-done.13, bf16[1024,1536]{1,0:T(8,128)(2,1)} %get-tuple-element.93), kind=kLoop, calls=%fused_computation | loop fusion | flops 8388608 | bytes 12582912 | tf_op jit(solution)/shard_map/convert_element_type | solution.py:1727
  399.5 1.9 add_convert_fusion.refs_5_
  401.4 125.9 %sum_and_gather.1 = (bf16[2048,1024]{1,0:T(8,128)(2,1)}, bf16[2048,256]{1,0:T(8,128)(2,1)}, f32[64,640]{1,0:T(8,128)}, bf16[512,2048]{1,0:T(8,128)(2,1)}, bf16[5...) custom-call(bf16[2048,1024]{1,0:T(8,128)(2,1)} %get-tuple-element.80.refs_0_, bf16[2048,256]{1,0:T(8,128)(2,1)} %get-tuple-element.81.refs_1_, ...), custom_call_target="tpu_custom_call" | custom-call | tf_op jit(solution)/shard_map/sum_and_gather/pallas_call | solution.py:746
  527.3 1.0 slice.81
  528.3 0.9 reshape.113
  529.2 6.7 %convert_element_type.55 = f32[2048,1024]{1,0:T(8,128)} convert(bf16[2048,1024]{1,0:T(8,128)(2,1)} %get-tuple-element.91) | non-fusion elementwise | flops 2097152 | bytes 12582912 | tf_op jit(solution)/shard_map/convert_element_type | solution.py:1722
  536.0 0.5 fusion.9
  536.5 0.6 fusion.8
  537.1 0.7 slice_bitcast_fusion
  537.8 1.5 slice_convert_fusion
  539.2 3.4 convert_bitcast_fusion
  542.7 3.6 convert_bitcast_fusion.1
  546.3 1.3 copy.55
  547.6 1.0 copy-done.6
  548.6 1.3 copy.56
  549.9 1.3 copy-done.5
  551.3 1.7 copy.57
  (84 shorter events, 3.5 us)
Async XLA Ops:
  7.2 74.6 %copy-start = (s32[512,8]{0,1:T(8,128)S(1)}, s32[512,8]{0,1:T(8,128)}, u32[]{:S(2)}) copy-start(s32[512,8]{0,1:T(8,128)} %param.18) | copy-start | bytes 49156
  7.2 3.7 copy-start.19
  7.2 392.3 %reduce-scatter.4.cloned.1.call-start = ((), (), s32[]{:S(2)}) async-start(), calls=%async_computation.3 | async-start | bytes 4718592 | tf_op jit(solution)/shard_map/reduce_scatter | solution.py:1652
  7.3 71.9 %collective-permute-start = (bf16[2,192,2048]{2,1,0:T(8,128)(2,1)}, bf16[2,192,2048]{2,1,0:T(8,128)(2,1)}, u32[]{:S(2)}, u32[]{:S(2)}) collective-permute-start(bf16[2,192,2048]{2,1,0:T(8,128)(2,1)} %bitcast.45), channel_id=1, source_target_pairs={{0,2},{1,3},{2,0},{3,1},{4,6},{5,7},{6,4},{7,5},{8,10},{9,11},{10,... | collective-permute-start | bytes 4718600 | tf_op jit(solution)/shard_map/ppermute | solution.py:1484
  10.3 71.0 %copy-start.4 = (bf16[1,192,2048]{2,1,0:T(8,128)(2,1)}, bf16[1,192,2048]{2,1,0:T(8,128)(2,1)S(1)}, u32[]{:S(2)}) copy-start(bf16[1,192,2048]{2,1,0:T(8,128)(2,1)S(1)} %get-tuple-element.103.refs_8_) | copy-start | bytes 2359300
  10.3 125.2 %copy-start.3 = (bf16[1,192,2048]{2,1,0:T(8,128)(2,1)}, bf16[1,192,2048]{2,1,0:T(8,128)(2,1)S(1)}, u32[]{:S(2)}) copy-start(bf16[1,192,2048]{2,1,0:T(8,128)(2,1)S(1)} %get-tuple-element.68.refs_12_) | copy-start | bytes 2359300
  10.3 68.8 %collective-permute-start.1 = (bf16[1,192,2048]{2,1,0:T(8,128)(2,1)S(1)}, bf16[1,192,2048]{2,1,0:T(8,128)(2,1)}, u32[]{:S(2)}, u32[]{:S(2)}) collective-permute-start(bf16[1,192,2048]{2,1,0:T(8,128)(2,1)S(1)} %get-tuple-element.103.refs_8_), channel_id=1, source_target_pairs={{0,2},{1,3},{2,0},{3,1},{4,6},{5,7},{6,4},{7,5},{8,10},{9,11},{10,... | collective-permute-start | bytes 2359304 | tf_op jit(solution)/shard_map/ppermute | solution.py:1484
  16.4 62.8 %copy-start.10 = (bf16[2,192,2048]{2,1,0:T(8,128)(2,1)S(1)}, bf16[2,192,2048]{2,1,0:T(8,128)(2,1)}, u32[]{:S(2)}) copy-start(bf16[2,192,2048]{2,1,0:T(8,128)(2,1)} %refs_16_) | copy-start | bytes 4718596
  16.4 64.9 %copy-start.9 = (bf16[2,2048,192]{1,2,0:T(8,128)(2,1)S(1)}, bf16[2,2048,192]{1,2,0:T(8,128)(2,1)}, u32[]{:S(2)}) copy-start(bf16[2,2048,192]{1,2,0:T(8,128)(2,1)} %param.28) | copy-start | bytes 4718596
  16.4 122.7 %copy-start.18 = (bf16[2048,16]{0,1:T(8,128)(2,1)S(1)}, bf16[2048,16]{0,1:T(8,128)(2,1)}, u32[]{:S(2)}) copy-start(bf16[2048,16]{0,1:T(8,128)(2,1)} %param.27) | copy-start | bytes 196612
  79.2 56.4 %collective-permute-start.3 = (bf16[2,192,2048]{2,1,0:T(8,128)(2,1)S(1)}, bf16[2,192,2048]{2,1,0:T(8,128)(2,1)}, u32[]{:S(2)}, u32[]{:S(2)}) collective-permute-start(bf16[2,192,2048]{2,1,0:T(8,128)(2,1)S(1)} %copy-done.10), channel_id=1, source_target_pairs={{0,2},{1,3},{2,0},{3,1},{4,6},{5,7},{6,4},{7,5},{8,10},{9,11},{10,... | collective-permute-start | bytes 4718600 | tf_op jit(solution)/shard_map/ppermute | solution.py:1484
  79.8 55.7 %collective-permute-start.2 = (bf16[1,192,2048]{2,1,0:T(8,128)(2,1)S(1)}, bf16[1,192,2048]{2,1,0:T(8,128)(2,1)}, u32[]{:S(2)}, u32[]{:S(2)}) collective-permute-start(bf16[1,192,2048]{2,1,0:T(8,128)(2,1)S(1)} %get-tuple-element.68.refs_12_), channel_id=1, source_target_pairs={{0,2},{1,3},{2,0},{3,1},{4,6},{5,7},{6,4},{7,5},{8,10},{9,11},{10,... | collective-permute-start | bytes 2359304 | tf_op jit(solution)/shard_map/ppermute | solution.py:1484
  81.3 54.9 %collective-permute-start.4 = (bf16[2,192,2048]{2,1,0:T(8,128)(2,1)S(1)}, bf16[2,192,2048]{2,1,0:T(8,128)(2,1)S(1)}, u32[]{:S(2)}, u32[]{:S(2)}) collective-permute-start(bf16[2,192,2048]{2,1,0:T(8,128)(2,1)S(1)} %bitcast.47), channel_id=1, source_target_pairs={{0,1},{1,0},{2,3},{3,2},{4,5},{5,4},{6,7},{7,6},{8,9},{9,8},{10,11... | collective-permute-start | bytes 4718600 | tf_op jit(solution)/shard_map/ppermute | solution.py:1480
  81.3 54.8 %collective-permute-start.6 = (bf16[1,192,2048]{2,1,0:T(8,128)(2,1)S(1)}, bf16[1,192,2048]{2,1,0:T(8,128)(2,1)S(1)}, u32[]{:S(2)}, u32[]{:S(2)}) collective-permute-start(bf16[1,192,2048]{2,1,0:T(8,128)(2,1)S(1)} %get-tuple-element.103.refs_8_), channel_id=1, source_target_pairs={{0,1},{1,0},{2,3},{3,2},{4,5},{5,4},{6,7},{7,6},{8,9},{9,8},{10,11... | collective-permute-start | bytes 2359304 | tf_op jit(solution)/shard_map/ppermute | solution.py:1480
  82.6 57.9 %collective-permute-start.10 = (bf16[2,192,2048]{2,1,0:T(8,128)(2,1)S(1)}, bf16[2,192,2048]{2,1,0:T(8,128)(2,1)}, u32[]{:S(2)}, u32[]{:S(2)}) collective-permute-start(bf16[2,192,2048]{2,1,0:T(8,128)(2,1)S(1)} %copy-done.10), channel_id=1, source_target_pairs={{0,1},{1,0},{2,3},{3,2},{4,5},{5,4},{6,7},{7,6},{8,9},{9,8},{10,11... | collective-permute-start | bytes 4718600 | tf_op jit(solution)/shard_map/ppermute | solution.py:1480
  135.5 2.6 collective-permute-start.8
  135.6 6.0 %collective-permute-start.5 = (bf16[2,192,2048]{2,1,0:T(8,128)(2,1)}, bf16[2,192,2048]{2,1,0:T(8,128)(2,1)}, u32[]{:S(2)}, u32[]{:S(2)}) collective-permute-start(bf16[2,192,2048]{2,1,0:T(8,128)(2,1)} %collective-permute-done.refs_6_), channel_id=1, source_target_pairs={{0,1},{1,0},{2,3},{3,2},{4,5},{5,4},{6,7},{7,6},{8,9},{9,8},{10,11... | collective-permute-start | bytes 4718600 | tf_op jit(solution)/shard_map/ppermute | solution.py:1480
  136.1 2.0 copy-start.15
  136.1 8.9 %collective-permute-start.11 = (bf16[2,192,2048]{2,1,0:T(8,128)(2,1)}, bf16[2,192,2048]{2,1,0:T(8,128)(2,1)}, u32[]{:S(2)}, u32[]{:S(2)}) collective-permute-start(bf16[2,192,2048]{2,1,0:T(8,128)(2,1)} %collective-permute-done.3.refs_18_), channel_id=1, source_target_pairs={{0,1},{1,0},{2,3},{3,2},{4,5},{5,4},{6,7},{7,6},{8,9},{9,8},{10,11... | collective-permute-start | bytes 4718600 | tf_op jit(solution)/shard_map/ppermute | solution.py:1480
  136.2 1.9 copy-start.11
  136.2 4.4 collective-permute-start.7
  138.1 0.9 copy-start.16
  139.0 6.0 %collective-permute-start.9 = (bf16[1,192,2048]{2,1,0:T(8,128)(2,1)}, bf16[1,192,2048]{2,1,0:T(8,128)(2,1)}, u32[]{:S(2)}, u32[]{:S(2)}) collective-permute-start(bf16[1,192,2048]{2,1,0:T(8,128)(2,1)} %collective-permute-done.2.refs_14_), channel_id=1, source_target_pairs={{0,1},{1,0},{2,3},{3,2},{4,5},{5,4},{6,7},{7,6},{8,9},{9,8},{10,11... | collective-permute-start | bytes 2359304 | tf_op jit(solution)/shard_map/ppermute | solution.py:1480
  140.5 0.9 copy-start.17
  243.8 295.4 %reduce-scatter.8.cloned.1.call-start = ((), (), s32[]{:S(2)}) async-start(), calls=%async_computation.5 | async-start | bytes 7864320 | tf_op jit(solution)/shard_map/reduce_scatter | solution.py:1654
  244.5 298.1 %reduce-scatter.6.cloned.1.call-start = ((), (), s32[]{:S(2)}) async-start(), calls=%async_computation.4 | async-start | bytes 7864320 | tf_op jit(solution)/shard_map/reduce_scatter | solution.py:1654
  244.6 2.8 copy-start.8
  245.3 2.6 copy-start.2
  245.3 2.8 copy-start.12
  245.3 3.0 copy-start.20
  389.6 3.5 copy-start.13
  529.2 8.5 %copy-start.14 = (bf16[2048,256]{1,0:T(8,128)(2,1)S(1)}, bf16[2048,256]{1,0:T(8,128)(2,1)}, u32[]{:S(2)}) copy-start(bf16[2048,256]{1,0:T(8,128)(2,1)} %get-tuple-element.92) | copy-start | bytes 3145732
  542.7 3.6 copy-start.7
  546.3 2.3 copy-start.6
  548.6 2.6 copy-start.5
  548.6 4.3 copy-start.1
Sparse Core Ops, SparseCore 0:
  243.9 119.0 reduce-scatter.3
  365.7 61.5 reduce-scatter.7
  429.8 75.4 reduce-scatter.5

commit v5 on v4

--- a/solution.py
+++ b/solution.py
@@ -761,7 +761,6 @@
 PAIR_US = 1.5
 HEAD_US = 5.5
 TILE_US = 1.5
-FORWARD_US = 3.0
 EXTRA = 128
 
 
@@ -1060,9 +1059,9 @@
     return inverse * scaled - vector * (inverse * inverse * inverse * inner)
 
 
-def attention_forward(arrays, cot_own, heads, number):
-    grid, side = grid_of("expert"), grid_of("shard")
-    size, shards = grid[1] * grid[2], side[1] * side[2]
+def attention_forward(arrays, heads, number):
+    side = grid_of("shard")
+    shards = side[1] * side[2]
     names = list(arrays)
     tokens, columns = arrays["rows"].shape
     inner = arrays["query_weight"].shape[1]
@@ -1075,34 +1074,21 @@
     def kernel(*refs):
         take = Taker(refs)
         hbm_refs = take.take(len(names))
-        cot_ref = take.one()
         normed, query_lin, key_lin, query, key, value, mixed, log_total = take.take(8)
         residual, normed_two = take.take(2)
-        cot_all = take.one()
         v = dict(zip(names, take.take(len(names))))
         bias, parts, summed = take.take(3)
         buffers = take.take(3)
-        load_sems, own_sems = take.take(2)
+        load_sems = take.one()
         job = Scatter(side, parts, buffers, 2, take.take(6))
-        cot_job = Gather(grid, cot_ref, cot_all, 2, take.take(4))
         shard = lax.axis_index("shard")
-        cot_plan = Plan(grid[1])
-        for p in range(2):
-            plan_gather(cot_plan, cot_job, p, 0.0)
-        cot_order = cot_plan.order()
-
-        def own_cot(z):
-            return pltpu.make_async_copy(cot_ref, cot_job.own_slot(z), own_sems.at[0])
-
         loads = [
             pltpu.make_async_copy(ref, v[name], load_sems.at[i])
             for i, (name, ref) in enumerate(zip(names, hbm_refs))
         ]
         for c in loads:
             c.start()
-        at_each_line(grid, lambda z: own_cot(z).start())
-        greet([grid, side])
-        cot_plan.run(grid, cot_order, 0.0, 2.0)
+        greet([side])
         for c in loads[:-1]:
             c.wait()
 
@@ -1130,8 +1116,6 @@
         cols_at = lax.broadcasted_iota(jnp.int32, (tokens, tokens), 1)
         allowed = jnp.logical_and(v["doc_col"][...] == v["doc_row"][...], rows_at >= cols_at)
         bias[...] = jnp.where(allowed, 0.0, -1e30)
-
-        cot_order_late = [[s for s in steps if s[0] >= 2.0] for steps in cot_order]
 
         @pl.loop(0, heads)
         def _(h):
@@ -1147,7 +1131,6 @@
                 log_total[h, rows, :] = top + jnp.log(total)
                 probs = (powers * (1.0 / total)).astype(BF)
                 mixed[rows, lanes] = dot(probs, value[keys, :]).astype(BF)
-            cot_plan.run_step(grid, cot_order_late, h, 10.0, FORWARD_US, heads, True)
 
         loads[-1].wait()
 
@@ -1163,7 +1146,6 @@
         for p in range(2):
             plan_scatter(plan, job, p, put)
         plan.run(side, plan.order(), *ALWAYS)
-        cot_plan.run(grid, cot_order, 10.0 + heads * FORWARD_US, 1e9)
 
         @pl.loop(0, own_rows // 16)
         def _(i):
@@ -1174,12 +1156,6 @@
             normed_two[rows, :] = norm(total, v["norm_two_gain"][...]).astype(BF)
 
         at_each_line(side, job.finish)
-
-        def end_cot(z):
-            cot_job.finish(z)
-            own_cot(z).wait()
-
-        at_each_line(grid, end_cot)
 
     values = [arrays[name] for name in names]
     shape = jax.ShapeDtypeStruct
@@ -1196,10 +1172,9 @@
             shape((heads, tokens, 1), F32),
             shape((own_rows, columns), F32),
             shape((own_rows, columns), BF),
-            shape((size * own_rows, columns), BF),
         ],
-        in_specs=[hbm()] * (len(names) + 1),
-        out_specs=[vmem()] * 10 + [hbm()],
+        in_specs=[hbm()] * len(names),
+        out_specs=[vmem()] * 10,
         scratch_shapes=[pltpu.VMEM(a.shape, a.dtype) for a in values]
         + [
             pltpu.VMEM((tokens, tokens), F32),
@@ -1207,12 +1182,11 @@
             pltpu.VMEM((own_rows, columns), F32),
         ]
         + Scatter.buffers(side, own_rows, columns, BF)
-        + [pltpu.SemaphoreType.DMA((len(names),)), pltpu.SemaphoreType.DMA((1,))]
-        + Scatter.sems(side, 2)
-        + Gather.sems(grid, 2),
+        + [pltpu.SemaphoreType.DMA((len(names),))]
+        + Scatter.sems(side, 2),
         compiler_params=params(number),
         name="attention_forward",
-    )(*values, cot_own)
+    )(*values)
 
 
 def attention_backward(arrays, d_own, heads, number):
@@ -1522,6 +1496,7 @@
 
     fused = expert_peers * rows_here <= VMEM_ROWS
     cot_own = own(cotangent)
+    cot_all = lax.all_gather(cot_own, "expert", axis=0, tiled=True)
     routes_own = own(routes)
     experts = jnp.arange(experts_all, dtype=jnp.int32)
     chosen_own = jnp.any(routes_own[:, :, None] == experts[None, None, :], axis=1)
@@ -1556,9 +1531,9 @@
         rows=layer_input, norm_two_gain=norm2_gain[None, :], **shared, out_weight=out_weight
     )
     normed_one, query_lin, key_lin, query, key, value, mixed, log_total, *rest = (
-        attention_forward(forward, cot_own, heads_here, 1)
+        attention_forward(forward, heads_here, 1)
     )
-    residual, normed_two, cot_all = rest
+    residual, normed_two = rest
     if fused:
         gate_far, first_far, residual, normed_two = lax.optimization_barrier(
             (gate_far, first_far, residual, normed_two)

time: 560 us -> 562 us (level)
  transfers between devices with their start and end apart: 15 -> 16, of which waited for: 4 -> 4; matrix products, arithmetic and copies ran while one was open for 8% -> 7% of each run, Pallas kernels for 68% -> 68%
where the time goes in v5:
time: 562 us; the launch traced here: 561 us
  Pallas kernels  481 us (86%)
  other arithmetic  29.9 us (5%)
  local copies, waits for them, and re-layouts  21.7 us (4%)
  between operations  14.1 us (3%)
  waiting for transfers between devices  6.5 us (1%)
  starting transfers between devices  6.19 us (1%)
    pallas_call x1, Pallas kernels, attention_backward(): pl.pallas_call(kernel, out_shape=[jax.ShapeDtypeStruct((columns, share),...  138 us
    pallas_call x1, Pallas kernels, sum_and_gather(): pl.pallas_call(kernel, out_shape=[jax.ShapeDtypeStruct(a.shape, a.dtype)...  126 us
    pallas_call x1, Pallas kernels, expert_rows(): pl.pallas_call(kernel, out_shape=[jax.ShapeDtypeStruct((count, columns +...  98.8 us
    pallas_call x1, Pallas kernels, attention_forward(): pl.pallas_call(kernel, out_shape=[shape((tokens, columns), BF), shape((to...  65.7 us
    pallas_call x1, Pallas kernels, gather_rows(): pl.pallas_call(kernel, out_shape=[jax.ShapeDtypeStruct((g[1] * g[2] * a.s...  52.8 us
  transfers between devices with their start and end apart: 16, of which 4 were waited for; matrix products, arithmetic and copies ran while one was open for 7% of the time, Pallas kernels for 68%

profile of v5, /device:TPU:8, one launch (start us, length us, event | category | flops | bytes accessed | tf_op | source)
XLA Modules:
  0.0 561.1 jit_solution(7282489766329091454)
XLA Ops:
  7.3 2.0 constant_dynamic-slice_fusion.1
  9.3 1.6 collective-permute-start
  11.1 0.6 collective-permute-start.1
  12.3 0.8 copy.38.refs_6_.refs_15_
  13.3 1.0 fusion
  14.3 1.0 pad_maximum_fusion
  15.3 65.7 %attention_forward.1 = (bf16[512,2048]{1,0:T(8,128)(2,1)}, f32[512,1024]{1,0:T(8,128)}, f32[512,128]{1,0:T(8,128)}, bf16[512,1024]{1,0:T(8,128)(2,1)}, bf16[512,...) custom-call(bf16[512,2048]{1,0:T(8,128)(2,1)} %refs_0_.1, ...), custom_call_target="tpu_custom_call" | custom-call | tf_op jit(solution)/shard_map/attention_forward/pallas_call | solution.py:1162
  81.0 0.6 collective-permute-start.3
  81.6 1.5 collective-permute-start.2
  83.1 0.5 collective-permute-start.6
  83.7 0.6 pad_convert_fusion.refs_1_
  84.4 52.8 %gather_rows.1 = (bf16[1024,2048]{1,0:T(8,128)(2,1)}, bf16[1024,128]{1,0:T(8,128)(2,1)}) custom-call(bf16[128,2048]{1,0:T(8,128)(2,1)} %get-tuple-element.69.refs_0_, bf16[128,128]{1,0:T(8,128)(2,1)} %pad_convert_fusion.refs_1_), custom_call_target="tpu_custom_call" | custom-call | tf_op jit(solution)/shard_map/gather_rows/pallas_call | solution.py:594
  137.4 0.5 collective-permute-start.5
  137.9 0.4 collective-permute-start.7
  138.4 1.5 collective-permute-done.8.refs_13_
  139.9 0.9 copy-done.17
  141.1 0.9 pad.16.refs_3_
  142.3 0.9 copy-done.18
  143.3 3.4 collective-permute-done.9.refs_15_
  146.7 98.8 %expert_rows.1 = (f32[128,2176]{1,0:T(8,128)}, bf16[1024,2048]{1,0:T(8,128)(2,1)}, bf16[4,2,192,2048]{3,2,1,0:T(8,128)(2,1)}, bf16[4,2,192,2048]{3,2,1,0:T(8,128)(2,1)}, bf16[4,2,192,2048]{3,2,1,0:T(8,128)(2,1)}) custom-call(bf16[1024,2048]{1,0:T(8,128)(2,1)} %get-tuple-element.71.refs_0_, bf16[1024,2048]{1,0:T(8,128)(2,1)} %all-gather.2.cloned.1.call-done.refs_1_, ...), custom_call_target="tpu_custom_call" | custom-call | tf_op jit(solution)/shard_map/expert_rows/pallas_call | solution.py:1013
  245.6 0.7 reduce-scatter.8.cloned.1.call-update
  246.3 0.5 reduce-scatter.6.cloned.1.call-update
  246.9 2.0 constant_dynamic-slice_fusion.2.refs_9_
  248.9 0.4 fusion.10
  249.9 0.6 multiply_reduce_fusion
  250.4 2.5 fusion.6
  253.0 138.3 %attention_backward.1 = (bf16[2048,1024]{1,0:T(8,128)(2,1)}, bf16[2048,256]{1,0:T(8,128)(2,1)}, bf16[128,2048]{1,0:T(8,128)(2,1)}, f32[8,2048]{1,0:T(8,128)}, f3...) custom-call(bf16[512,1024]{1,0:T(8,128)(2,1)} %get-tuple-element.55.refs_0_, ...), custom_call_target="tpu_custom_call" | custom-call | tf_op jit(solution)/shard_map/attention_backward/pallas_call | solution.py:1399
  391.3 0.9 slice.72
  392.6 0.7 constant_dynamic-update-slice_fusion.1
  393.3 0.7 constant_dynamic-update-slice_fusion
  394.0 0.7 reshape.112.refs_3_
  394.7 6.5 %maximum_convert_fusion = f32[1024,2048]{1,0:T(8,128)} fusion(bf16[1024,512]{1,0:T(8,128)(2,1)S(1)} %copy-done.14, bf16[1024,1536]{1,0:T(8,128)(2,1)} %get-tuple-element.91), kind=kLoop, calls=%fused_computation | loop fusion | flops 8388608 | bytes 12582912 | tf_op jit(solution)/shard_map/convert_element_type | solution.py:1702
  401.2 1.9 add_convert_fusion.refs_5_
  403.1 125.9 %sum_and_gather.1 = (bf16[2048,1024]{1,0:T(8,128)(2,1)}, bf16[2048,256]{1,0:T(8,128)(2,1)}, f32[64,640]{1,0:T(8,128)}, bf16[512,2048]{1,0:T(8,128)(2,1)}, bf16[5...) custom-call(bf16[2048,1024]{1,0:T(8,128)(2,1)} %get-tuple-element.78.refs_0_, bf16[2048,256]{1,0:T(8,128)(2,1)} %get-tuple-element.79.refs_1_, ...), custom_call_target="tpu_custom_call" | custom-call | tf_op jit(solution)/shard_map/sum_and_gather/pallas_call | solution.py:746
  529.0 1.0 slice.81
  530.0 0.9 reshape.113
  530.9 6.7 %convert_element_type.55 = f32[2048,1024]{1,0:T(8,128)} convert(bf16[2048,1024]{1,0:T(8,128)(2,1)} %get-tuple-element.89) | non-fusion elementwise | flops 2097152 | bytes 12582912 | tf_op jit(solution)/shard_map/convert_element_type | solution.py:1697
  537.6 0.5 fusion.9
  538.1 0.6 fusion.8
  538.7 0.7 slice_bitcast_fusion
  539.4 1.5 slice_convert_fusion
  540.9 3.4 convert_bitcast_fusion
  544.3 3.6 convert_bitcast_fusion.1
  547.9 1.3 copy.55
  549.2 1.0 copy-done.6
  550.3 1.3 copy.56
  551.6 1.3 copy-done.5
  552.9 1.7 copy.57
  (89 shorter events, 3.4 us)
Async XLA Ops:
  7.2 76.4 %copy-start = (s32[512,8]{0,1:T(8,128)S(1)}, s32[512,8]{0,1:T(8,128)}, u32[]{:S(2)}) copy-start(s32[512,8]{0,1:T(8,128)} %param.18) | copy-start | bytes 49156
  7.2 3.7 copy-start.9
  7.2 139.5 %all-gather.2.cloned.1.call-start = ((), (), s32[]{:S(2)}) async-start(), calls=%async_computation.3 | async-start | bytes 4718592 | tf_op jit(solution)/shard_map/all_gather | solution.py:1499
  9.3 2.4 copy-start.20
  9.3 391.9 %reduce-scatter.4.cloned.1.call-start = ((), (), s32[]{:S(2)}) async-start(), calls=%async_computation.4 | async-start | bytes 4718592 | tf_op jit(solution)/shard_map/reduce_scatter | solution.py:1627
  9.3 71.6 %collective-permute-start = (bf16[2,192,2048]{2,1,0:T(8,128)(2,1)}, bf16[2,192,2048]{2,1,0:T(8,128)(2,1)}, u32[]{:S(2)}, u32[]{:S(2)}) collective-permute-start(bf16[2,192,2048]{2,1,0:T(8,128)(2,1)} %bitcast.45), channel_id=1, source_target_pairs={{0,2},{1,3},{2,0},{3,1},{4,6},{5,7},{6,4},{7,5},{8,10},{9,11},{10,... | collective-permute-start | bytes 4718600 | tf_op jit(solution)/shard_map/ppermute | solution.py:1458
  11.1 72.0 %copy-start.4 = (bf16[1,192,2048]{2,1,0:T(8,128)(2,1)}, bf16[1,192,2048]{2,1,0:T(8,128)(2,1)S(1)}, u32[]{:S(2)}) copy-start(bf16[1,192,2048]{2,1,0:T(8,128)(2,1)S(1)} %get-tuple-element.101.refs_8_) | copy-start | bytes 2359300
  11.1 126.2 %copy-start.3 = (bf16[1,192,2048]{2,1,0:T(8,128)(2,1)}, bf16[1,192,2048]{2,1,0:T(8,128)(2,1)S(1)}, u32[]{:S(2)}) copy-start(bf16[1,192,2048]{2,1,0:T(8,128)(2,1)S(1)} %get-tuple-element.67.refs_12_) | copy-start | bytes 2359300
  11.1 69.8 %collective-permute-start.1 = (bf16[1,192,2048]{2,1,0:T(8,128)(2,1)S(1)}, bf16[1,192,2048]{2,1,0:T(8,128)(2,1)}, u32[]{:S(2)}, u32[]{:S(2)}) collective-permute-start(bf16[1,192,2048]{2,1,0:T(8,128)(2,1)S(1)} %get-tuple-element.101.refs_8_), channel_id=1, source_target_pairs={{0,2},{1,3},{2,0},{3,1},{4,6},{5,7},{6,4},{7,5},{8,10},{9,11},{10,... | collective-permute-start | bytes 2359304 | tf_op jit(solution)/shard_map/ppermute | solution.py:1458
  15.3 65.7 %copy-start.11 = (bf16[2,192,2048]{2,1,0:T(8,128)(2,1)S(1)}, bf16[2,192,2048]{2,1,0:T(8,128)(2,1)}, u32[]{:S(2)}) copy-start(bf16[2,192,2048]{2,1,0:T(8,128)(2,1)} %refs_16_) | copy-start | bytes 4718596
  15.3 67.8 %copy-start.10 = (bf16[2,2048,192]{1,2,0:T(8,128)(2,1)S(1)}, bf16[2,2048,192]{1,2,0:T(8,128)(2,1)}, u32[]{:S(2)}) copy-start(bf16[2,2048,192]{1,2,0:T(8,128)(2,1)} %param.28) | copy-start | bytes 4718596
  15.3 125.6 %copy-start.19 = (bf16[2048,16]{0,1:T(8,128)(2,1)S(1)}, bf16[2048,16]{0,1:T(8,128)(2,1)}, u32[]{:S(2)}) copy-start(bf16[2048,16]{0,1:T(8,128)(2,1)} %param.27) | copy-start | bytes 196612
  81.0 56.4 %collective-permute-start.3 = (bf16[2,192,2048]{2,1,0:T(8,128)(2,1)S(1)}, bf16[2,192,2048]{2,1,0:T(8,128)(2,1)}, u32[]{:S(2)}, u32[]{:S(2)}) collective-permute-start(bf16[2,192,2048]{2,1,0:T(8,128)(2,1)S(1)} %copy-done.11), channel_id=1, source_target_pairs={{0,2},{1,3},{2,0},{3,1},{4,6},{5,7},{6,4},{7,5},{8,10},{9,11},{10,... | collective-permute-start | bytes 4718600 | tf_op jit(solution)/shard_map/ppermute | solution.py:1458
  81.6 55.7 %collective-permute-start.2 = (bf16[1,192,2048]{2,1,0:T(8,128)(2,1)S(1)}, bf16[1,192,2048]{2,1,0:T(8,128)(2,1)}, u32[]{:S(2)}, u32[]{:S(2)}) collective-permute-start(bf16[1,192,2048]{2,1,0:T(8,128)(2,1)S(1)} %get-tuple-element.67.refs_12_), channel_id=1, source_target_pairs={{0,2},{1,3},{2,0},{3,1},{4,6},{5,7},{6,4},{7,5},{8,10},{9,11},{10,... | collective-permute-start | bytes 2359304 | tf_op jit(solution)/shard_map/ppermute | solution.py:1458
  83.1 54.9 %collective-permute-start.4 = (bf16[2,192,2048]{2,1,0:T(8,128)(2,1)S(1)}, bf16[2,192,2048]{2,1,0:T(8,128)(2,1)S(1)}, u32[]{:S(2)}, u32[]{:S(2)}) collective-permute-start(bf16[2,192,2048]{2,1,0:T(8,128)(2,1)S(1)} %bitcast.47), channel_id=1, source_target_pairs={{0,1},{1,0},{2,3},{3,2},{4,5},{5,4},{6,7},{7,6},{8,9},{9,8},{10,11... | collective-permute-start | bytes 4718600 | tf_op jit(solution)/shard_map/ppermute | solution.py:1454
  83.1 54.8 %collective-permute-start.6 = (bf16[1,192,2048]{2,1,0:T(8,128)(2,1)S(1)}, bf16[1,192,2048]{2,1,0:T(8,128)(2,1)S(1)}, u32[]{:S(2)}, u32[]{:S(2)}) collective-permute-start(bf16[1,192,2048]{2,1,0:T(8,128)(2,1)S(1)} %get-tuple-element.101.refs_8_), channel_id=1, source_target_pairs={{0,1},{1,0},{2,3},{3,2},{4,5},{5,4},{6,7},{7,6},{8,9},{9,8},{10,11... | collective-permute-start | bytes 2359304 | tf_op jit(solution)/shard_map/ppermute | solution.py:1454
  84.4 57.9 %collective-permute-start.10 = (bf16[2,192,2048]{2,1,0:T(8,128)(2,1)S(1)}, bf16[2,192,2048]{2,1,0:T(8,128)(2,1)}, u32[]{:S(2)}, u32[]{:S(2)}) collective-permute-start(bf16[2,192,2048]{2,1,0:T(8,128)(2,1)S(1)} %copy-done.11), channel_id=1, source_target_pairs={{0,1},{1,0},{2,3},{3,2},{4,5},{5,4},{6,7},{7,6},{8,9},{9,8},{10,11... | collective-permute-start | bytes 4718600 | tf_op jit(solution)/shard_map/ppermute | solution.py:1454
  137.3 2.6 collective-permute-start.8
  137.4 6.0 %collective-permute-start.5 = (bf16[2,192,2048]{2,1,0:T(8,128)(2,1)}, bf16[2,192,2048]{2,1,0:T(8,128)(2,1)}, u32[]{:S(2)}, u32[]{:S(2)}) collective-permute-start(bf16[2,192,2048]{2,1,0:T(8,128)(2,1)} %collective-permute-done.refs_6_), channel_id=1, source_target_pairs={{0,1},{1,0},{2,3},{3,2},{4,5},{5,4},{6,7},{7,6},{8,9},{9,8},{10,11... | collective-permute-start | bytes 4718600 | tf_op jit(solution)/shard_map/ppermute | solution.py:1454
  137.8 2.0 copy-start.16
  137.8 8.9 %collective-permute-start.11 = (bf16[2,192,2048]{2,1,0:T(8,128)(2,1)}, bf16[2,192,2048]{2,1,0:T(8,128)(2,1)}, u32[]{:S(2)}, u32[]{:S(2)}) collective-permute-start(bf16[2,192,2048]{2,1,0:T(8,128)(2,1)} %collective-permute-done.3.refs_18_), channel_id=1, source_target_pairs={{0,1},{1,0},{2,3},{3,2},{4,5},{5,4},{6,7},{7,6},{8,9},{9,8},{10,11... | collective-permute-start | bytes 4718600 | tf_op jit(solution)/shard_map/ppermute | solution.py:1454
  137.9 1.9 copy-start.12
  137.9 4.4 collective-permute-start.7
  139.8 0.9 copy-start.17
  140.7 6.0 %collective-permute-start.9 = (bf16[1,192,2048]{2,1,0:T(8,128)(2,1)}, bf16[1,192,2048]{2,1,0:T(8,128)(2,1)}, u32[]{:S(2)}, u32[]{:S(2)}) collective-permute-start(bf16[1,192,2048]{2,1,0:T(8,128)(2,1)} %collective-permute-done.2.refs_14_), channel_id=1, source_target_pairs={{0,1},{1,0},{2,3},{3,2},{4,5},{5,4},{6,7},{7,6},{8,9},{9,8},{10,11... | collective-permute-start | bytes 2359304 | tf_op jit(solution)/shard_map/ppermute | solution.py:1454
  142.3 0.9 copy-start.18
  245.5 295.3 %reduce-scatter.8.cloned.1.call-start = ((), (), s32[]{:S(2)}) async-start(), calls=%async_computation.6 | async-start | bytes 7864320 | tf_op jit(solution)/shard_map/reduce_scatter | solution.py:1629
  246.3 298.0 %reduce-scatter.6.cloned.1.call-start = ((), (), s32[]{:S(2)}) async-start(), calls=%async_computation.5 | async-start | bytes 7864320 | tf_op jit(solution)/shard_map/reduce_scatter | solution.py:1629
  246.3 2.6 copy-start.8
  246.9 2.6 copy-start.2
  246.9 2.8 copy-start.13
  246.9 3.0 copy-start.21
  391.3 3.4 copy-start.14
  530.9 8.5 %copy-start.15 = (bf16[2048,256]{1,0:T(8,128)(2,1)S(1)}, bf16[2048,256]{1,0:T(8,128)(2,1)}, u32[]{:S(2)}) copy-start(bf16[2048,256]{1,0:T(8,128)(2,1)} %get-tuple-element.90) | copy-start | bytes 3145732
  544.3 3.6 copy-start.7
  547.9 2.3 copy-start.6
  550.3 2.6 copy-start.5
  550.3 4.3 copy-start.1
Sparse Core Ops, SparseCore 0:
  10.7 73.8 all-gather.1
  245.7 118.4 reduce-scatter.3
  366.9 61.4 reduce-scatter.7
  430.8 74.6 reduce-scatter.5
